TPU v7x, 128 devices: a whole 4x4x4 slice. The times are simulated.
128 devices in a mesh: front: 8 (over y, core), grp: 16 (over x, z).
Axes of the slice: x: 4, y: 4, z: 4, core: 2. Of those that a mesh axis runs over, the one named last changes fastest.
Arguments:
- front_entries: bfloat16 [8, 8192, 8192], P('front', 'grp'), may hold values from -6 to 6
- child_blocks: bfloat16 [16384, 32, 512], P(('front', 'grp')), may hold values from -6 to 6
- dest_device: int32 [16384, 1], P(('front', 'grp')), may hold values from 0 to 127; in each aligned block of 128 rows (0 to 127, 128 to 255, ...) at most 2 rows name the same one
- dest_tile: int32 [16384], P(('front', 'grp')), may hold values from 0 to 255
- child_count: int32 [128], P(('front', 'grp')), may hold values from 96 to 128, as said below
- diag_inverse: float32 [8, 2, 512, 512], P('front'), as said below
Outputs:
- schur: bfloat16 [8, 7168, 7168], P('front', 'grp')
- panel_factor: float32 [8, 2, 8192, 512], P('front', None, 'grp')
Inputs may be any that keep to these rules, and one draw needn't show every extreme that they name: `dest_device`: the 128 slots of one device name one device at most 2 times, and some device exactly 2 times. `child_count`: some device has all 128 slots live in every draw. `diag_inverse`: each panel's matrix is lower triangular with a positive diagonal.
All inputs are finite; a program needn't handle non-finite values.
Results may differ from a plain program's by a relative error of at most 0.001.
Values may be sent and summed in bfloat16 or wider, within the bound.
No kernel may reach another device: no remote copies, remote signals or barrier semaphores. Data moves between devices by JAX's collectives and lax.ppermute only.
A program may use at most 256 MiB of HBM per device.

v0:
```python
import jax
import jax.numpy as jnp
from jax import lax
from jax.sharding import PartitionSpec as P


def local(front_entries, child_blocks, dest_device, dest_tile, child_count, diag_inverse):
    grp_total = lax.axis_size("grp")
    front_total = lax.axis_size("front")
    device_total = grp_total * front_total
    children_dev, block_rows, block_cols = child_blocks.shape
    capacity = max(2, 2 * children_dev // device_total)
    rows_dev = front_entries.shape[1]
    width = front_entries.shape[2]
    panel_count = diag_inverse.shape[1]
    panel = diag_inverse.shape[2]
    pivots = panel // grp_total
    tiles_dev = rows_dev // block_rows * (width // block_cols)
    active = jnp.arange(children_dev, dtype=jnp.int32) < child_count[0]
    target = dest_device[:, 0]
    onehot = (target[:, None] == jnp.arange(device_total, dtype=jnp.int32)[None, :]).astype(
        jnp.int32
    )
    occurrence = jnp.sum(jnp.cumsum(onehot, axis=0) * onehot, axis=1) - 1
    position = target * capacity + occurrence
    blocks = jnp.where(active[:, None, None], child_blocks, jnp.zeros_like(child_blocks))
    outgoing = (
        jnp.zeros((device_total * capacity, block_rows, block_cols), jnp.bfloat16)
        .at[position]
        .set(blocks)
    )
    labels = (
        jnp.full((device_total * capacity,), tiles_dev, jnp.int32)
        .at[position]
        .set(jnp.where(active, dest_tile, tiles_dev))
    )
    arrived, arrived_labels = (
        lax.all_to_all(
            outgoing.reshape(device_total, capacity, block_rows, block_cols),
            ("front", "grp"),
            split_axis=0,
            concat_axis=0,
            tiled=True,
        ),
        lax.all_to_all(
            labels.reshape(device_total, capacity),
            ("front", "grp"),
            split_axis=0,
            concat_axis=0,
            tiled=True,
        ),
    )
    arrived = arrived.reshape(device_total * capacity, block_rows, block_cols)
    arrived_labels = arrived_labels.reshape(device_total * capacity)
    tiles = (
        jnp.zeros((tiles_dev, block_rows, block_cols), jnp.float32)
        .at[arrived_labels]
        .add(arrived.astype(jnp.float32), mode="drop")
    )
    added = (
        tiles.reshape(rows_dev // block_rows, width // block_cols, block_rows, block_cols)
        .transpose(0, 2, 1, 3)
        .reshape(rows_dev, width)
    )
    assembled = front_entries[0].astype(jnp.float32) + added
    current = assembled.reshape(rows_dev, grp_total, rows_dev)
    factors = []
    for step in range(panel_count):
        height = rows_dev - step * pivots
        rest = height - pivots
        panel_cols = current[:, :, :pivots].reshape(height, panel)
        inverse = diag_inverse[0, step]
        factor = jnp.dot(
            panel_cols,
            inverse.T,
            precision=lax.Precision.HIGHEST,
            preferred_element_type=jnp.float32,
        )
        factors.append(
            jnp.concatenate([jnp.zeros((step * pivots, panel), jnp.float32), factor], axis=0)
        )
        own_rows = factor[pivots:]
        trailing = current[pivots:, :, pivots:].reshape(rest, grp_total * rest)

        def update_from_factor(piece, start, own_rows=own_rows):
            return jnp.dot(
                own_rows,
                piece.T,
                precision=lax.Precision.HIGHEST,
                preferred_element_type=jnp.float32,
            )

        correction = update_from_factor(
            lax.all_gather(own_rows, "grp", axis=0, tiled=True), jnp.int32(0)
        )
        current = (trailing - correction).reshape(rest, grp_total, rest)
    final_rows = current.shape[0]
    schur = current.reshape(final_rows, grp_total * final_rows).astype(jnp.bfloat16)
    return (schur[None], jnp.stack(factors)[None])


def solution(mesh):
    placed = (
        P("front", "grp", None),
        P(("front", "grp"), None, None),
        P(("front", "grp"), None),
        P(("front", "grp")),
        P(("front", "grp")),
        P("front", None, None, None),
    )
    return jax.shard_map(
        local,
        mesh=mesh,
        in_specs=placed,
        out_specs=(P("front", "grp", None), P("front", None, "grp", None)),
        check_vma=False,
    )
```

profile of v0, /device:TPU:1, one launch (start us, length us, event | category | flops | bytes accessed | tf_op | source)
XLA Modules:
  0.0 582.3 jit_solution(7986387056649078374)
XLA Ops:
  10.9 1.0 scatter_custom_fusion
  12.6 11.5 %all-to-all-start = ((s32[128,1,2]{2,1,0:T(1,128)}), s32[128,1,2]{2,1,0:T(1,128)S(1)}, u32[]{:S(2)}, u32[]{:S(2)}) async-start(s32[128,1,2]{2,1,0:T(1,128)} %bitcast.4), calls=%async_computation | async-start | bytes 131072 | tf_op jit(solution)/shard_map/all_to_all | solution.py:45
  24.2 4.6 broadcast_select_fusion
  28.7 4.3 broadcast_in_dim.32
  33.0 19.3 %scatter_fusion = bf16[256,32,512]{2,1,0:T(8,128)(2,1)} fusion(bf16[256,32,512]{2,1,0:T(8,128)(2,1)} %broadcast_in_dim.32, s32[128]{0:T(128)S(1)} %fusion.8, bf16[128,32,512]{2,1,0:T(8,128)(2,1)} %broadcast_select_fusion), kind=kCustom, calls=%fused_computation.1 | custom fusion | bytes 12583424 | tf_op jit(solution)/shard_map/scatter | solution.py:30
  52.3 10.2 %all-to-all-start.1 = ((bf16[128,2,32,512]{3,2,1,0:T(8,128)(2,1)}), bf16[128,2,32,512]{3,2,1,0:T(8,128)(2,1)}, u32[]{:S(2)}, u32[]{:S(2)}) async-start(bf16[128,2,32,512]{3,2,1,0:T(8,128)(2,1)} %bitcast.46), calls=%async_computation.1 | async-start | bytes 16777216 | tf_op jit(solution)/shard_map/all_to_all | solution.py:38
  63.1 17.4 %copy.19 = f32[64,8,16,512]{3,2,1,0:T(8,128)} copy(bf16[64,8,16,512]{3,1,2,0:T(8,128)(2,1)} %bitcast.48) | data formatting | bytes 25165824
  82.0 81.8 %all-to-all-done.1 = bf16[128,2,32,512]{3,2,1,0:T(8,128)(2,1)} async-done(((bf16[128,2,32,512]{3,2,1,0:T(8,128)(2,1)}), bf16[128,2,32,512]{3,2,1,0:T(8,128)(2,1)}, u32[]{:S(2)}, u32[]{:S(2)}) %all-to-all-start.1) | async-done | bytes 8388640 | tf_op jit(solution)/shard_map/all_to_all | solution.py:38
  163.8 11.5 %bitcast_convert_fusion = f32[256,32,512]{2,1,0:T(8,128)} fusion(bf16[128,2,32,512]{3,2,1,0:T(8,128)(2,1)} %all-to-all-done.1), kind=kLoop, calls=%fused_computation.7 | loop fusion | flops 4194304 | bytes 25165824 | tf_op jit(solution)/shard_map/convert_element_type | solution.py:58
  175.3 7.9 %broadcast_in_dim.31 = f32[256,32,512]{2,1,0:T(8,128)} broadcast(f32[]{:T(128)} %constant.6.clone.1), dimensions={} | broadcast | bytes 16777220 | tf_op jit(solution)/shard_map/broadcast_in_dim | solution.py:56
  183.1 51.0 %scatter_fusion.1 = f32[256,32,512]{2,1,0:T(8,128)} fusion(f32[256,32,512]{2,1,0:T(8,128)} %broadcast_in_dim.31, s32[256]{0:T(256)S(1)} %bitcast.51, f32[256,32,512]{2,1,0:T(8,128)} %bitcast_convert_fusion), kind=kCustom, calls=%fused_computation.2 | custom fusion | flops 4194304 | bytes 50332672 | tf_op jit(solution)/shard_map/scatter-add | solution.py:58
  234.1 17.7 %copy.15 = f32[16,32,16,512]{3,2,1,0:T(8,128)} copy(f32[16,32,16,512]{3,1,2,0:T(8,128)} %bitcast.45) | data formatting | bytes 33554432 | tf_op jit(solution)/shard_map/transpose | solution.py:62
  251.8 11.9 %bitcast_add_fusion = f32[512,16,512]{2,1,0:T(8,128)S(1)} fusion(f32[64,8,16,512]{3,2,1,0:T(8,128)} %copy.19, f32[16,32,16,512]{3,2,1,0:T(8,128)} %copy.15), kind=kLoop, calls=%fused_computation.3 | loop fusion | flops 4194304 | bytes 50331648 | tf_op jit(solution)/shard_map/add | solution.py:65
  263.7 5.8 copy-done
  269.5 2.6 slice.33
  272.1 2.8 copy.16
  275.0 4.7 fusion.3
  279.7 1.0 slice.34
  281.0 15.8 %slice.32 = f32[480,16,480]{2,1,0:T(8,128)} slice(f32[512,16,512]{2,1,0:T(8,128)} %copy-done), slice={[32:512], [0:16], [32:512]} | slice | bytes 29491200 | tf_op jit(solution)/shard_map/slice | solution.py:83
  296.7 17.5 %reshape.89 = f32[480,7680]{1,0:T(8,128)} reshape(f32[480,16,480]{2,1,0:T(8,128)} %slice.32) | data formatting | bytes 29491200 | tf_op jit(solution)/shard_map/reshape | solution.py:83
  314.2 74.1 %all-gather.3.cloned.1.call-done = f32[7680,512]{1,0:T(8,128)} async-done(((f32[480,512]{1,0:T(8,128)}), f32[7680,512]{1,0:T(8,128)}) %all-gather.3.cloned.1.call-update) | async-done | bytes 15728656 | tf_op jit(solution)/shard_map/all_gather | solution.py:94
  388.3 29.1 %convolution_subtract_fusion = f32[480,7680]{1,0:T(8,128)} fusion(f32[480,7680]{1,0:T(8,128)} %reshape.89, f32[7680,512]{1,0:T(8,128)} %all-gather.3.cloned.1.call-done, f32[512,512]{1,0:T(8,128)S(1)} %fusion.3), kind=kOutput, calls=%fused_computation.5 | convolution fusion | flops 22652928000 | bytes 46202880 | tf_op jit(solution)/shard_map/dot_general | solution.py:86
  417.4 18.2 %reshape.91 = f32[480,16,480]{2,1,0:T(8,128)} reshape(f32[480,7680]{1,0:T(8,128)} %convolution_subtract_fusion) | data formatting | bytes 29491200 | tf_op jit(solution)/shard_map/reshape | solution.py:96
  435.6 4.3 slice.36
  439.9 3.0 copy.18
  442.8 4.7 fusion.1
  447.5 1.0 slice.37
  448.5 14.6 %slice.35 = f32[448,16,448]{2,1,0:T(8,128)} slice(f32[480,16,480]{2,1,0:T(8,128)} %reshape.91), slice={[32:480], [0:16], [32:480]} | slice | bytes 25690112 | tf_op jit(solution)/shard_map/slice | solution.py:83
  463.1 16.5 %reshape.92 = f32[448,7168]{1,0:T(8,128)} reshape(f32[448,16,448]{2,1,0:T(8,128)} %slice.35) | data formatting | bytes 25690112 | tf_op jit(solution)/shard_map/reshape | solution.py:83
  479.7 1.5 maximum_bitcast_fusion
  481.3 67.7 %all-gather.5.cloned.1.call-done = f32[7168,512]{1,0:T(8,128)} async-done(((f32[448,512]{1,0:T(8,128)}), f32[7168,512]{1,0:T(8,128)}) %all-gather.5.cloned.1.call-update) | async-done | bytes 14680080 | tf_op jit(solution)/shard_map/all_gather | solution.py:94
  549.0 25.9 %fusion = bf16[1,448,7168]{2,1,0:T(8,128)(2,1)} fusion(f32[448,7168]{1,0:T(8,128)} %reshape.92, f32[7168,512]{1,0:T(8,128)} %all-gather.5.cloned.1.call-done, f32[480,512]{1,0:T(8,128)S(1)} %fusion.1), kind=kOutput, calls=%fused_computation.6 | convolution fusion | flops 19736428544 | bytes 34865152 | tf_op jit(solution)/shard_map/dot_general | solution.py:86
  (18 shorter events, 6.2 us)
Async XLA Ops:
  12.6 39.7 %all-to-all-start = ((s32[128,1,2]{2,1,0:T(1,128)}), s32[128,1,2]{2,1,0:T(1,128)S(1)}, u32[]{:S(2)}, u32[]{:S(2)}) async-start(s32[128,1,2]{2,1,0:T(1,128)} %bitcast.4), calls=%async_computation | async-start | bytes 131072 | tf_op jit(solution)/shard_map/all_to_all | solution.py:45
  52.3 111.4 %all-to-all-start.1 = ((bf16[128,2,32,512]{3,2,1,0:T(8,128)(2,1)}), bf16[128,2,32,512]{3,2,1,0:T(8,128)(2,1)}, u32[]{:S(2)}, u32[]{:S(2)}) async-start(bf16[128,2,32,512]{3,2,1,0:T(8,128)(2,1)} %bitcast.46), calls=%async_computation.1 | async-start | bytes 16777216 | tf_op jit(solution)/shard_map/all_to_all | solution.py:38
  62.6 325.7 %all-gather.3.cloned.1.call-start = ((), (), s32[]{:S(2)}) async-start(), calls=%async_computation.2 | async-start | bytes 16711680 | tf_op jit(solution)/shard_map/all_gather | solution.py:94
  263.7 5.8 copy-start
  280.7 268.3 %all-gather.5.cloned.1.call-start = ((), (), s32[]{:S(2)}) async-start(), calls=%async_computation.3 | async-start | bytes 15597568 | tf_op jit(solution)/shard_map/all_gather | solution.py:94
Sparse Core Ops, SparseCore 0:
  280.8 107.4 all-gather.2
  448.7 100.3 all-gather.4
where the time goes:
time: 588 us; the launch traced here: 582 us
  waiting for transfers between devices  224 us (38%)
  local copies, waits for them, and re-layouts  172 us (29%)
  other arithmetic  84.4 us (14%)
  matrix products  64.4 us (11%)
  starting transfers between devices  22.5 us (4%)
  between operations  15.3 us (3%)
    all_gather x2, waiting for transfers between devices, local(): lax.all_gather(own_rows, 'grp', axis=0, tiled=True)  142 us
    all_to_all x1, waiting for transfers between devices, local(): lax.all_to_all(outgoing.reshape(device_total, capacity, block_rows, block...  81.8 us
    dot_general x2, matrix products, update_from_factor(): jnp.dot(own_rows, piece.T, precision=lax.Precision.HIGHEST, preferred_ele...  55.1 us
    scatter-add x1, other arithmetic, local(): tiles = jnp.zeros((tiles_dev, block_rows, block_cols), jnp.float32).at[ar...  51 us
    reshape x2, local copies, waits for them, and re-layouts, local(): trailing = current[pivots:, :, pivots:].reshape(rest, grp_total * rest)  34 us
    slice x2, local copies, waits for them, and re-layouts, local(): trailing = current[pivots:, :, pivots:].reshape(rest, grp_total * rest)  30.4 us
    unnamed x4, local copies, waits for them, and re-layouts  26.1 us
    scatter x1, local copies, waits for them, and re-layouts, local(): outgoing = jnp.zeros((device_total * capacity, block_rows, block_cols), j...  19.3 us
  transfers between devices with their start and end apart: 4, of which 3 were waited for; matrix products, arithmetic and copies ran while one was open for 19% of the time, Pallas kernels for 0%

commit v1 on v0

v1 whole, which is shorter than its diff:
```python
import functools

import jax
import jax.numpy as jnp
from jax import lax
from jax.experimental import pallas as pl
from jax.experimental.pallas import tpu as pltpu
from jax.sharding import PartitionSpec as P

LANE = 128
ROWTILE = 16
VMEM_LIMIT = 56 * 1024 * 1024
NT = (((1,), (1,)), ((), ()))


def params():
    return pltpu.CompilerParams(vmem_limit_bytes=VMEM_LIMIT)


def split(x):
    high = x.astype(jnp.bfloat16)
    return high, (x - high.astype(jnp.float32)).astype(jnp.bfloat16)


def dot_nt(a, b):
    return lax.dot_general(a, b, NT, preferred_element_type=jnp.float32)


def dot3(a, b):
    a_high, a_low = a
    b_high, b_low = b
    return dot_nt(a_high, b_high) + (dot_nt(a_high, b_low) + dot_nt(a_low, b_high))


def split_code(code):
    wide = code.astype(jnp.int32)
    high = ((wide + 128) >> 8) << 8
    low = wide - high
    return (
        high.astype(jnp.float32).astype(jnp.bfloat16),
        low.astype(jnp.float32).astype(jnp.bfloat16),
    )


def encode(x):
    rows = x.shape[0]
    largest = jnp.max(jnp.abs(x), axis=1, keepdims=True)
    exponent = jnp.ceil(jnp.log2(jnp.clip(largest, 1e-30, 1e38)))
    scaled = jnp.round(x * jnp.exp2(15.0 - exponent))
    code = jnp.clip(scaled, -32767.0, 32767.0).astype(jnp.int32).astype(jnp.int16)
    along = jnp.transpose(jnp.broadcast_to(exponent, (rows, LANE)))[:ROWTILE]
    return code, along.astype(jnp.int32).astype(jnp.int16)


def scale_of(exponent):
    return jnp.exp2(exponent.astype(jnp.int32).astype(jnp.float32) - 15.0)


def pack_first_kernel(count, position, blocks, labels, out, sem, label_sem):
    slots, rows, _ = blocks.shape

    def copy(i):
        at = position[i]
        return pltpu.make_async_copy(
            blocks.at[i, :, pl.ds(0, LANE)],
            out.at[at // 2, pl.ds(pl.multiple_of((at % 2) * rows, rows), rows), :],
            sem,
        )

    label_copy = pltpu.make_async_copy(labels, out.at[:, pl.ds(2 * rows, ROWTILE), :], label_sem)
    label_copy.start()

    @pl.loop(0, count[0])
    def _(i):
        copy(i).start()

    label_copy.wait()

    @pl.loop(0, count[0])
    def _(i):
        copy(i).wait()


def pack_rest_kernel(count, position, blocks, out, sem):
    width = blocks.shape[2]

    def copy(i):
        return pltpu.make_async_copy(
            blocks.at[i, :, pl.ds(LANE, width - LANE)], out.at[position[i]], sem
        )

    @pl.loop(0, count[0])
    def _(i):
        copy(i).start()

    @pl.loop(0, count[0])
    def _(i):
        copy(i).wait()


def gather_lanes(acc, start, width, groups):
    rows = acc.shape[1]
    per = LANE // width
    lane = lax.broadcasted_iota(jnp.int32, (rows, LANE), 1)
    out = []
    for tile in range(groups // per):
        total = None
        for k in range(per):
            piece = acc[tile * per + k]
            shift = (k * width - start) % LANE
            if shift:
                piece = pltpu.roll(piece, shift, 1)
            total = piece if total is None else jnp.where(lane >= k * width, piece, total)
        out.append(total)
    return jnp.concatenate(out, axis=1)


def panel_kernel(pivots, slot_count, label, arrived, front, inverse, factor, second, code, entries, acc, sem):
    groups, rows, _ = acc.shape
    block_rows = rows // groups
    width = front.shape[2] // groups

    def copy(c):
        return pltpu.make_async_copy(
            front.at[0, :, pl.ds(c * width, LANE)], entries.at[c], sem.at[c]
        )

    for c in range(groups):
        copy(c).start()
    for c in range(groups):
        copy(c).wait()
        acc[c] = entries[c].astype(jnp.float32)

    @pl.loop(0, slot_count)
    def _(s):
        at = label[s]

        @pl.when(at >= 0)
        def _():
            r, c = at // groups, at % groups
            where = pl.ds(pl.multiple_of(r * block_rows, block_rows), block_rows)
            source = pl.ds(pl.multiple_of((s % 2) * block_rows, block_rows), block_rows)
            acc[c, where, :] += arrived[s // 2, source, :].astype(jnp.float32)

    second[...] = gather_lanes(acc, pivots, pivots, groups)
    columns = gather_lanes(acc, 0, pivots, groups)
    result = dot3(split(columns), split(inverse[0, 0]))
    factor[...] = result
    codes, exponents = encode(result)
    code[: rows - pivots] = codes[pivots:]
    code[rows - pivots :] = exponents


def second_kernel(pivots, gathered, factor, second, inverse, factors, code, pivot_code, exponent, sem):
    groups = gathered.shape[0]
    rows, panel = factor.shape
    copies = [
        pltpu.make_async_copy(gathered.at[:, pl.ds(0, pivots), :], pivot_code, sem.at[0]),
        pltpu.make_async_copy(
            gathered.at[:, pl.ds(rows - pivots, ROWTILE), :], exponent, sem.at[1]
        ),
    ]
    for copy in copies:
        copy.start()
    factors[0, 0] = factor[...]
    for copy in copies:
        copy.wait()
    lane = lax.broadcasted_iota(jnp.int32, (ROWTILE, panel), 1)
    total = jnp.zeros((ROWTILE, panel), jnp.float32)
    for g in range(groups):
        scale = pltpu.roll(scale_of(exponent[g]), (g * pivots - pivots) % panel, 1)
        total = jnp.where((lane >= g * pivots) & (lane < (g + 1) * pivots), scale, total)
    pivot_rows = split_code(pivot_code[...].reshape(groups * pivots, panel))
    update = dot3(split(factor[pivots:]), pivot_rows) * total[:1]
    result = dot3(split(second[pivots:] - update), split(inverse[0, 0]))
    factors[0, 1, :pivots] = jnp.zeros((pivots, panel), jnp.float32)
    factors[0, 1, pivots:] = result
    codes, exponents = encode(jnp.concatenate([jnp.zeros((pivots, panel), jnp.float32), result], axis=0))
    code[: rows - 2 * pivots] = codes[2 * pivots :]
    code[rows - 2 * pivots :] = exponents


def update_kernel(pivots, factors, code0, code1, out, left, right):
    rows, panel = factors.shape[2], factors.shape[3]
    dead = 2 * pivots

    @pl.when(pl.program_id(0) == 0)
    def _():
        for k in range(2):
            high, low = split(factors[0, k, dead:])
            left[k, :, :panel] = high
            left[k, :, panel : 2 * panel] = high
            left[k, :, 2 * panel :] = low
            right[k] = jnp.zeros(right.shape[1:], jnp.bfloat16)

    total = None
    for k, code in enumerate((code0, code1)):
        first = (k + 1) * pivots
        kept = rows - first
        high, low = split_code(code[0, :kept])
        right[k, first:, :panel] = high
        right[k, first:, panel : 2 * panel] = low
        right[k, first:, 2 * panel :] = high
        scale = scale_of(code[0, kept : kept + ROWTILE])[:1]
        term = dot_nt(left[k], right[k]) * scale
        total = term if total is None else total + term
    out[...] = total


def finish_kernel(pivots, slot_count, label, first, rest, front, update, out, head, follow, buf):
    groups, block_rows, width = buf.shape
    dead = 2 * pivots
    step = pl.program_id(0)
    skipped = dead // block_rows

    @pl.when(step == 0)
    def _():
        @pl.loop(0, groups)
        def _(r):
            head[r] = -1

        @pl.loop(0, slot_count)
        def _(s):
            at = label[s]

            @pl.when(at >= 0)
            def _():
                r = at // groups
                follow[s] = head[r]
                head[r] = s

    for c in range(groups):
        columns = slice(c * width, (c + 1) * width)
        buf[c] = front[0, :, columns].astype(jnp.float32) - update[:, columns]

    def more(s):
        return s >= 0

    def add(s):
        c = label[s] % groups
        source = pl.ds(pl.multiple_of((s % 2) * block_rows, block_rows), block_rows)
        buf[c, :, :LANE] += first[s // 2, source, :].astype(jnp.float32)
        buf[c, :, LANE:] += rest[s].astype(jnp.float32)
        return follow[s]

    lax.while_loop(more, add, head[step + skipped])

    kept = width - dead
    for m in range(groups // 2):
        pair = jnp.concatenate([buf[2 * m][:, dead:], buf[2 * m + 1][:, dead:]], axis=1)
        out[0, :, 2 * m * kept : 2 * (m + 1) * kept] = pair.astype(jnp.bfloat16)


def local(front_entries, child_blocks, dest_device, dest_tile, child_count, diag_inverse):
    grp_total = lax.axis_size("grp")
    device_total = grp_total * lax.axis_size("front")
    axes = ("front", "grp")
    slots, block_rows, block_cols = child_blocks.shape
    _, rows, width = front_entries.shape
    panel = diag_inverse.shape[2]
    pivots = panel // grp_total
    slot_count = 2 * device_total
    rest_cols = block_cols - LANE
    hbm = pl.BlockSpec(memory_space=pl.ANY)
    smem = pl.BlockSpec(memory_space=pltpu.SMEM)
    vmem = pl.BlockSpec(memory_space=pltpu.VMEM)

    target = dest_device[:, 0]
    index = jnp.arange(slots, dtype=jnp.int32)
    same = (target[:, None] == target[None, :]) & (index[None, :] < index[:, None])
    occurrence = jnp.sum(same.astype(jnp.int32), axis=1)
    position = target * 2 + occurrence
    names = jnp.arange(slot_count, dtype=jnp.int32)
    live_label = jnp.where(index < child_count[0], dest_tile + 1, 0)
    labels = jnp.sum(
        jnp.where(position[None, :] == names[:, None], live_label[None, :], 0), axis=1
    ).reshape(device_total, 2)
    label_rows = jnp.concatenate(
        [
            jnp.broadcast_to(labels[:, :, None], (device_total, 2, LANE)),
            jnp.zeros((device_total, ROWTILE - 2, LANE), jnp.int32),
        ],
        axis=1,
    ).astype(jnp.bfloat16)

    first_out = pl.pallas_call(
        pack_first_kernel,
        out_shape=jax.ShapeDtypeStruct(
            (device_total, 2 * block_rows + ROWTILE, LANE), jnp.bfloat16
        ),
        in_specs=[smem, smem, hbm, hbm],
        out_specs=hbm,
        scratch_shapes=[pltpu.SemaphoreType.DMA, pltpu.SemaphoreType.DMA],
        compiler_params=params(),
        name="pack_first",
    )(child_count, position, child_blocks, label_rows)
    first = lax.all_to_all(first_out, axes, split_axis=0, concat_axis=0, tiled=True)
    rest_out = pl.pallas_call(
        pack_rest_kernel,
        out_shape=jax.ShapeDtypeStruct((slot_count, block_rows, rest_cols), jnp.bfloat16),
        in_specs=[smem, smem, hbm],
        out_specs=hbm,
        scratch_shapes=[pltpu.SemaphoreType.DMA],
        compiler_params=params(),
        name="pack_rest",
    )(child_count, position, child_blocks)
    first, rest_out = lax.optimization_barrier((first, rest_out))
    rest = lax.all_to_all(rest_out, axes, split_axis=0, concat_axis=0, tiled=True)
    label = first[:, 2 * block_rows : 2 * block_rows + 2, 0].astype(jnp.int32).reshape(-1) - 1

    code_rows = rows - pivots + ROWTILE
    inverse_spec = lambda k: pl.BlockSpec((1, 1, panel, panel), lambda i: (0, k, 0, 0))
    whole = lambda *shape: pl.BlockSpec(shape, lambda i: (0,) * len(shape))
    factor, second, code0 = pl.pallas_call(
        functools.partial(panel_kernel, pivots, slot_count),
        grid=(1,),
        out_shape=(
            jax.ShapeDtypeStruct((rows, panel), jnp.float32),
            jax.ShapeDtypeStruct((rows, panel), jnp.float32),
            jax.ShapeDtypeStruct((code_rows, panel), jnp.int16),
        ),
        in_specs=[smem, whole(*first.shape), hbm, inverse_spec(0)],
        out_specs=(whole(rows, panel), whole(rows, panel), whole(code_rows, panel)),
        scratch_shapes=[
            pltpu.VMEM((grp_total, rows, LANE), jnp.bfloat16),
            pltpu.VMEM((grp_total, rows, LANE), jnp.float32),
            pltpu.SemaphoreType.DMA((grp_total,)),
        ],
        compiler_params=params(),
        cost_estimate=pl.CostEstimate(flops=2 * 10**9, bytes_accessed=10 * 2**20, transcendentals=0),
        name="first_panel",
    )(label, first, front_entries, diag_inverse)
    gathered0 = lax.all_gather(code0, "grp", axis=0, tiled=False)

    code_rows1 = code_rows - pivots
    factors, code1 = pl.pallas_call(
        functools.partial(second_kernel, pivots),
        grid=(1,),
        out_shape=(
            jax.ShapeDtypeStruct((1, 2, rows, panel), jnp.float32),
            jax.ShapeDtypeStruct((code_rows1, panel), jnp.int16),
        ),
        in_specs=[hbm, whole(rows, panel), whole(rows, panel), inverse_spec(1)],
        out_specs=(whole(1, 2, rows, panel), whole(code_rows1, panel)),
        scratch_shapes=[
            pltpu.VMEM((grp_total, pivots, panel), jnp.int16),
            pltpu.VMEM((grp_total, ROWTILE, panel), jnp.int16),
            pltpu.SemaphoreType.DMA((2,)),
        ],
        compiler_params=params(),
        cost_estimate=pl.CostEstimate(flops=4 * 10**9, bytes_accessed=8 * 2**20, transcendentals=0),
        name="second_panel",
    )(gathered0, factor, second, diag_inverse)
    gathered1 = lax.all_gather(code1, "grp", axis=0, tiled=False)

    kept = rows - 2 * pivots
    update = pl.pallas_call(
        functools.partial(update_kernel, pivots),
        grid=(grp_total,),
        out_shape=jax.ShapeDtypeStruct((kept, width), jnp.float32),
        in_specs=[
            whole(1, 2, rows, panel),
            pl.BlockSpec((1, code_rows, panel), lambda i: (i, 0, 0)),
            pl.BlockSpec((1, code_rows1, panel), lambda i: (i, 0, 0)),
        ],
        out_specs=pl.BlockSpec((kept, rows), lambda i: (0, i)),
        scratch_shapes=[
            pltpu.VMEM((2, kept, 3 * panel), jnp.bfloat16),
            pltpu.VMEM((2, rows, 3 * panel), jnp.bfloat16),
        ],
        compiler_params=params(),
        cost_estimate=pl.CostEstimate(flops=20 * 10**9, bytes_accessed=32 * 2**20, transcendentals=0),
        name="update",
    )(factors, gathered0, gathered1)

    row_blocks = rows // block_rows
    skipped = 2 * pivots // block_rows
    schur = pl.pallas_call(
        functools.partial(finish_kernel, pivots, slot_count),
        grid=(row_blocks - skipped,),
        out_shape=jax.ShapeDtypeStruct((1, kept, grp_total * kept), jnp.bfloat16),
        in_specs=[
            smem,
            whole(*first.shape),
            whole(*rest.shape),
            pl.BlockSpec((1, block_rows, width), lambda i: (0, i + skipped, 0)),
            pl.BlockSpec((block_rows, width), lambda i: (i, 0)),
        ],
        out_specs=pl.BlockSpec((1, block_rows, grp_total * kept), lambda i: (0, i, 0)),
        scratch_shapes=[
            pltpu.SMEM((row_blocks,), jnp.int32),
            pltpu.SMEM((slot_count,), jnp.int32),
            pltpu.VMEM((width // block_cols, block_rows, block_cols), jnp.float32),
        ],
        compiler_params=params(),
        cost_estimate=pl.CostEstimate(flops=10**7, bytes_accessed=40 * 2**20, transcendentals=0),
        name="finish",
    )(label, first, rest, front_entries, update)
    return schur, factors


def solution(mesh):
    placed = (
        P("front", "grp", None),
        P(("front", "grp"), None, None),
        P(("front", "grp"), None),
        P(("front", "grp")),
        P(("front", "grp")),
        P("front", None, None, None),
    )
    return jax.shard_map(
        local,
        mesh=mesh,
        in_specs=placed,
        out_specs=(P("front", "grp", None), P("front", None, "grp", None)),
        check_vma=False,
    )
```

time: 588 us -> 395 us (0.67)
  waiting for transfers between devices: 224 us -> 0.01 us
  Pallas kernels: 0 us -> 203 us
  local copies, waits for them, and re-layouts: 172 us -> 1.92 us
  blocking collectives: 0 us -> 145 us
  other arithmetic: 84.4 us -> 3.93 us
  matrix products: 64.4 us -> 0 us
  between operations: 15.3 us -> 1.38 us
  starting transfers between devices: 22.5 us -> 35.5 us
    pallas_call x0 -> x6, Pallas kernels: none -> 203 us  [the longest x1 84.5 us: local(): pl.pallas_call(pack_rest_kernel, out_shape=jax.ShapeDtypeStruct((slot_cou...]
    all_gather x0 -> x2, blocking collectives: none -> 145 us  [the longest x1 100 us: local(): gathered0 = lax.all_gather(code0, 'grp', axis=0, tiled=False)]
    all_gather x2 -> x0, waiting for transfers between devices: 142 us -> none  [local(): lax.all_gather(own_rows, 'grp', axis=0, tiled=True)]
    all_to_all x2, waiting for transfers between devices: 81.8 us -> 0.01 us  [the longest x1 0.01 us: local(): lax.all_to_all(first_out, axes, split_axis=0, concat_axis=0, tiled=True)]
    dot_general x4 -> x0, matrix products: 64.4 us -> none  [the longest x2 55.1 us: update_from_factor(): jnp.dot(own_rows, piece.T, precision=lax.Precision.HIGHEST, preferred_ele...]
    reshape x4 -> x0, local copies, waits for them, and re-layouts: 52.3 us -> none  [the longest x2 34 us: local(): trailing = current[pivots:, :, pivots:].reshape(rest, grp_total * rest)]
    scatter-add x1 -> x0, other arithmetic: 51 us -> none  [local(): tiles = jnp.zeros((tiles_dev, block_rows, block_cols), jnp.float32).at[ar...]
    slice x7 -> x0, local copies, waits for them, and re-layouts: 42.1 us -> none  [the longest x2 30.4 us: local(): trailing = current[pivots:, :, pivots:].reshape(rest, grp_total * rest)]
  transfers between devices with their start and end apart: 4 -> 2, of which waited for: 3 -> 0; matrix products, arithmetic and copies ran while one was open for 19% -> 1% of each run, Pallas kernels for 0% -> 34%
where the time goes in v1:
time: 395 us; the launch traced here: 391 us
  Pallas kernels  203 us (51%)
  blocking collectives  145 us (37%)
  starting transfers between devices  35.5 us (9%)
    all_gather x1, blocking collectives, local(): gathered0 = lax.all_gather(code0, 'grp', axis=0, tiled=False)  100 us
    pallas_call x1, Pallas kernels, local(): pl.pallas_call(pack_rest_kernel, out_shape=jax.ShapeDtypeStruct((slot_cou...  84.5 us
    pallas_call x1, Pallas kernels, local(): pl.pallas_call(pack_first_kernel, out_shape=jax.ShapeDtypeStruct((device_...  45.2 us
    all_gather x1, blocking collectives, local(): gathered1 = lax.all_gather(code1, 'grp', axis=0, tiled=False)  44.9 us
    pallas_call x1, Pallas kernels, local(): pl.pallas_call(functools.partial(update_kernel, pivots), grid=(grp_total,...  30.4 us
    pallas_call x1, Pallas kernels, local(): pl.pallas_call(functools.partial(finish_kernel, pivots, slot_count), grid...  23.2 us
    all_to_all x1, starting transfers between devices, local(): lax.all_to_all(rest_out, axes, split_axis=0, concat_axis=0, tiled=True)  21.3 us
    all_to_all x1, starting transfers between devices, local(): lax.all_to_all(first_out, axes, split_axis=0, concat_axis=0, tiled=True)  14.2 us
  transfers between devices with their start and end apart: 2, of which 0 were waited for; matrix products, arithmetic and copies ran while one was open for 1% of the time, Pallas kernels for 34%

profile of v1, /device:TPU:1, one launch (start us, length us, event | category | flops | bytes accessed | tf_op | source)
XLA Modules:
  0.0 391.1 jit_solution(13427953172769428828)
XLA Ops:
  1.3 0.9 convert_reduce_fusion
  2.2 0.7 compare_select_fusion
  2.9 0.0 copy-start.1
  2.9 0.1 select_reduce_fusion
  3.0 0.2 reshape.20
  3.2 0.2 broadcast_in_dim.33
  3.4 0.9 concatenate.3.labels
  4.2 0.0 copy-done.1
  4.2 45.2 %pack_first.1 = bf16[128,80,128]{2,1,0:T(8,128)(2,1)} custom-call(s32[1]{0:T(128)} %copy.8.count, s32[128]{0:T(128)} %copy-done.1, bf16[128,32,512]{2,1,0:T(8,128)(2,1)} %blocks.3, bf16[128,16,128]{2,1,0:T(8,128)(2,1)} %concatenate.3.labels), custom_call_target="tpu_custom_call" | custom-call | tf_op jit(solution)/shard_map/pack_first/pallas_call | solution.py:286
  49.5 14.2 %all-to-all-start = ((bf16[128,80,128]{2,1,0:T(8,128)(2,1)}), bf16[128,80,128]{2,1,0:T(8,128)(2,1)S(1)}, u32[]{:S(2)}, u32[]{:S(2)}) async-start(bf16[128,80,128]{2,1,0:T(8,128)(2,1)} %pack_first.1), calls=%async_computation | async-start | bytes 5242880 | tf_op jit(solution)/shard_map/all_to_all | solution.py:297
  63.7 84.5 %pack_rest.1 = bf16[256,32,384]{2,1,0:T(8,128)(2,1)} custom-call(s32[1]{0:T(128)} %copy.8.count, s32[128]{0:T(128)} %copy-done.1, bf16[128,32,512]{2,1,0:T(8,128)(2,1)} %blocks.3), custom_call_target="tpu_custom_call" | custom-call | tf_op jit(solution)/shard_map/pack_rest/pallas_call | solution.py:298
  148.1 0.0 all-to-all-done.arrived.first
  148.2 0.0 copy-start
  148.2 21.3 %all-to-all-start.1 = ((bf16[256,32,384]{2,1,0:T(8,128)(2,1)}), bf16[256,32,384]{2,1,0:T(8,128)(2,1)}, u32[]{:S(2)}, u32[]{:S(2)}) async-start(bf16[256,32,384]{2,1,0:T(8,128)(2,1)} %pack_rest.1), calls=%async_computation.1 | async-start | bytes 12582912 | tf_op jit(solution)/shard_map/all_to_all | solution.py:308
  169.5 0.0 copy-done
  169.5 2.2 add_reduce_fusion
  171.7 0.7 sub.7.label
  172.4 13.8 %first_panel.1 = (f32[512,512]{1,0:T(8,128)}, f32[512,512]{1,0:T(8,128)}, s16[496,512]{1,0:T(8,128)(2,1)}) custom-call(s32[256]{0:T(256)} %sub.7.label, bf16[128,80,128]{2,1,0:T(8,128)(2,1)} %copy-done, bf16[1,512,8192]{2,1,0:T(8,128)(2,1)} %front.3, f32[1,2,512,512]{3,2,1,0:T(8,128)} %inverse.3), custom_call_target="tpu_custom_call" | custom-call | flops 2000000000 | bytes 10485760 | tf_op jit(solution)/shard_map/first_panel/pallas_call | solution.py:314
  186.2 100.3 %all-gather.4 = s16[7936,512]{1,0:T(8,128)(2,1)} all-gather(s16[496,512]{1,0:T(8,128)(2,1)} %get-tuple-element.11), channel_id=2, replica_groups=mesh['front'=8,'grp'=16] {'grp'}, dimensions={0}, use_global_device_ids=true | all-gather | bytes 8634368 | tf_op jit(solution)/shard_map/all_gather | solution.py:333
  286.5 6.3 %second_panel.1 = (f32[1,2,512,512]{3,2,1,0:T(8,128)}, s16[464,512]{1,0:T(8,128)(2,1)}) custom-call(s16[16,496,512]{2,1,0:T(8,128)(2,1)} %bitcast.6, f32[512,512]{1,0:T(8,128)} %get-tuple-element.12.factor, f32[512,512]{1,0:T(8,128)} %get-tuple-element.13.second, f32[1,2,512,512]{3,2,1,0:T(8,128)} %inverse.3), custom_call_target="tpu_custom_call" | custom-call | flops 4000000000 | bytes 8388608 | tf_op jit(solution)/shard_map/second_panel/pallas_call | solution.py:336
  292.7 44.9 %all-gather.5 = s16[7424,512]{1,0:T(8,128)(2,1)} all-gather(s16[464,512]{1,0:T(8,128)(2,1)} %get-tuple-element.15), channel_id=3, replica_groups=mesh['front'=8,'grp'=16] {'grp'}, dimensions={0}, use_global_device_ids=true | all-gather | bytes 8077312 | tf_op jit(solution)/shard_map/all_gather | solution.py:354
  337.6 30.4 %update.1 = f32[448,8192]{1,0:T(8,128)} custom-call(f32[1,2,512,512]{3,2,1,0:T(8,128)} %get-tuple-element.8.factors, s16[16,496,512]{2,1,0:T(8,128)(2,1)} %bitcast.7, s16[16,464,512]{2,1,0:T(8,128)(2,1)} %bitcast.8), custom_call_target="tpu_custom_call" | custom-call | flops 20000000000 | bytes 33554432 | tf_op jit(solution)/shard_map/update/pallas_call | solution.py:357
  368.0 0.0 all-to-all-done.1.rest
  368.0 23.2 %finish.1 = bf16[1,448,7168]{2,1,0:T(8,128)(2,1)} custom-call(s32[256]{0:T(256)} %sub.7.label, bf16[128,80,128]{2,1,0:T(8,128)(2,1)} %copy-done, bf16[256,32,384]{2,1,0:T(8,128)(2,1)} %all-to-all-done.1.rest, bf16[1,512,8192]{2,1,0:T(8,128)(2,1)} %front.3, f32[448,8192]{1,0:T(8,128)} %update.1), custom_call_target="tpu_custom_call" | custom-call | flops 10000000 | bytes 41943040 | tf_op jit(solution)/shard_map/finish/pallas_call | solution.py:378
  (1 shorter events, 0.0 us)
Async XLA Ops:
  2.9 1.4 copy-start.1
  49.5 98.7 %all-to-all-start = ((bf16[128,80,128]{2,1,0:T(8,128)(2,1)}), bf16[128,80,128]{2,1,0:T(8,128)(2,1)S(1)}, u32[]{:S(2)}, u32[]{:S(2)}) async-start(bf16[128,80,128]{2,1,0:T(8,128)(2,1)} %pack_first.1), calls=%async_computation | async-start | bytes 5242880 | tf_op jit(solution)/shard_map/all_to_all | solution.py:297
  148.2 21.3 %copy-start = (bf16[128,80,128]{2,1,0:T(8,128)(2,1)}, bf16[128,80,128]{2,1,0:T(8,128)(2,1)S(1)}, u32[]{:S(2)}) copy-start(bf16[128,80,128]{2,1,0:T(8,128)(2,1)S(1)} %all-to-all-done.arrived.first) | copy-start | bytes 7864324
  148.2 219.8 %all-to-all-start.1 = ((bf16[256,32,384]{2,1,0:T(8,128)(2,1)}), bf16[256,32,384]{2,1,0:T(8,128)(2,1)}, u32[]{:S(2)}, u32[]{:S(2)}) async-start(bf16[256,32,384]{2,1,0:T(8,128)(2,1)} %pack_rest.1), calls=%async_computation.1 | async-start | bytes 12582912 | tf_op jit(solution)/shard_map/all_to_all | solution.py:308

commit v2 on v1

v2 whole, which is shorter than its diff:
```python
import functools

import jax
import jax.numpy as jnp
from jax import lax
from jax.experimental import pallas as pl
from jax.experimental.pallas import tpu as pltpu
from jax.sharding import PartitionSpec as P

LANE = 128
ROWTILE = 16
VMEM_LIMIT = 56 * 1024 * 1024
NT = (((1,), (1,)), ((), ()))
NN = (((1,), (0,)), ((), ()))


def params():
    return pltpu.CompilerParams(vmem_limit_bytes=VMEM_LIMIT)


def split(x):
    high = x.astype(jnp.bfloat16)
    return high, (x - high.astype(jnp.float32)).astype(jnp.bfloat16)


def dot_nt(a, b, form=NT):
    return lax.dot_general(a, b, form, preferred_element_type=jnp.float32)


def dot3(a, b, form=NT):
    a_high, a_low = a
    b_high, b_low = b
    return dot_nt(a_high, b_high, form) + (
        dot_nt(a_high, b_low, form) + dot_nt(a_low, b_high, form)
    )


def split_code(code):
    wide = code.astype(jnp.int32)
    high = ((wide + 128) >> 8) << 8
    low = wide - high
    return (
        high.astype(jnp.float32).astype(jnp.bfloat16),
        low.astype(jnp.float32).astype(jnp.bfloat16),
    )


def encode(x):
    rows = x.shape[0]
    largest = jnp.max(jnp.abs(x), axis=1, keepdims=True)
    exponent = jnp.ceil(jnp.log2(jnp.clip(largest, 1e-30, 1e38)))
    scaled = jnp.round(x * jnp.exp2(15.0 - exponent))
    code = jnp.clip(scaled, -32767.0, 32767.0).astype(jnp.int32).astype(jnp.int16)
    along = jnp.transpose(jnp.broadcast_to(exponent, (rows, LANE)))[:ROWTILE]
    return code, along.astype(jnp.int32)


def scale_of(exponent):
    return jnp.exp2(exponent.astype(jnp.int32).astype(jnp.float32) - 15.0)


def pack_first_kernel(count, position, blocks, labels, out):
    rows = blocks.shape[1]
    out[:, 2 * rows :, :] = labels[...]

    @pl.loop(0, count[0])
    def _(i):
        at = position[i]
        out[at // 2, pl.ds(pl.multiple_of((at % 2) * rows, rows), rows), :] = blocks[i]


def pack_rest_kernel(count, position, blocks, out):
    @pl.loop(0, count[0])
    def _(i):
        out[position[i]] = blocks[i, :, LANE:]


def gather_lanes(acc, start, width, groups):
    rows = acc.shape[1]
    per = LANE // width
    lane = lax.broadcasted_iota(jnp.int32, (rows, LANE), 1)
    out = []
    for tile in range(groups // per):
        total = None
        for k in range(per):
            piece = acc[tile * per + k]
            shift = (k * width - start) % LANE
            if shift:
                piece = pltpu.roll(piece, shift, 1)
            total = piece if total is None else jnp.where(lane >= k * width, piece, total)
        out.append(total)
    return jnp.concatenate(out, axis=1)


def panel_kernel(
    pivots, slot_count, label, arrived, front, inverse, factor, second, middle, code, entries, acc, sem
):
    groups, rows, _ = acc.shape
    block_rows = rows // groups
    width = front.shape[2] // groups
    dead = 2 * pivots

    def copy(c):
        return pltpu.make_async_copy(
            front.at[0, :, pl.ds(c * width, LANE)], entries.at[c], sem.at[c]
        )

    for c in range(groups):
        copy(c).start()
    for c in range(groups):
        copy(c).wait()
        acc[c] = entries[c].astype(jnp.float32)

    @pl.loop(0, slot_count)
    def _(s):
        at = label[s]

        @pl.when(at >= 0)
        def _():
            r, c = at // groups, at % groups
            where = pl.ds(pl.multiple_of(r * block_rows, block_rows), block_rows)
            source = pl.ds(pl.multiple_of((s % 2) * block_rows, block_rows), block_rows)
            acc[c, where, :] += arrived[s // 2, source, :].astype(jnp.float32)

    middle[...] = acc[:, dead:, :]
    later = gather_lanes(acc, pivots, pivots, groups)
    second[...] = later
    columns = gather_lanes(acc, 0, pivots, groups)
    result = dot3(split(columns), split(inverse[0, 0]))
    factor[...] = result
    codes, exponents = encode(result)
    later_codes, later_exponents = encode(later)
    kept, kept_later = rows - pivots, rows - dead
    code[:kept] = codes[pivots:]
    code[kept : kept + kept_later] = later_codes[dead:]
    row = lax.broadcasted_iota(jnp.int32, exponents.shape, 0)
    code[kept + kept_later :] = jnp.where(row == 0, exponents, later_exponents).astype(jnp.int16)


def left_kernel(pivots, gathered, factor, second, inverse, factors, left, pivot_code, exponent, sem):
    groups, code_rows, _ = gathered.shape
    rows, panel = factor.shape
    copies = [
        pltpu.make_async_copy(gathered.at[:, pl.ds(0, pivots), :], pivot_code, sem.at[0]),
        pltpu.make_async_copy(
            gathered.at[:, pl.ds(code_rows - ROWTILE, ROWTILE), :], exponent, sem.at[1]
        ),
    ]
    for copy in copies:
        copy.start()
    factors[0, 0] = factor[...]
    for copy in copies:
        copy.wait()
    lane = lax.broadcasted_iota(jnp.int32, (ROWTILE, panel), 1)
    total = jnp.zeros((ROWTILE, panel), jnp.float32)
    for g in range(groups):
        scale = pltpu.roll(scale_of(exponent[g]), (g * pivots - pivots) % panel, 1)
        total = jnp.where((lane >= g * pivots) & (lane < (g + 1) * pivots), scale, total)
    scale = total[:1]
    pivot_rows = split_code(pivot_code[...].reshape(groups * pivots, panel))
    inverse_parts = split(inverse[0, 0])
    first = factor[pivots:]
    update = dot3(split(first), pivot_rows) * scale
    result = dot3(split(second[pivots:] - update), inverse_parts)
    factors[0, 1, :pivots] = jnp.zeros((pivots, panel), jnp.float32)
    factors[0, 1, pivots:] = result
    own = dot3(split(result[pivots:]), inverse_parts, NN)
    mixed = first[pivots:] - dot3(split(own * scale), pivot_rows, NN)
    for k, part in enumerate((mixed, own)):
        high, low = split(part)
        left[k, :, :panel] = high
        left[k, :, panel : 2 * panel] = high
        left[k, :, 2 * panel :] = low


def update_kernel(pivots, slot_count, label, left, code, front, middle, out, head, follow, right):
    rows, panel = right.shape[1], code.shape[2]
    groups = head.shape[0]
    dead = 2 * pivots

    @pl.when(pl.program_id(0) == 0)
    def _():
        right[...] = jnp.zeros(right.shape, jnp.bfloat16)

        @pl.loop(0, groups)
        def _(r):
            head[r] = -1

        @pl.loop(0, slot_count)
        def _(s):
            at = label[s]

            @pl.when(at >= 0)
            def _():
                r = at // groups
                follow[s] = head[r]
                head[r] = s

    kept = (rows - pivots, rows - dead)
    starts = (0, kept[0])
    sides = []
    for d in range(2):
        scale = scale_of(code[d, kept[0] + kept[1] :])
        columns = slice(d * rows + LANE, (d + 1) * rows)
        total = jnp.concatenate(
            [middle[d], front[0, dead:, columns].astype(jnp.float32)], axis=1
        )
        for k in range(2):
            high, low = split_code(code[d, starts[k] : starts[k] + kept[k]])
            right[k, rows - kept[k] :, :panel] = high
            right[k, rows - kept[k] :, panel : 2 * panel] = low
            right[k, rows - kept[k] :, 2 * panel :] = high
            total = total - dot_nt(left[k], right[k]) * scale[k : k + 1]
        sides.append(total[:, dead:])
    out[...] = jnp.concatenate(sides, axis=1)


def finish_kernel(label, head, follow, rest, trailing, out, buf):
    groups = head.shape[0]
    _, block_rows, width = rest.shape
    pairs, _, pair_width = buf.shape
    kept = pair_width // 2
    step = pl.program_id(0)
    skipped = groups - pl.num_programs(0)
    for m in range(pairs):
        buf[m] = trailing[:, m * pair_width : (m + 1) * pair_width]

    def more(s):
        return s >= 0

    def add(s):
        c = label[s] % groups
        m = c // 2
        block = rest[s].astype(jnp.float32)
        offset = kept - width

        @pl.when(c % 2 == 0)
        def _():
            pad = jnp.zeros((block_rows, offset), jnp.float32)
            buf[m, :, : width + 2 * offset] += jnp.concatenate([pad, block, pad], axis=1)

        @pl.when(c % 2 == 1)
        def _():
            buf[m, :, kept + offset :] += block

        return follow[s]

    lax.while_loop(more, add, head[step + skipped])
    for m in range(pairs):
        out[0, :, m * pair_width : (m + 1) * pair_width] = buf[m].astype(jnp.bfloat16)


def local(front_entries, child_blocks, dest_device, dest_tile, child_count, diag_inverse):
    grp_total = lax.axis_size("grp")
    device_total = grp_total * lax.axis_size("front")
    axes = ("front", "grp")
    slots, block_rows, block_cols = child_blocks.shape
    _, rows, width = front_entries.shape
    panel = diag_inverse.shape[2]
    pivots = panel // grp_total
    slot_count = 2 * device_total
    rest_cols = block_cols - LANE
    hbm = pl.BlockSpec(memory_space=pl.ANY)
    smem = pl.BlockSpec(memory_space=pltpu.SMEM)
    whole = lambda *shape: pl.BlockSpec(shape, lambda i: (0,) * len(shape))

    target = dest_device[:, 0]
    index = jnp.arange(slots, dtype=jnp.int32)
    same = (target[:, None] == target[None, :]) & (index[None, :] < index[:, None])
    occurrence = jnp.sum(same.astype(jnp.int32), axis=1)
    position = target * 2 + occurrence
    names = jnp.arange(slot_count, dtype=jnp.int32)
    live_label = jnp.where(index < child_count[0], dest_tile + 1, 0)
    labels = jnp.sum(
        jnp.where(position[None, :] == names[:, None], live_label[None, :], 0), axis=1
    ).reshape(device_total, 2)
    label_rows = jnp.concatenate(
        [
            jnp.broadcast_to(labels[:, :, None], (device_total, 2, LANE)),
            jnp.zeros((device_total, ROWTILE - 2, LANE), jnp.int32),
        ],
        axis=1,
    ).astype(jnp.bfloat16)

    first_out = pl.pallas_call(
        pack_first_kernel,
        grid=(1,),
        out_shape=jax.ShapeDtypeStruct(
            (device_total, 2 * block_rows + ROWTILE, LANE), jnp.bfloat16
        ),
        in_specs=[smem, smem, whole(slots, block_rows, LANE), whole(*label_rows.shape)],
        out_specs=whole(device_total, 2 * block_rows + ROWTILE, LANE),
        compiler_params=params(),
        name="pack_first",
    )(child_count, position, child_blocks, label_rows)
    first = lax.all_to_all(first_out, axes, split_axis=0, concat_axis=0, tiled=True)
    rest_out = pl.pallas_call(
        pack_rest_kernel,
        grid=(1,),
        out_shape=jax.ShapeDtypeStruct((slot_count, block_rows, rest_cols), jnp.bfloat16),
        in_specs=[smem, smem, whole(*child_blocks.shape)],
        out_specs=whole(slot_count, block_rows, rest_cols),
        compiler_params=params(),
        cost_estimate=pl.CostEstimate(flops=0, bytes_accessed=10 * 2**20, transcendentals=0),
        name="pack_rest",
    )(child_count, position, child_blocks)
    first, rest_out = lax.optimization_barrier((first, rest_out))
    label = first[:, 2 * block_rows : 2 * block_rows + 2, 0].astype(jnp.int32).reshape(-1) - 1

    kept = rows - 2 * pivots
    code_rows = (rows - pivots) + kept + ROWTILE
    inverse_spec = lambda k: pl.BlockSpec((1, 1, panel, panel), lambda i: (0, k, 0, 0))
    factor, second, middle, code = pl.pallas_call(
        functools.partial(panel_kernel, pivots, slot_count),
        grid=(1,),
        out_shape=(
            jax.ShapeDtypeStruct((rows, panel), jnp.float32),
            jax.ShapeDtypeStruct((rows, panel), jnp.float32),
            jax.ShapeDtypeStruct((grp_total, kept, LANE), jnp.float32),
            jax.ShapeDtypeStruct((code_rows, panel), jnp.int16),
        ),
        in_specs=[smem, whole(*first.shape), hbm, inverse_spec(0)],
        out_specs=(
            whole(rows, panel),
            whole(rows, panel),
            whole(grp_total, kept, LANE),
            whole(code_rows, panel),
        ),
        scratch_shapes=[
            pltpu.VMEM((grp_total, rows, LANE), jnp.bfloat16),
            pltpu.VMEM((grp_total, rows, LANE), jnp.float32),
            pltpu.SemaphoreType.DMA((grp_total,)),
        ],
        compiler_params=params(),
        cost_estimate=pl.CostEstimate(flops=2 * 10**9, bytes_accessed=10 * 2**20, transcendentals=0),
        name="panels",
    )(label, first, front_entries, diag_inverse)
    gathered = lax.all_gather(code, "grp", axis=0, tiled=False)

    gathered, rest_out = lax.optimization_barrier((gathered, rest_out))
    rest = lax.all_to_all(rest_out, axes, split_axis=0, concat_axis=0, tiled=True)

    factors, left = pl.pallas_call(
        functools.partial(left_kernel, pivots),
        grid=(1,),
        out_shape=(
            jax.ShapeDtypeStruct((1, 2, rows, panel), jnp.float32),
            jax.ShapeDtypeStruct((2, kept, 3 * panel), jnp.bfloat16),
        ),
        in_specs=[hbm, whole(rows, panel), whole(rows, panel), inverse_spec(1)],
        out_specs=(whole(1, 2, rows, panel), whole(2, kept, 3 * panel)),
        scratch_shapes=[
            pltpu.VMEM((grp_total, pivots, panel), jnp.int16),
            pltpu.VMEM((grp_total, ROWTILE, panel), jnp.int16),
            pltpu.SemaphoreType.DMA((2,)),
        ],
        compiler_params=params(),
        cost_estimate=pl.CostEstimate(flops=4 * 10**9, bytes_accessed=8 * 2**20, transcendentals=0),
        name="left_factors",
    )(gathered, factor, second, diag_inverse)

    trailing, head, follow = pl.pallas_call(
        functools.partial(update_kernel, pivots, slot_count),
        grid=(grp_total // 2,),
        out_shape=(
            jax.ShapeDtypeStruct((kept, grp_total * kept), jnp.float32),
            jax.ShapeDtypeStruct((rows // block_rows,), jnp.int32),
            jax.ShapeDtypeStruct((slot_count,), jnp.int32),
        ),
        in_specs=[
            smem,
            whole(2, kept, 3 * panel),
            pl.BlockSpec((2, code_rows, panel), lambda i: (i, 0, 0)),
            pl.BlockSpec((1, rows, 2 * rows), lambda i: (0, 0, i)),
            pl.BlockSpec((2, kept, LANE), lambda i: (i, 0, 0)),
        ],
        out_specs=(pl.BlockSpec((kept, 2 * kept), lambda i: (0, i)), smem, smem),
        scratch_shapes=[pltpu.VMEM((2, rows, 3 * panel), jnp.bfloat16)],
        compiler_params=params(),
        cost_estimate=pl.CostEstimate(flops=20 * 10**9, bytes_accessed=40 * 2**20, transcendentals=0),
        name="update",
    )(label, left, gathered, front_entries, middle)

    row_blocks = rows // block_rows
    skipped = 2 * pivots // block_rows
    schur = pl.pallas_call(
        finish_kernel,
        grid=(row_blocks - skipped,),
        out_shape=jax.ShapeDtypeStruct((1, kept, grp_total * kept), jnp.bfloat16),
        in_specs=[
            smem,
            smem,
            smem,
            whole(*rest.shape),
            pl.BlockSpec((block_rows, grp_total * kept), lambda i: (i, 0)),
        ],
        out_specs=pl.BlockSpec((1, block_rows, grp_total * kept), lambda i: (0, i, 0)),
        scratch_shapes=[pltpu.VMEM((grp_total // 2, block_rows, 2 * kept), jnp.float32)],
        compiler_params=params(),
        cost_estimate=pl.CostEstimate(flops=10**7, bytes_accessed=30 * 2**20, transcendentals=0),
        name="finish",
    )(label, head, follow, rest, trailing)
    return schur, factors


def solution(mesh):
    placed = (
        P("front", "grp", None),
        P(("front", "grp"), None, None),
        P(("front", "grp"), None),
        P(("front", "grp")),
        P(("front", "grp")),
        P("front", None, None, None),
    )
    return jax.shard_map(
        local,
        mesh=mesh,
        in_specs=placed,
        out_specs=(P("front", "grp", None), P("front", None, "grp", None)),
        check_vma=False,
    )
```

time: 395 us -> 261 us (0.66)
  Pallas kernels: 203 us -> 86.4 us
  waiting for transfers between devices: 0.01 us -> 59.8 us
  blocking collectives: 145 us -> 85.7 us
  starting transfers between devices: 35.5 us -> 19.2 us
    pallas_call x5, Pallas kernels: 189 us -> 72.7 us  [the longest x1 37 us: local(): pl.pallas_call(functools.partial(update_kernel, pivots, slot_count), grid...]
    all_gather x2 -> x1, blocking collectives: 145 us -> 85.7 us  [local(): gathered = lax.all_gather(code, 'grp', axis=0, tiled=False)]
    all_to_all x1, waiting for transfers between devices: 0.01 us -> 30.4 us  [local(): lax.all_to_all(rest_out, axes, split_axis=0, concat_axis=0, tiled=True)]
    all_to_all x1, waiting for transfers between devices: 0.01 us -> 29.4 us  [local(): lax.all_to_all(first_out, axes, split_axis=0, concat_axis=0, tiled=True)]
    all_to_all x1, starting transfers between devices: 21.3 us -> 7.78 us  [local(): lax.all_to_all(rest_out, axes, split_axis=0, concat_axis=0, tiled=True)]
  transfers between devices with their start and end apart: 2 -> 2, of which waited for: 0 -> 2; matrix products, arithmetic and copies ran while one was open for 1% -> 0% of each run, Pallas kernels for 34% -> 20%
where the time goes in v2:
time: 261 us; the launch traced here: 258 us
  Pallas kernels  86.4 us (33%)
  blocking collectives  85.7 us (33%)
  waiting for transfers between devices  59.8 us (23%)
  starting transfers between devices  19.2 us (7%)
  other arithmetic  3.93 us (2%)
    all_gather x1, blocking collectives, local(): gathered = lax.all_gather(code, 'grp', axis=0, tiled=False)  85.7 us
    pallas_call x1, Pallas kernels, local(): pl.pallas_call(functools.partial(update_kernel, pivots, slot_count), grid...  37 us
    all_to_all x1, waiting for transfers between devices, local(): lax.all_to_all(rest_out, axes, split_axis=0, concat_axis=0, tiled=True)  30.4 us
    all_to_all x1, waiting for transfers between devices, local(): lax.all_to_all(first_out, axes, split_axis=0, concat_axis=0, tiled=True)  29.4 us
    pallas_call x1, Pallas kernels, local(): pl.pallas_call(finish_kernel, grid=(row_blocks - skipped,), out_shape=jax...  16.8 us
    pallas_call x1, Pallas kernels, local(): pl.pallas_call(functools.partial(panel_kernel, pivots, slot_count), grid=...  13.7 us
    all_to_all x1, starting transfers between devices, local(): lax.all_to_all(first_out, axes, split_axis=0, concat_axis=0, tiled=True)  11.4 us
    pallas_call x1, Pallas kernels, local(): pl.pallas_call(functools.partial(left_kernel, pivots), grid=(1,), out_sha...  8.54 us
  transfers between devices with their start and end apart: 2, of which 2 were waited for; matrix products, arithmetic and copies ran while one was open for 0% of the time, Pallas kernels for 20%

profile of v2, /device:TPU:1, one launch (start us, length us, event | category | flops | bytes accessed | tf_op | source)
XLA Modules:
  0.0 258.3 jit_solution(13054097699065649858)
XLA Ops:
  1.3 0.9 convert_reduce_fusion
  2.2 0.7 compare_select_fusion
  2.9 0.0 copy-start.1
  2.9 0.1 select_reduce_fusion
  3.0 0.2 reshape.20
  3.2 0.2 broadcast_in_dim.33
  3.4 0.9 concatenate.3.labels
  4.2 0.0 copy-done.1
  4.2 4.6 %pack_first.1 = bf16[128,80,128]{2,1,0:T(8,128)(2,1)} custom-call(s32[1]{0:T(128)} %copy.8.count, s32[128]{0:T(128)} %copy-done.1, bf16[128,32,512]{2,1,0:T(8,128)(2,1)} %blocks.3, bf16[128,16,128]{2,1,0:T(8,128)(2,1)} %concatenate.3.labels), custom_call_target="tpu_custom_call" | custom-call | tf_op jit(solution)/shard_map/pack_first/pallas_call | solution.py:285
  8.8 11.4 %all-to-all-start = ((bf16[128,80,128]{2,1,0:T(8,128)(2,1)}), bf16[128,80,128]{2,1,0:T(8,128)(2,1)S(1)}, u32[]{:S(2)}, u32[]{:S(2)}) async-start(bf16[128,80,128]{2,1,0:T(8,128)(2,1)} %pack_first.1), calls=%async_computation | async-start | bytes 5242880 | tf_op jit(solution)/shard_map/all_to_all | solution.py:296
  20.3 5.8 %pack_rest.1 = bf16[256,32,384]{2,1,0:T(8,128)(2,1)} custom-call(s32[1]{0:T(128)} %copy.8.count, s32[128]{0:T(128)} %copy-done.1, bf16[128,32,512]{2,1,0:T(8,128)(2,1)} %blocks.3), custom_call_target="tpu_custom_call" | custom-call | bytes 10485760 | tf_op jit(solution)/shard_map/pack_rest/pallas_call | solution.py:297
  26.1 29.4 %all-to-all-done.arrived = bf16[128,80,128]{2,1,0:T(8,128)(2,1)S(1)} async-done(((bf16[128,80,128]{2,1,0:T(8,128)(2,1)}), bf16[128,80,128]{2,1,0:T(8,128)(2,1)S(1)}, u32[]{:S(2)}, u32[]{:S(2)}) %all-to-all-start) | async-done | bytes 2621472 | tf_op jit(solution)/shard_map/all_to_all | solution.py:296
  55.5 0.0 copy-start
  55.5 2.2 add_reduce_fusion
  57.7 0.7 sub.7.label
  58.4 0.0 copy-done
  58.4 13.7 %panels.1 = (f32[512,512]{1,0:T(8,128)}, f32[512,512]{1,0:T(8,128)}, f32[16,448,128]{2,1,0:T(8,128)}, s16[944,512]{1,0:T(8,128)(2,1)}) custom-call(s32[256]{0:T(256)} %sub.7.label, bf16[128,80,128]{2,1,0:T(8,128)(2,1)} %copy-done, bf16[1,512,8192]{2,1,0:T(8,128)(2,1)} %front.3, f32[1,2,512,512]{3,2,1,0:T(8,128)} %inverse.3), custom_call_target="tpu_custom_call" | custom-call | flops 2000000000 | bytes 10485760 | tf_op jit(solution)/shard_map/panels/pallas_call | solution.py:313
  72.1 85.7 %all-gather.2 = s16[15104,512]{1,0:T(8,128)(2,1)} all-gather(s16[944,512]{1,0:T(8,128)(2,1)} %get-tuple-element.16), channel_id=2, replica_groups=mesh['front'=8,'grp'=16] {'grp'}, dimensions={0}, use_global_device_ids=true | all-gather | bytes 16433152 | tf_op jit(solution)/shard_map/all_gather | solution.py:338
  157.8 7.8 %all-to-all-start.1 = ((bf16[256,32,384]{2,1,0:T(8,128)(2,1)}), bf16[256,32,384]{2,1,0:T(8,128)(2,1)}, u32[]{:S(2)}, u32[]{:S(2)}) async-start(bf16[256,32,384]{2,1,0:T(8,128)(2,1)} %pack_rest.1), calls=%async_computation.1 | async-start | bytes 12582912 | tf_op jit(solution)/shard_map/all_to_all | solution.py:341
  165.6 8.5 %left_factors.1 = (f32[1,2,512,512]{3,2,1,0:T(8,128)}, bf16[2,448,1536]{2,1,0:T(8,128)(2,1)}) custom-call(s16[16,944,512]{2,1,0:T(8,128)(2,1)} %bitcast.5, f32[512,512]{1,0:T(8,128)} %get-tuple-element.19.factor, f32[512,512]{1,0:T(8,128)} %get-tuple-element.20.second, f32[1,2,512,512]{3,2,1,0:T(8,128)} %inverse.3), custom_call_target="tpu_custom_call" | custom-call | flops 4000000000 | bytes 8388608 | tf_op jit(solution)/shard_map/left_factors/pallas_call | solution.py:343
  174.2 37.0 %update.1 = (f32[448,7168]{1,0:T(8,128)}, s32[16]{0:T(128)}, s32[256]{0:T(256)}) custom-call(s32[256]{0:T(256)} %sub.7.label, bf16[2,448,1536]{2,1,0:T(8,128)(2,1)} %get-tuple-element.21.left, s16[16,944,512]{2,1,0:T(8,128)(2,1)} %bitcast.6, bf16[1,512,8192]{2,1,0:T(8,128)(2,1)} %front.3, f32[16,448,128]{2,1,0:T(8,128)} %get-tuple-element.22.middle), custom_call_target="tpu_custom_call" | custom-call | flops 20000000000 | bytes 41943040 | tf_op jit(solution)/shard_map/update/pallas_call | solution.py:362
  211.2 30.4 %all-to-all-done.1.rest = bf16[256,32,384]{2,1,0:T(8,128)(2,1)} async-done(((bf16[256,32,384]{2,1,0:T(8,128)(2,1)}), bf16[256,32,384]{2,1,0:T(8,128)(2,1)}, u32[]{:S(2)}, u32[]{:S(2)}) %all-to-all-start.1) | async-done | bytes 6291488 | tf_op jit(solution)/shard_map/all_to_all | solution.py:341
  241.5 16.8 %finish.1 = bf16[1,448,7168]{2,1,0:T(8,128)(2,1)} custom-call(s32[256]{0:T(256)} %sub.7.label, s32[16]{0:T(128)} %get-tuple-element.23.head, s32[256]{0:T(256)} %get-tuple-element.24.follow, bf16[256,32,384]{2,1,0:T(8,128)(2,1)} %all-to-all-done.1.rest, f32[448,7168]{1,0:T(8,128)} %get-tuple-element.26.trailing), custom_call_target="tpu_custom_call" | custom-call | flops 10000000 | bytes 31457280 | tf_op jit(solution)/shard_map/finish/pallas_call | solution.py:386
  (1 shorter events, 0.0 us)
Async XLA Ops:
  2.9 1.4 copy-start.1
  8.8 46.6 %all-to-all-start = ((bf16[128,80,128]{2,1,0:T(8,128)(2,1)}), bf16[128,80,128]{2,1,0:T(8,128)(2,1)S(1)}, u32[]{:S(2)}, u32[]{:S(2)}) async-start(bf16[128,80,128]{2,1,0:T(8,128)(2,1)} %pack_first.1), calls=%async_computation | async-start | bytes 5242880 | tf_op jit(solution)/shard_map/all_to_all | solution.py:296
  55.5 3.0 %copy-start = (bf16[128,80,128]{2,1,0:T(8,128)(2,1)}, bf16[128,80,128]{2,1,0:T(8,128)(2,1)S(1)}, u32[]{:S(2)}) copy-start(bf16[128,80,128]{2,1,0:T(8,128)(2,1)S(1)} %all-to-all-done.arrived) | copy-start | bytes 7864324
  157.8 83.7 %all-to-all-start.1 = ((bf16[256,32,384]{2,1,0:T(8,128)(2,1)}), bf16[256,32,384]{2,1,0:T(8,128)(2,1)}, u32[]{:S(2)}, u32[]{:S(2)}) async-start(bf16[256,32,384]{2,1,0:T(8,128)(2,1)} %pack_rest.1), calls=%async_computation.1 | async-start | bytes 12582912 | tf_op jit(solution)/shard_map/all_to_all | solution.py:341

commit v3 on v2

v3 whole, which is shorter than its diff:
```python
import functools

import jax
import jax.numpy as jnp
from jax import lax
from jax.experimental import pallas as pl
from jax.experimental.pallas import tpu as pltpu
from jax.sharding import PartitionSpec as P

LANE = 128
ROWTILE = 16
LABELROWS = 8
VMEM_LIMIT = 56 * 1024 * 1024
NT = (((1,), (1,)), ((), ()))
NN = (((1,), (0,)), ((), ()))


def params():
    return pltpu.CompilerParams(vmem_limit_bytes=VMEM_LIMIT)


def split(x):
    high = x.astype(jnp.bfloat16)
    return high, (x - high.astype(jnp.float32)).astype(jnp.bfloat16)


def dot_nt(a, b, form=NT):
    return lax.dot_general(a, b, form, preferred_element_type=jnp.float32)


def dot3(a, b, form=NT):
    a_high, a_low = a
    b_high, b_low = b
    return dot_nt(a_high, b_high, form) + (
        dot_nt(a_high, b_low, form) + dot_nt(a_low, b_high, form)
    )


def split_code(code):
    wide = code.astype(jnp.int32)
    high = ((wide + 128) >> 8) << 8
    low = wide - high
    return (
        high.astype(jnp.float32).astype(jnp.bfloat16),
        low.astype(jnp.float32).astype(jnp.bfloat16),
    )


def encode(x):
    rows = x.shape[0]
    largest = jnp.max(jnp.abs(x), axis=1, keepdims=True)
    exponent = jnp.ceil(jnp.log2(jnp.clip(largest, 1e-30, 1e38)))
    scaled = jnp.round(x * jnp.exp2(15.0 - exponent))
    code = jnp.clip(scaled, -32767.0, 32767.0).astype(jnp.int32).astype(jnp.int16)
    along = jnp.transpose(jnp.broadcast_to(exponent, (rows, LANE)))[:ROWTILE]
    return code, along.astype(jnp.int32)


def scale_of(exponent):
    return jnp.exp2(exponent.astype(jnp.int32).astype(jnp.float32) - 15.0)


def pack_first_kernel(count, target, tile, blocks, out, position, load, marks, sem):
    devices = out.shape[0]
    slots, rows, _ = blocks.shape
    copy = pltpu.make_async_copy(blocks.at[:, :, pl.ds(0, LANE)], load, sem)
    copy.start()

    @pl.loop(0, devices, unroll=8)
    def _(t):
        marks[2, t] = 2 * t
        marks[0, t] = 0
        marks[1, t] = 0

    @pl.loop(0, slots, unroll=4)
    def _(i):
        t = target[i]
        at = marks[2, t]
        marks[2, t] = at + 1
        position[i] = at
        marks[at % 2, t] = jnp.where(i < count[0], tile[i] + 1, 0)

    row = lax.broadcasted_iota(jnp.int32, (LABELROWS, LANE), 0)

    @pl.loop(0, devices, unroll=8)
    def _(t):
        both = jnp.where(row == 0, marks[0, t], jnp.where(row == 1, marks[1, t], 0))
        out[t, 2 * rows :, :] = both.astype(jnp.float32).astype(jnp.bfloat16)

    copy.wait()

    @pl.loop(0, slots, unroll=4)
    def _(i):
        at = position[i]
        out[at // 2, pl.ds(pl.multiple_of((at % 2) * rows, rows), rows), :] = load[i]


def pack_rest_kernel(position, blocks, front, middle, rest, entries, sem):
    groups = entries.shape[0]
    width = front.shape[2] // groups

    def copy(c):
        return pltpu.make_async_copy(
            front.at[0, :, pl.ds(c * width, LANE)], entries.at[c], sem.at[c]
        )

    for c in range(groups):
        copy(c).start()

    @pl.loop(0, blocks.shape[0], unroll=2)
    def _(i):
        at = position[i]
        middle[at] = blocks[i, :, LANE : 2 * LANE]
        rest[at] = blocks[i, :, 2 * LANE :]

    for c in range(groups):
        copy(c).wait()


def gather_lanes(acc, rows, start, width, groups):
    per = LANE // width
    lane = lax.broadcasted_iota(jnp.int32, (rows, LANE), 1)
    out = []
    for tile in range(groups // per):
        total = None
        for k in range(per):
            piece = acc[tile * per + k, :rows]
            shift = (k * width - start) % LANE
            if shift:
                piece = pltpu.roll(piece, shift, 1)
            total = piece if total is None else jnp.where(lane >= k * width, piece, total)
        out.append(total)
    return jnp.concatenate(out, axis=1)


def panel_kernel(
    pivots, arrived, entries, inverse, factor, second, code, label, acc, marks, load, later, result, sem
):
    groups, rows, _ = entries.shape
    sources = arrived.shape[0]
    block_rows = rows // groups
    dead = 2 * pivots
    inverse_copy = pltpu.make_async_copy(inverse.at[0, 0], load, sem.at[1])
    inverse_copy.start()

    shape = (sources, LABELROWS, LANE)
    own = lax.broadcasted_iota(jnp.int32, shape, 0) == lax.broadcasted_iota(jnp.int32, shape, 2)
    sent = arrived[:, 2 * block_rows :, :].astype(jnp.float32)
    label[...] = jnp.sum(jnp.where(own, sent, 0.0), axis=0).astype(jnp.int32) - 1
    copy = pltpu.make_async_copy(label, marks, sem.at[0])
    copy.start()
    acc[:, :rows] = entries[...].astype(jnp.float32)
    copy.wait()

    @pl.loop(0, sources, unroll=4)
    def _(source):
        for k in range(2):
            at = marks[k, source]
            at = jnp.where(at < 0, groups * groups, at)
            r, c = at // groups, at % groups
            where = pl.ds(pl.multiple_of(r * block_rows, block_rows), block_rows)
            block = arrived[source, k * block_rows : (k + 1) * block_rows, :]
            acc[c, where, :] += block.astype(jnp.float32)

    later[...] = gather_lanes(acc, rows, pivots, pivots, groups)
    later_copy = pltpu.make_async_copy(later, second, sem.at[2])
    later_copy.start()
    columns = gather_lanes(acc, rows, 0, pivots, groups)
    inverse_copy.wait()
    result[...] = dot3(split(columns), split(load[...]))
    result_copy = pltpu.make_async_copy(result, factor, sem.at[3])
    result_copy.start()
    codes, exponents = encode(result[...])
    later_codes, later_exponents = encode(later[...])
    kept, kept_later = rows - pivots, rows - dead
    code[:kept] = codes[pivots:]
    code[kept : kept + kept_later] = later_codes[dead:]
    row = lax.broadcasted_iota(jnp.int32, exponents.shape, 0)
    code[kept + kept_later :] = jnp.where(row == 0, exponents, later_exponents).astype(jnp.int16)
    later_copy.wait()
    result_copy.wait()


def left_kernel(pivots, gathered, factor, second, inverse, factors, left, pivot_code, exponent, sem):
    groups, code_rows, _ = gathered.shape
    rows, panel = factor.shape
    copies = [
        pltpu.make_async_copy(gathered.at[:, pl.ds(0, pivots), :], pivot_code, sem.at[0]),
        pltpu.make_async_copy(
            gathered.at[:, pl.ds(code_rows - ROWTILE, ROWTILE), :], exponent, sem.at[1]
        ),
    ]
    for copy in copies:
        copy.start()
    factors[0, 0] = factor[...]
    for copy in copies:
        copy.wait()
    lane = lax.broadcasted_iota(jnp.int32, (ROWTILE, panel), 1)
    total = jnp.zeros((ROWTILE, panel), jnp.float32)
    for g in range(groups):
        scale = pltpu.roll(scale_of(exponent[g]), (g * pivots - pivots) % panel, 1)
        total = jnp.where((lane >= g * pivots) & (lane < (g + 1) * pivots), scale, total)
    scale = total[:1]
    pivot_rows = split_code(pivot_code[...].reshape(groups * pivots, panel))
    inverse_parts = split(inverse[0, 0])
    first = factor[pivots:]
    update = dot3(split(first), pivot_rows) * scale
    result = dot3(split(second[pivots:] - update), inverse_parts)
    factors[0, 1, :pivots] = jnp.zeros((pivots, panel), jnp.float32)
    factors[0, 1, pivots:] = result
    own = dot3(split(result[pivots:]), inverse_parts, NN)
    mixed = first[pivots:] - dot3(split(own * scale), pivot_rows, NN)
    for k, part in enumerate((mixed, own)):
        high, low = split(part)
        left[k, :, :panel] = high
        left[k, :, panel : 2 * panel] = high
        left[k, :, 2 * panel :] = low


def list_blocks(label, groups, start, order, column, head, follow):
    sources = label.shape[1]

    @pl.loop(0, groups)
    def _(r):
        start[r] = 0
        head[r] = -1

    def each(act):
        @pl.loop(0, sources)
        def _(source):
            for k in range(2):
                at = label[k, source]

                @pl.when(at >= 0)
                def _():
                    act(2 * source + k, at // groups, at % groups)

    def count(slot, r, c):
        start[r] += 1
        follow[slot] = head[c]
        head[c] = slot

    def place(slot, r, c):
        at = start[r] - 1
        start[r] = at
        order[at] = slot
        column[at] = c

    each(count)
    start[groups] = 0

    @pl.loop(0, groups)
    def _(r):
        start[groups] += start[r]
        start[r] = start[groups]

    each(place)


def update_kernel(
    pivots, label, left, code, front, first, middle, done, open_, start, order, column, head, follow, right, acc
):
    rows, panel = right.shape[1], code.shape[2]
    groups = head.shape[0]
    block_rows = rows // groups
    dead = 2 * pivots
    step = pl.program_id(0)

    @pl.when(step == 0)
    def _():
        right[...] = jnp.zeros(right.shape, jnp.bfloat16)
        list_blocks(label, groups, start, order, column, head, follow)

    for d in range(2):
        acc[d] = front[0, :, d * rows : d * rows + 2 * LANE].astype(jnp.float32)

        def add(slot, d=d):
            k = slot % 2
            r = label[k, slot // 2] // groups
            where = pl.ds(pl.multiple_of(r * block_rows, block_rows), block_rows)
            source = pl.ds(pl.multiple_of(k * block_rows, block_rows), block_rows)
            acc[d, where, :LANE] += first[slot // 2, source, :].astype(jnp.float32)
            acc[d, where, LANE:] += middle[slot].astype(jnp.float32)
            return follow[slot]

        lax.while_loop(lambda slot: slot >= 0, add, head[2 * step + d])

    kept = (rows - pivots, rows - dead)
    starts = (0, kept[0])
    for d in range(2):
        scale = scale_of(code[d, kept[0] + kept[1] :])
        columns = slice(d * rows + 2 * LANE, (d + 1) * rows)
        total = jnp.concatenate(
            [acc[d, dead:], front[0, dead:, columns].astype(jnp.float32)], axis=1
        )
        for k in range(2):
            high, low = split_code(code[d, starts[k] : starts[k] + kept[k]])
            right[k, rows - kept[k] :, :panel] = high
            right[k, rows - kept[k] :, panel : 2 * panel] = low
            right[k, rows - kept[k] :, 2 * panel :] = high
            total = total - dot_nt(left[k], right[k]) * scale[k : k + 1]
        done[d] = total[:, : 2 * LANE].astype(jnp.bfloat16)
        open_[d] = total[:, 2 * LANE :]


def finish_kernel(pivots, start, order, column, rest, done, open_, out, acc):
    groups, step_rows, _ = acc.shape
    block_rows = rest.shape[1]
    dead = 2 * pivots
    kept = 4 * LANE - dead
    per = step_rows // block_rows
    row = pl.program_id(0) * per + groups - pl.num_programs(0) * per
    acc[...] = jnp.zeros(acc.shape, jnp.float32)
    for p in range(per):

        @pl.loop(start[row + p], start[row + p + 1])
        def _(i):
            block = rest[order[i]].astype(jnp.float32)
            acc[column[i], p * block_rows : (p + 1) * block_rows, :] += block

    for m in range(groups // 2):
        sides = []
        for c in (2 * m, 2 * m + 1):
            sides.append(done[c, :, dead:])
            sides.append((open_[c] + acc[c]).astype(jnp.bfloat16))
        pair = jnp.concatenate(sides, axis=1)
        out[0, :, 2 * m * kept : 2 * (m + 1) * kept] = pair


def local(front_entries, child_blocks, dest_device, dest_tile, child_count, diag_inverse):
    grp_total = lax.axis_size("grp")
    device_total = grp_total * lax.axis_size("front")
    axes = ("front", "grp")
    slots, block_rows, block_cols = child_blocks.shape
    _, rows, width = front_entries.shape
    panel = diag_inverse.shape[2]
    pivots = panel // grp_total
    slot_count = 2 * device_total
    rest_cols = block_cols - 2 * LANE
    hbm = pl.BlockSpec(memory_space=pl.ANY)
    smem = pl.BlockSpec(memory_space=pltpu.SMEM)
    whole = lambda *shape: pl.BlockSpec(shape, lambda i: (0,) * len(shape))

    first_rows = 2 * block_rows + LABELROWS
    first_out, position = pl.pallas_call(
        pack_first_kernel,
        grid=(1,),
        out_shape=(
            jax.ShapeDtypeStruct((device_total, first_rows, LANE), jnp.bfloat16),
            jax.ShapeDtypeStruct((slots,), jnp.int32),
        ),
        in_specs=[smem, smem, smem, hbm],
        out_specs=(whole(device_total, first_rows, LANE), smem),
        scratch_shapes=[
            pltpu.VMEM((slots, block_rows, LANE), jnp.bfloat16),
            pltpu.SMEM((3, device_total), jnp.int32),
            pltpu.SemaphoreType.DMA,
        ],
        compiler_params=params(),
        name="pack_first",
    )(child_count, dest_device.reshape(slots), dest_tile, child_blocks)
    first = lax.all_to_all(first_out, axes, split_axis=0, concat_axis=0, tiled=True)
    middle_out, rest_out, entries = pl.pallas_call(
        pack_rest_kernel,
        grid=(1,),
        out_shape=(
            jax.ShapeDtypeStruct((slot_count, block_rows, LANE), jnp.bfloat16),
            jax.ShapeDtypeStruct((slot_count, block_rows, rest_cols), jnp.bfloat16),
            jax.ShapeDtypeStruct((grp_total, rows, LANE), jnp.bfloat16),
        ),
        in_specs=[smem, whole(*child_blocks.shape), hbm],
        out_specs=(
            whole(slot_count, block_rows, LANE),
            whole(slot_count, block_rows, rest_cols),
            whole(grp_total, rows, LANE),
        ),
        scratch_shapes=[pltpu.SemaphoreType.DMA((grp_total,))],
        compiler_params=params(),
        cost_estimate=pl.CostEstimate(flops=0, bytes_accessed=16 * 2**20, transcendentals=0),
        name="pack_rest",
    )(position, child_blocks, front_entries)
    middle = lax.all_to_all(middle_out, axes, split_axis=0, concat_axis=0, tiled=True)
    first, rest_out, entries = lax.optimization_barrier((first, rest_out, entries))

    kept = rows - 2 * pivots
    code_rows = (rows - pivots) + kept + ROWTILE
    inverse_spec = lambda k: pl.BlockSpec((1, 1, panel, panel), lambda i: (0, k, 0, 0))
    factor, second, code, label = pl.pallas_call(
        functools.partial(panel_kernel, pivots),
        grid=(1,),
        out_shape=(
            jax.ShapeDtypeStruct((rows, panel), jnp.float32),
            jax.ShapeDtypeStruct((rows, panel), jnp.float32),
            jax.ShapeDtypeStruct((code_rows, panel), jnp.int16),
            jax.ShapeDtypeStruct((LABELROWS, LANE), jnp.int32),
        ),
        in_specs=[whole(*first.shape), whole(*entries.shape), hbm],
        out_specs=(hbm, hbm, whole(code_rows, panel), whole(LABELROWS, LANE)),
        scratch_shapes=[
            pltpu.VMEM((grp_total, rows + block_rows, LANE), jnp.float32),
            pltpu.SMEM((LABELROWS, LANE), jnp.int32),
            pltpu.VMEM((panel, panel), jnp.float32),
            pltpu.VMEM((rows, panel), jnp.float32),
            pltpu.VMEM((rows, panel), jnp.float32),
            pltpu.SemaphoreType.DMA((4,)),
        ],
        compiler_params=params(),
        cost_estimate=pl.CostEstimate(flops=2 * 10**9, bytes_accessed=10 * 2**20, transcendentals=0),
        name="panels",
    )(first, entries, diag_inverse)
    gathered = lax.all_gather(code, "grp", axis=0, tiled=False)

    gathered, rest_out = lax.optimization_barrier((gathered, rest_out))
    rest = lax.all_to_all(rest_out, axes, split_axis=0, concat_axis=0, tiled=True)

    factors, left = pl.pallas_call(
        functools.partial(left_kernel, pivots),
        grid=(1,),
        out_shape=(
            jax.ShapeDtypeStruct((1, 2, rows, panel), jnp.float32),
            jax.ShapeDtypeStruct((2, kept, 3 * panel), jnp.bfloat16),
        ),
        in_specs=[hbm, whole(rows, panel), whole(rows, panel), inverse_spec(1)],
        out_specs=(whole(1, 2, rows, panel), whole(2, kept, 3 * panel)),
        scratch_shapes=[
            pltpu.VMEM((grp_total, pivots, panel), jnp.int16),
            pltpu.VMEM((grp_total, ROWTILE, panel), jnp.int16),
            pltpu.SemaphoreType.DMA((2,)),
        ],
        compiler_params=params(),
        cost_estimate=pl.CostEstimate(flops=4 * 10**9, bytes_accessed=8 * 2**20, transcendentals=0),
        name="left_factors",
    )(gathered, factor, second, diag_inverse)

    row_blocks = rows // block_rows
    lists = (row_blocks + 1, slot_count, slot_count)
    done, open_, *lists = pl.pallas_call(
        functools.partial(update_kernel, pivots),
        grid=(grp_total // 2,),
        out_shape=(
            jax.ShapeDtypeStruct((grp_total, kept, 2 * LANE), jnp.bfloat16),
            jax.ShapeDtypeStruct((grp_total, kept, rest_cols), jnp.float32),
            *(jax.ShapeDtypeStruct((length,), jnp.int32) for length in lists),
        ),
        in_specs=[
            smem,
            whole(2, kept, 3 * panel),
            pl.BlockSpec((2, code_rows, panel), lambda i: (i, 0, 0)),
            pl.BlockSpec((1, rows, 2 * rows), lambda i: (0, 0, i)),
            whole(*first.shape),
            whole(*middle.shape),
        ],
        out_specs=(
            pl.BlockSpec((2, kept, 2 * LANE), lambda i: (i, 0, 0)),
            pl.BlockSpec((2, kept, rest_cols), lambda i: (i, 0, 0)),
            smem,
            smem,
            smem,
        ),
        scratch_shapes=[
            pltpu.SMEM((row_blocks,), jnp.int32),
            pltpu.SMEM((slot_count,), jnp.int32),
            pltpu.VMEM((2, rows, 3 * panel), jnp.bfloat16),
            pltpu.VMEM((2, rows, 2 * LANE), jnp.float32),
        ],
        compiler_params=params(),
        cost_estimate=pl.CostEstimate(flops=20 * 10**9, bytes_accessed=40 * 2**20, transcendentals=0),
        name="update",
    )(label, left, gathered, front_entries, first, middle)

    step_rows = kept // 2
    schur = pl.pallas_call(
        functools.partial(finish_kernel, pivots),
        grid=(kept // step_rows,),
        out_shape=jax.ShapeDtypeStruct((1, kept, grp_total * kept), jnp.bfloat16),
        in_specs=[
            smem,
            smem,
            smem,
            whole(*rest.shape),
            pl.BlockSpec((grp_total, step_rows, 2 * LANE), lambda i: (0, i, 0)),
            pl.BlockSpec((grp_total, step_rows, rest_cols), lambda i: (0, i, 0)),
        ],
        out_specs=pl.BlockSpec((1, step_rows, grp_total * kept), lambda i: (0, i, 0)),
        scratch_shapes=[pltpu.VMEM((grp_total, step_rows, rest_cols), jnp.float32)],
        compiler_params=params(),
        cost_estimate=pl.CostEstimate(flops=10**7, bytes_accessed=30 * 2**20, transcendentals=0),
        name="finish",
    )(*lists, rest, done, open_)
    return schur, factors


def solution(mesh):
    placed = (
        P("front", "grp", None),
        P(("front", "grp"), None, None),
        P(("front", "grp"), None),
        P(("front", "grp")),
        P(("front", "grp")),
        P("front", None, None, None),
    )
    return jax.shard_map(
        local,
        mesh=mesh,
        in_specs=placed,
        out_specs=(P("front", "grp", None), P("front", None, "grp", None)),
        check_vma=False,
    )
```

time: 261 us -> 235 us (0.900)
  waiting for transfers between devices: 59.8 us -> 25.9 us
  blocking collectives: 85.7 us -> 98.4 us
  starting transfers between devices: 19.2 us -> 23.9 us
  other arithmetic: 3.93 us -> 0 us
  Pallas kernels: 86.4 us -> 82.6 us
    all_to_all x1, waiting for transfers between devices: 30.4 us -> 0.79 us  [local(): lax.all_to_all(rest_out, axes, split_axis=0, concat_axis=0, tiled=True)]
    all_gather x1, blocking collectives: 85.7 us -> 98.4 us  [local(): gathered = lax.all_gather(code, 'grp', axis=0, tiled=False)]
    all_to_all x0 -> x1, starting transfers between devices: none -> 5.65 us  [local(): lax.all_to_all(middle_out, axes, split_axis=0, concat_axis=0, tiled=True)]
    all_to_all x1, waiting for transfers between devices: 29.4 us -> 25.1 us  [local(): lax.all_to_all(first_out, axes, split_axis=0, concat_axis=0, tiled=True)]
    pallas_call x5, Pallas kernels: 77.8 us -> 74 us  [the longest x1 42.7 us: local(): pl.pallas_call(functools.partial(update_kernel, pivots), grid=(grp_total...]
  transfers between devices with their start and end apart: 2 -> 3, of which waited for: 2 -> 2; matrix products, arithmetic and copies ran while one was open for 0% -> 0% of each run, Pallas kernels for 20% -> 30%
where the time goes in v3:
time: 235 us; the launch traced here: 232 us
  blocking collectives  98.4 us (42%)
  Pallas kernels  82.6 us (35%)
  waiting for transfers between devices  25.9 us (11%)
  starting transfers between devices  23.9 us (10%)
    all_gather x1, blocking collectives, local(): gathered = lax.all_gather(code, 'grp', axis=0, tiled=False)  98.4 us
    pallas_call x1, Pallas kernels, local(): pl.pallas_call(functools.partial(update_kernel, pivots), grid=(grp_total...  42.7 us
    all_to_all x1, waiting for transfers between devices, local(): lax.all_to_all(first_out, axes, split_axis=0, concat_axis=0, tiled=True)  25.1 us
    all_to_all x1, starting transfers between devices, local(): lax.all_to_all(first_out, axes, split_axis=0, concat_axis=0, tiled=True)  11.5 us
    pallas_call x1, Pallas kernels, local(): pl.pallas_call(functools.partial(panel_kernel, pivots), grid=(1,), out_sh...  9.93 us
    pallas_call x1, Pallas kernels, local(): pl.pallas_call(functools.partial(left_kernel, pivots), grid=(1,), out_sha...  8.55 us
    pallas_call x1, Pallas kernels, local(): pl.pallas_call(functools.partial(finish_kernel, pivots), grid=(kept // st...  8.4 us
    pallas_call x1, Pallas kernels, local(): pl.pallas_call(pack_rest_kernel, grid=(1,), out_shape=(jax.ShapeDtypeStru...  7.3 us
  transfers between devices with their start and end apart: 3, of which 2 were waited for; matrix products, arithmetic and copies ran while one was open for 0% of the time, Pallas kernels for 30%

profile of v3, /device:TPU:1, one launch (start us, length us, event | category | flops | bytes accessed | tf_op | source)
XLA Modules:
  0.0 232.2 jit_solution(17271720042769950665)
XLA Ops:
  1.3 5.7 %pack_first.1 = (bf16[128,72,128]{2,1,0:T(8,128)(2,1)}, s32[128]{0:T(128)}) custom-call(s32[1]{0:T(128)S(6)} %copy.8.count, s32[128]{0:T(128)} %bitcast.4, s32[128]{0:T(128)} %tile.1, bf16[128,32,512]{2,1,0:T(8,128)(2,1)} %blocks.3), custom_call_target="tpu_custom_call" | custom-call | tf_op jit(solution)/shard_map/pack_first/pallas_call | solution.py:345
  6.9 11.5 %all-to-all-start = ((bf16[128,72,128]{2,1,0:T(8,128)(2,1)}), bf16[128,72,128]{2,1,0:T(8,128)(2,1)S(1)}, u32[]{:S(2)}, u32[]{:S(2)}) async-start(bf16[128,72,128]{2,1,0:T(8,128)(2,1)} %get-tuple-element.23), calls=%async_computation | async-start | bytes 4718592 | tf_op jit(solution)/shard_map/all_to_all | solution.py:362
  18.4 7.3 %pack_rest.1 = (bf16[256,32,128]{2,1,0:T(8,128)(2,1)}, bf16[256,32,256]{2,1,0:T(8,128)(2,1)}, bf16[16,512,128]{2,1,0:T(8,128)(2,1)}) custom-call(s32[128]{0:T(128)} %get-tuple-element.24.position, bf16[128,32,512]{2,1,0:T(8,128)(2,1)} %blocks.3, bf16[1,512,8192]{2,1,0:T(8,128)(2,1)} %front.3), custom_call_target="tpu_custom_call" | custom-call | bytes 16777216 | tf_op jit(solution)/shard_map/pack_rest/pallas_call | solution.py:363
  25.8 25.1 %all-to-all-done.arrived.first = bf16[128,72,128]{2,1,0:T(8,128)(2,1)S(1)} async-done(((bf16[128,72,128]{2,1,0:T(8,128)(2,1)}), bf16[128,72,128]{2,1,0:T(8,128)(2,1)S(1)}, u32[]{:S(2)}, u32[]{:S(2)}) %all-to-all-start) | async-done | bytes 2359328 | tf_op jit(solution)/shard_map/all_to_all | solution.py:362
  50.9 0.0 copy-start
  50.9 5.7 %all-to-all-start.1 = ((bf16[256,32,128]{2,1,0:T(8,128)(2,1)}), bf16[256,32,128]{2,1,0:T(8,128)(2,1)}, u32[]{:S(2)}, u32[]{:S(2)}) async-start(bf16[256,32,128]{2,1,0:T(8,128)(2,1)} %get-tuple-element.36), calls=%async_computation.1 | async-start | bytes 4194304 | tf_op jit(solution)/shard_map/all_to_all | solution.py:382
  56.6 0.0 copy-done
  56.6 9.9 %panels.1 = (f32[512,512]{1,0:T(8,128)}, f32[512,512]{1,0:T(8,128)}, s16[944,512]{1,0:T(8,128)(2,1)}, s32[8,128]{1,0:T(8,128)}) custom-call(bf16[128,72,128]{2,1,0:T(8,128)(2,1)} %copy-done, bf16[16,512,128]{2,1,0:T(8,128)(2,1)} %get-tuple-element.28.entries, f32[1,2,512,512]{3,2,1,0:T(8,128)} %inverse.3), custom_call_target="tpu_custom_call" | custom-call | flops 2000000000 | bytes 10485760 | tf_op jit(solution)/shard_map/panels/pallas_call | solution.py:388
  66.5 98.4 %all-gather.2 = s16[15104,512]{1,0:T(8,128)(2,1)} all-gather(s16[944,512]{1,0:T(8,128)(2,1)} %get-tuple-element.30), channel_id=2, replica_groups=mesh['front'=8,'grp'=16] {'grp'}, dimensions={0}, use_global_device_ids=true | all-gather | bytes 16433152 | tf_op jit(solution)/shard_map/all_gather | solution.py:411
  164.9 0.0 all-to-all-done.1.middle
  164.9 6.7 %all-to-all-start.2 = ((bf16[256,32,256]{2,1,0:T(8,128)(2,1)}), bf16[256,32,256]{2,1,0:T(8,128)(2,1)}, u32[]{:S(2)}, u32[]{:S(2)}) async-start(bf16[256,32,256]{2,1,0:T(8,128)(2,1)} %get-tuple-element.40), calls=%async_computation.2 | async-start | bytes 8388608 | tf_op jit(solution)/shard_map/all_to_all | solution.py:414
  171.7 8.5 %left_factors.1 = (f32[1,2,512,512]{3,2,1,0:T(8,128)}, bf16[2,448,1536]{2,1,0:T(8,128)(2,1)}) custom-call(s16[16,944,512]{2,1,0:T(8,128)(2,1)} %bitcast.2, f32[512,512]{1,0:T(8,128)} %get-tuple-element.33.factor, f32[512,512]{1,0:T(8,128)} %get-tuple-element.34.second, f32[1,2,512,512]{3,2,1,0:T(8,128)} %inverse.3), custom_call_target="tpu_custom_call" | custom-call | flops 4000000000 | bytes 8388608 | tf_op jit(solution)/shard_map/left_factors/pallas_call | solution.py:416
  180.2 42.7 %update.1 = (bf16[16,448,256]{2,1,0:T(8,128)(2,1)}, f32[16,448,256]{2,1,0:T(8,128)}, s32[17]{0:T(128)}, s32[256]{0:T(256)}, s32[256]{0:T(256)}) custom-call(s32[8,128]{1,0:T(8,128)} %get-tuple-element.29.label, bf16[2,448,1536]{2,1,0:T(8,128)(2,1)} %get-tuple-element.35.left, s16[16,944,512]{2,1,0:T(8,128)(2,1)} %bitcast.3, bf16[1,512,8192]{2,1,0:T(8,128)(2,1)} %front.3, ...), custom_call_target="tpu_custom_call" | custom-call | flops 20000000000 | bytes 41943040 | tf_op jit(solution)/shard_map/update/pallas_call | solution.py:437
  223.0 0.8 all-to-all-done.2.rest
  223.7 8.4 %finish.1 = bf16[1,448,7168]{2,1,0:T(8,128)(2,1)} custom-call(s32[17]{0:T(128)} %get-tuple-element.37.start, s32[256]{0:T(256)} %get-tuple-element.38.order, s32[256]{0:T(256)} %get-tuple-element.39.column, bf16[256,32,256]{2,1,0:T(8,128)(2,1)} %all-to-all-done.2.rest, bf16[16,448,256]{2,1,0:T(8,128)(2,1)} %get-tuple-element.41.done, ...), custom_call_target="tpu_custom_call" | custom-call | flops 10000000 | bytes 31457280 | tf_op jit(solution)/shard_map/finish/pallas_call | solution.py:472
Async XLA Ops:
  6.9 44.0 %all-to-all-start = ((bf16[128,72,128]{2,1,0:T(8,128)(2,1)}), bf16[128,72,128]{2,1,0:T(8,128)(2,1)S(1)}, u32[]{:S(2)}, u32[]{:S(2)}) async-start(bf16[128,72,128]{2,1,0:T(8,128)(2,1)} %get-tuple-element.23), calls=%async_computation | async-start | bytes 4718592 | tf_op jit(solution)/shard_map/all_to_all | solution.py:362
  50.9 5.7 %copy-start = (bf16[128,72,128]{2,1,0:T(8,128)(2,1)}, bf16[128,72,128]{2,1,0:T(8,128)(2,1)S(1)}, u32[]{:S(2)}) copy-start(bf16[128,72,128]{2,1,0:T(8,128)(2,1)S(1)} %all-to-all-done.arrived.first) | copy-start | bytes 7077892
  50.9 114.0 %all-to-all-start.1 = ((bf16[256,32,128]{2,1,0:T(8,128)(2,1)}), bf16[256,32,128]{2,1,0:T(8,128)(2,1)}, u32[]{:S(2)}, u32[]{:S(2)}) async-start(bf16[256,32,128]{2,1,0:T(8,128)(2,1)} %get-tuple-element.36), calls=%async_computation.1 | async-start | bytes 4194304 | tf_op jit(solution)/shard_map/all_to_all | solution.py:382
  164.9 58.8 %all-to-all-start.2 = ((bf16[256,32,256]{2,1,0:T(8,128)(2,1)}), bf16[256,32,256]{2,1,0:T(8,128)(2,1)}, u32[]{:S(2)}, u32[]{:S(2)}) async-start(bf16[256,32,256]{2,1,0:T(8,128)(2,1)} %get-tuple-element.40), calls=%async_computation.2 | async-start | bytes 8388608 | tf_op jit(solution)/shard_map/all_to_all | solution.py:414

commit v4 on v3

--- a/solution.py
+++ b/solution.py
@@ -10,13 +10,13 @@
 LANE = 128
 ROWTILE = 16
 LABELROWS = 8
-VMEM_LIMIT = 56 * 1024 * 1024
+MIB = 1024 * 1024
 NT = (((1,), (1,)), ((), ()))
 NN = (((1,), (0,)), ((), ()))
 
 
-def params():
-    return pltpu.CompilerParams(vmem_limit_bytes=VMEM_LIMIT)
+def params(mebibytes=56):
+    return pltpu.CompilerParams(vmem_limit_bytes=mebibytes * MIB)
 
 
 def split(x):
@@ -37,13 +37,7 @@
 
 
 def split_code(code):
-    wide = code.astype(jnp.int32)
-    high = ((wide + 128) >> 8) << 8
-    low = wide - high
-    return (
-        high.astype(jnp.float32).astype(jnp.bfloat16),
-        low.astype(jnp.float32).astype(jnp.bfloat16),
-    )
+    return split(code.astype(jnp.int32).astype(jnp.float32))
 
 
 def encode(x):
@@ -133,8 +127,49 @@
     return jnp.concatenate(out, axis=1)
 
 
+def list_blocks(label, groups, start, order, column, head, follow):
+    sources = label.shape[1]
+
+    @pl.loop(0, groups)
+    def _(r):
+        start[r] = 0
+        head[r] = -1
+
+    def each(act):
+        @pl.loop(0, sources)
+        def _(source):
+            for k in range(2):
+                at = label[k, source]
+
+                @pl.when(at >= 0)
+                def _():
+                    act(2 * source + k, at // groups, at % groups)
+
+    def count(slot, r, c):
+        start[r] += 1
+        follow[slot] = head[c]
+        head[c] = slot
+
+    def place(slot, r, c):
+        at = start[r] - 1
+        start[r] = at
+        order[at] = slot
+        column[at] = c
+
+    each(count)
+    start[groups] = 0
+
+    @pl.loop(0, groups)
+    def _(r):
+        start[groups] += start[r]
+        start[r] = start[groups]
+
+    each(place)
+
+
 def panel_kernel(
-    pivots, arrived, entries, inverse, factor, second, code, label, acc, marks, load, later, result, sem
+    pivots, arrived, entries, inverse, factor, second, code, label, start, order, column, head, follow,
+    acc, marks, load, later, result, sem,
 ):
     groups, rows, _ = entries.shape
     sources = arrived.shape[0]
@@ -177,6 +212,7 @@
     code[kept : kept + kept_later] = later_codes[dead:]
     row = lax.broadcasted_iota(jnp.int32, exponents.shape, 0)
     code[kept + kept_later :] = jnp.where(row == 0, exponents, later_exponents).astype(jnp.int16)
+    list_blocks(marks, groups, start, order, column, head, follow)
     later_copy.wait()
     result_copy.wait()
 
@@ -217,48 +253,8 @@
         left[k, :, 2 * panel :] = low
 
 
-def list_blocks(label, groups, start, order, column, head, follow):
-    sources = label.shape[1]
-
-    @pl.loop(0, groups)
-    def _(r):
-        start[r] = 0
-        head[r] = -1
-
-    def each(act):
-        @pl.loop(0, sources)
-        def _(source):
-            for k in range(2):
-                at = label[k, source]
-
-                @pl.when(at >= 0)
-                def _():
-                    act(2 * source + k, at // groups, at % groups)
-
-    def count(slot, r, c):
-        start[r] += 1
-        follow[slot] = head[c]
-        head[c] = slot
-
-    def place(slot, r, c):
-        at = start[r] - 1
-        start[r] = at
-        order[at] = slot
-        column[at] = c
-
-    each(count)
-    start[groups] = 0
-
-    @pl.loop(0, groups)
-    def _(r):
-        start[groups] += start[r]
-        start[r] = start[groups]
-
-    each(place)
-
-
 def update_kernel(
-    pivots, label, left, code, front, first, middle, done, open_, start, order, column, head, follow, right, acc
+    pivots, label, head, follow, left, code, front, first, middle, done, open_, right, acc
 ):
     rows, panel = right.shape[1], code.shape[2]
     groups = head.shape[0]
@@ -269,7 +265,6 @@
     @pl.when(step == 0)
     def _():
         right[...] = jnp.zeros(right.shape, jnp.bfloat16)
-        list_blocks(label, groups, start, order, column, head, follow)
 
     for d in range(2):
         acc[d] = front[0, :, d * rows : d * rows + 2 * LANE].astype(jnp.float32)
@@ -299,8 +294,8 @@
             right[k, rows - kept[k] :, panel : 2 * panel] = low
             right[k, rows - kept[k] :, 2 * panel :] = high
             total = total - dot_nt(left[k], right[k]) * scale[k : k + 1]
-        done[d] = total[:, : 2 * LANE].astype(jnp.bfloat16)
-        open_[d] = total[:, 2 * LANE :]
+        done[2 * step + d] = total[:, : 2 * LANE].astype(jnp.bfloat16)
+        open_[2 * step + d] = total[:, 2 * LANE :]
 
 
 def finish_kernel(pivots, start, order, column, rest, done, open_, out, acc):
@@ -310,6 +305,7 @@
     kept = 4 * LANE - dead
     per = step_rows // block_rows
     row = pl.program_id(0) * per + groups - pl.num_programs(0) * per
+    here = pl.ds(pl.multiple_of(pl.program_id(0) * step_rows, ROWTILE), step_rows)
     acc[...] = jnp.zeros(acc.shape, jnp.float32)
     for p in range(per):
 
@@ -321,8 +317,8 @@
     for m in range(groups // 2):
         sides = []
         for c in (2 * m, 2 * m + 1):
-            sides.append(done[c, :, dead:])
-            sides.append((open_[c] + acc[c]).astype(jnp.bfloat16))
+            sides.append(done[c, here, dead:])
+            sides.append((open_[c, here] + acc[c]).astype(jnp.bfloat16))
         pair = jnp.concatenate(sides, axis=1)
         out[0, :, 2 * m * kept : 2 * (m + 1) * kept] = pair
 
@@ -338,6 +334,7 @@
     slot_count = 2 * device_total
     rest_cols = block_cols - 2 * LANE
     hbm = pl.BlockSpec(memory_space=pl.ANY)
+    vmem = pl.BlockSpec(memory_space=pltpu.VMEM)
     smem = pl.BlockSpec(memory_space=pltpu.SMEM)
     whole = lambda *shape: pl.BlockSpec(shape, lambda i: (0,) * len(shape))
 
@@ -346,11 +343,11 @@
         pack_first_kernel,
         grid=(1,),
         out_shape=(
-            jax.ShapeDtypeStruct((device_total, first_rows, LANE), jnp.bfloat16),
+            pltpu.VMEM((device_total, first_rows, LANE), jnp.bfloat16),
             jax.ShapeDtypeStruct((slots,), jnp.int32),
         ),
         in_specs=[smem, smem, smem, hbm],
-        out_specs=(whole(device_total, first_rows, LANE), smem),
+        out_specs=(vmem, smem),
         scratch_shapes=[
             pltpu.VMEM((slots, block_rows, LANE), jnp.bfloat16),
             pltpu.SMEM((3, device_total), jnp.int32),
@@ -385,7 +382,9 @@
     kept = rows - 2 * pivots
     code_rows = (rows - pivots) + kept + ROWTILE
     inverse_spec = lambda k: pl.BlockSpec((1, 1, panel, panel), lambda i: (0, k, 0, 0))
-    factor, second, code, label = pl.pallas_call(
+    row_blocks = rows // block_rows
+    lengths = (row_blocks + 1, slot_count, slot_count, row_blocks, slot_count)
+    factor, second, code, label, start, order, column, head, follow = pl.pallas_call(
         functools.partial(panel_kernel, pivots),
         grid=(1,),
         out_shape=(
@@ -393,9 +392,10 @@
             jax.ShapeDtypeStruct((rows, panel), jnp.float32),
             jax.ShapeDtypeStruct((code_rows, panel), jnp.int16),
             jax.ShapeDtypeStruct((LABELROWS, LANE), jnp.int32),
+            *(jax.ShapeDtypeStruct((length,), jnp.int32) for length in lengths),
         ),
         in_specs=[whole(*first.shape), whole(*entries.shape), hbm],
-        out_specs=(hbm, hbm, whole(code_rows, panel), whole(LABELROWS, LANE)),
+        out_specs=(hbm, hbm, whole(code_rows, panel), whole(LABELROWS, LANE)) + (smem,) * 5,
         scratch_shapes=[
             pltpu.VMEM((grp_total, rows + block_rows, LANE), jnp.float32),
             pltpu.SMEM((LABELROWS, LANE), jnp.int32),
@@ -432,17 +432,16 @@
         name="left_factors",
     )(gathered, factor, second, diag_inverse)
 
-    row_blocks = rows // block_rows
-    lists = (row_blocks + 1, slot_count, slot_count)
-    done, open_, *lists = pl.pallas_call(
+    done, open_ = pl.pallas_call(
         functools.partial(update_kernel, pivots),
         grid=(grp_total // 2,),
         out_shape=(
-            jax.ShapeDtypeStruct((grp_total, kept, 2 * LANE), jnp.bfloat16),
-            jax.ShapeDtypeStruct((grp_total, kept, rest_cols), jnp.float32),
-            *(jax.ShapeDtypeStruct((length,), jnp.int32) for length in lists),
+            pltpu.VMEM((grp_total, kept, 2 * LANE), jnp.bfloat16),
+            pltpu.VMEM((grp_total, kept, rest_cols), jnp.float32),
         ),
         in_specs=[
+            smem,
+            smem,
             smem,
             whole(2, kept, 3 * panel),
             pl.BlockSpec((2, code_rows, panel), lambda i: (i, 0, 0)),
@@ -450,25 +449,18 @@
             whole(*first.shape),
             whole(*middle.shape),
         ],
-        out_specs=(
-            pl.BlockSpec((2, kept, 2 * LANE), lambda i: (i, 0, 0)),
-            pl.BlockSpec((2, kept, rest_cols), lambda i: (i, 0, 0)),
-            smem,
-            smem,
-            smem,
-        ),
+        out_specs=(vmem, vmem),
         scratch_shapes=[
-            pltpu.SMEM((row_blocks,), jnp.int32),
-            pltpu.SMEM((slot_count,), jnp.int32),
             pltpu.VMEM((2, rows, 3 * panel), jnp.bfloat16),
             pltpu.VMEM((2, rows, 2 * LANE), jnp.float32),
         ],
-        compiler_params=params(),
+        compiler_params=params(52),
         cost_estimate=pl.CostEstimate(flops=20 * 10**9, bytes_accessed=40 * 2**20, transcendentals=0),
         name="update",
-    )(label, left, gathered, front_entries, first, middle)
+    )(label, head, follow, left, gathered, front_entries, first, middle)
 
     step_rows = kept // 2
+    done, open_ = (pltpu.with_memory_space_constraint(x, pltpu.VMEM) for x in (done, open_))
     schur = pl.pallas_call(
         functools.partial(finish_kernel, pivots),
         grid=(kept // step_rows,),
@@ -478,15 +470,15 @@
             smem,
             smem,
             whole(*rest.shape),
-            pl.BlockSpec((grp_total, step_rows, 2 * LANE), lambda i: (0, i, 0)),
-            pl.BlockSpec((grp_total, step_rows, rest_cols), lambda i: (0, i, 0)),
+            vmem,
+            vmem,
         ],
         out_specs=pl.BlockSpec((1, step_rows, grp_total * kept), lambda i: (0, i, 0)),
         scratch_shapes=[pltpu.VMEM((grp_total, step_rows, rest_cols), jnp.float32)],
-        compiler_params=params(),
+        compiler_params=params(52),
         cost_estimate=pl.CostEstimate(flops=10**7, bytes_accessed=30 * 2**20, transcendentals=0),
         name="finish",
-    )(*lists, rest, done, open_)
+    )(start, order, column, rest, done, open_)
     return schur, factors
 
 

time: 235 us -> 237 us (level)
  local copies, waits for them, and re-layouts: 0.01 us -> 9.96 us
  Pallas kernels: 82.6 us -> 77.1 us
  blocking collectives: 98.4 us -> 93.1 us
  waiting for transfers between devices: 25.9 us -> 31 us
    unnamed x2 -> x10, local copies, waits for them, and re-layouts: 0.01 us -> 9.96 us
    pallas_call x1, Pallas kernels: 42.7 us -> 32.8 us  [local(): pl.pallas_call(functools.partial(update_kernel, pivots), grid=(grp_total...]
    pallas_call x1, Pallas kernels: 9.93 us -> 16 us  [local(): pl.pallas_call(functools.partial(panel_kernel, pivots), grid=(1,), out_sh...]
    all_gather x1, blocking collectives: 98.4 us -> 93.1 us  [local(): gathered = lax.all_gather(code, 'grp', axis=0, tiled=False)]
    all_to_all x1, waiting for transfers between devices: 0.79 us -> 5.88 us  [local(): lax.all_to_all(rest_out, axes, split_axis=0, concat_axis=0, tiled=True)]
  transfers between devices with their start and end apart: 3 -> 3, of which waited for: 2 -> 2; matrix products, arithmetic and copies ran while one was open for 0% -> 0% of each run, Pallas kernels for 30% -> 27%
where the time goes in v4:
time: 237 us; the launch traced here: 236 us
  blocking collectives  93.1 us (39%)
  Pallas kernels  77.1 us (33%)
  waiting for transfers between devices  31 us (13%)
  starting transfers between devices  23.3 us (10%)
  local copies, waits for them, and re-layouts  9.96 us (4%)
    all_gather x1, blocking collectives, local(): gathered = lax.all_gather(code, 'grp', axis=0, tiled=False)  93.1 us
    pallas_call x1, Pallas kernels, local(): pl.pallas_call(functools.partial(update_kernel, pivots), grid=(grp_total...  32.8 us
    all_to_all x1, waiting for transfers between devices, local(): lax.all_to_all(first_out, axes, split_axis=0, concat_axis=0, tiled=True)  25.1 us
    pallas_call x1, Pallas kernels, local(): pl.pallas_call(functools.partial(panel_kernel, pivots), grid=(1,), out_sh...  16 us
    all_to_all x1, starting transfers between devices, local(): lax.all_to_all(first_out, axes, split_axis=0, concat_axis=0, tiled=True)  11.5 us
    unnamed x10, local copies, waits for them, and re-layouts  9.96 us
    pallas_call x1, Pallas kernels, local(): pl.pallas_call(functools.partial(left_kernel, pivots), grid=(1,), out_sha...  8.56 us
    pallas_call x1, Pallas kernels, local(): pl.pallas_call(pack_rest_kernel, grid=(1,), out_shape=(jax.ShapeDtypeStru...  7.32 us
  transfers between devices with their start and end apart: 3, of which 2 were waited for; matrix products, arithmetic and copies ran while one was open for 0% of the time, Pallas kernels for 27%

profile of v4, /device:TPU:1, one launch (start us, length us, event | category | flops | bytes accessed | tf_op | source)
XLA Modules:
  0.0 235.9 jit_solution(7326989747338816239)
XLA Ops:
  1.3 5.7 %pack_first.1 = (bf16[128,72,128]{2,1,0:T(8,128)(2,1)}, s32[128]{0:T(128)}) custom-call(s32[1]{0:T(128)S(6)} %copy.8.count, s32[128]{0:T(128)} %bitcast.4, s32[128]{0:T(128)} %tile.1, bf16[128,32,512]{2,1,0:T(8,128)(2,1)} %blocks.3), custom_call_target="tpu_custom_call" | custom-call | tf_op jit(solution)/shard_map/pack_first/pallas_call | solution.py:342
  7.0 11.5 %all-to-all-start = ((bf16[128,72,128]{2,1,0:T(8,128)(2,1)}), bf16[128,72,128]{2,1,0:T(8,128)(2,1)S(1)}, u32[]{:S(2)}, u32[]{:S(2)}) async-start(bf16[128,72,128]{2,1,0:T(8,128)(2,1)} %get-tuple-element.25), calls=%async_computation | async-start | bytes 4718592 | tf_op jit(solution)/shard_map/all_to_all | solution.py:359
  18.5 7.3 %pack_rest.1 = (bf16[256,32,128]{2,1,0:T(8,128)(2,1)}, bf16[256,32,256]{2,1,0:T(8,128)(2,1)}, bf16[16,512,128]{2,1,0:T(8,128)(2,1)}) custom-call(s32[128]{0:T(128)} %get-tuple-element.26.position, bf16[128,32,512]{2,1,0:T(8,128)(2,1)} %blocks.3, bf16[1,512,8192]{2,1,0:T(8,128)(2,1)} %front.3), custom_call_target="tpu_custom_call" | custom-call | bytes 16777216 | tf_op jit(solution)/shard_map/pack_rest/pallas_call | solution.py:360
  25.8 25.1 %all-to-all-done.arrived.first = bf16[128,72,128]{2,1,0:T(8,128)(2,1)S(1)} async-done(((bf16[128,72,128]{2,1,0:T(8,128)(2,1)}), bf16[128,72,128]{2,1,0:T(8,128)(2,1)S(1)}, u32[]{:S(2)}, u32[]{:S(2)}) %all-to-all-start) | async-done | bytes 2359328 | tf_op jit(solution)/shard_map/all_to_all | solution.py:359
  50.9 0.0 copy-start.4
  50.9 5.7 %all-to-all-start.2 = ((bf16[256,32,128]{2,1,0:T(8,128)(2,1)}), bf16[256,32,128]{2,1,0:T(8,128)(2,1)}, u32[]{:S(2)}, u32[]{:S(2)}) async-start(bf16[256,32,128]{2,1,0:T(8,128)(2,1)} %get-tuple-element.44), calls=%async_computation.2 | async-start | bytes 4194304 | tf_op jit(solution)/shard_map/all_to_all | solution.py:379
  56.6 0.0 copy-done.4
  56.6 16.0 %panels.1 = (f32[512,512]{1,0:T(8,128)}, f32[512,512]{1,0:T(8,128)}, s16[944,512]{1,0:T(8,128)(2,1)}, s32[8,128]{1,0:T(8,128)}, s32[17]{0:T(128)}, /*index=5*/s3...) custom-call(bf16[128,72,128]{2,1,0:T(8,128)(2,1)} %copy-done.4, bf16[16,512,128]{2,1,0:T(8,128)(2,1)} %get-tuple-element.30.entries, ...), custom_call_target="tpu_custom_call" | custom-call | flops 2000000000 | bytes 10485760 | tf_op jit(solution)/shard_map/panels/pallas_call | solution.py:387
  72.6 93.1 %all-gather.2 = s16[15104,512]{1,0:T(8,128)(2,1)} all-gather(s16[944,512]{1,0:T(8,128)(2,1)} %get-tuple-element.34), channel_id=2, replica_groups=mesh['front'=8,'grp'=16] {'grp'}, dimensions={0}, use_global_device_ids=true | all-gather | bytes 16433152 | tf_op jit(solution)/shard_map/all_gather | solution.py:411
  165.7 0.0 all-to-all-done.2.middle
  165.7 6.2 %all-to-all-start.1 = ((bf16[256,32,256]{2,1,0:T(8,128)(2,1)}), bf16[256,32,256]{2,1,0:T(8,128)(2,1)}, u32[]{:S(2)}, u32[]{:S(2)}) async-start(bf16[256,32,256]{2,1,0:T(8,128)(2,1)} %get-tuple-element.36), calls=%async_computation.1 | async-start | bytes 8388608 | tf_op jit(solution)/shard_map/all_to_all | solution.py:414
  171.9 8.6 %left_factors.1 = (f32[1,2,512,512]{3,2,1,0:T(8,128)}, bf16[2,448,1536]{2,1,0:T(8,128)(2,1)}) custom-call(s16[16,944,512]{2,1,0:T(8,128)(2,1)} %bitcast.2, f32[512,512]{1,0:T(8,128)} %get-tuple-element.41.factor, f32[512,512]{1,0:T(8,128)} %get-tuple-element.42.second, f32[1,2,512,512]{3,2,1,0:T(8,128)} %inverse.3), custom_call_target="tpu_custom_call" | custom-call | flops 4000000000 | bytes 8388608 | tf_op jit(solution)/shard_map/left_factors/pallas_call | solution.py:416
  180.5 32.8 %update.1 = (bf16[16,448,256]{2,1,0:T(8,128)(2,1)S(1)}, f32[16,448,256]{2,1,0:T(8,128)S(1)}) custom-call(s32[8,128]{1,0:T(8,128)} %get-tuple-element.37.label, s32[16]{0:T(128)} %get-tuple-element.38.head, s32[256]{0:T(256)} %get-tuple-element.39.follow, bf16[2,448,1536]{2,1,0:T(8,128)(2,1)} %get-tuple-element.43.left, s16[16,944,512]{2,1,0:T(8,128)(2,1)} %bitcast.3, ...), custom_call_target="tpu_custom_call" | custom-call | flops 20000000000 | bytes 41943040 | tf_op jit(solution)/shard_map/update/pallas_call | solution.py:435
  213.3 0.0 copy-start
  213.3 2.9 %copy-done = f32[16,448,256]{2,1,0:T(8,128)} copy-done((f32[16,448,256]{2,1,0:T(8,128)}, f32[16,448,256]{2,1,0:T(8,128)S(1)}, u32[]{:S(2)}) %copy-start) | copy-done | bytes 7340056
  216.2 0.0 copy-start.2
  216.2 1.9 copy-done.2
  218.1 5.9 %all-to-all-done.1.rest = bf16[256,32,256]{2,1,0:T(8,128)(2,1)} async-done(((bf16[256,32,256]{2,1,0:T(8,128)(2,1)}), bf16[256,32,256]{2,1,0:T(8,128)(2,1)}, u32[]{:S(2)}, u32[]{:S(2)}) %all-to-all-start.1) | async-done | bytes 4194336 | tf_op jit(solution)/shard_map/all_to_all | solution.py:414
  224.0 0.0 copy-start.1
  224.0 3.1 %copy-done.1 = f32[16,448,256]{2,1,0:T(8,128)S(1)} copy-done((f32[16,448,256]{2,1,0:T(8,128)S(1)}, f32[16,448,256]{2,1,0:T(8,128)}, u32[]{:S(2)}) %copy-start.1) | copy-done | bytes 7340056
  227.1 0.0 copy-start.3
  227.1 2.0 copy-done.3
  229.1 6.7 %finish.1 = bf16[1,448,7168]{2,1,0:T(8,128)(2,1)} custom-call(s32[17]{0:T(128)} %get-tuple-element.31.start, s32[256]{0:T(256)} %get-tuple-element.32.order, s32[256]{0:T(256)} %get-tuple-element.33.column, bf16[256,32,256]{2,1,0:T(8,128)(2,1)} %all-to-all-done.1.rest, bf16[16,448,256]{2,1,0:T(8,128)(2,1)S(1)} %copy-done.3, f32[16,448,256]{2,1,0:T(8,128)S(1)} %copy-done.1), custom_call_target="tpu_custom_call" | custom-call | flops 10000000 | bytes 31457280 | tf_op jit(solution)/shard_map/finish/pallas_call | solution.py:464
Async XLA Ops:
  7.0 44.0 %all-to-all-start = ((bf16[128,72,128]{2,1,0:T(8,128)(2,1)}), bf16[128,72,128]{2,1,0:T(8,128)(2,1)S(1)}, u32[]{:S(2)}, u32[]{:S(2)}) async-start(bf16[128,72,128]{2,1,0:T(8,128)(2,1)} %get-tuple-element.25), calls=%async_computation | async-start | bytes 4718592 | tf_op jit(solution)/shard_map/all_to_all | solution.py:359
  50.9 5.7 %copy-start.4 = (bf16[128,72,128]{2,1,0:T(8,128)(2,1)}, bf16[128,72,128]{2,1,0:T(8,128)(2,1)S(1)}, u32[]{:S(2)}) copy-start(bf16[128,72,128]{2,1,0:T(8,128)(2,1)S(1)} %all-to-all-done.arrived.first) | copy-start | bytes 7077892
  50.9 114.8 %all-to-all-start.2 = ((bf16[256,32,128]{2,1,0:T(8,128)(2,1)}), bf16[256,32,128]{2,1,0:T(8,128)(2,1)}, u32[]{:S(2)}, u32[]{:S(2)}) async-start(bf16[256,32,128]{2,1,0:T(8,128)(2,1)} %get-tuple-element.44), calls=%async_computation.2 | async-start | bytes 4194304 | tf_op jit(solution)/shard_map/all_to_all | solution.py:379
  165.7 58.3 %all-to-all-start.1 = ((bf16[256,32,256]{2,1,0:T(8,128)(2,1)}), bf16[256,32,256]{2,1,0:T(8,128)(2,1)}, u32[]{:S(2)}, u32[]{:S(2)}) async-start(bf16[256,32,256]{2,1,0:T(8,128)(2,1)} %get-tuple-element.36), calls=%async_computation.1 | async-start | bytes 8388608 | tf_op jit(solution)/shard_map/all_to_all | solution.py:414
  213.3 2.9 %copy-start = (f32[16,448,256]{2,1,0:T(8,128)}, f32[16,448,256]{2,1,0:T(8,128)S(1)}, u32[]{:S(2)}) copy-start(f32[16,448,256]{2,1,0:T(8,128)S(1)} %get-tuple-element.46.open_) | copy-start | bytes 22020100
  216.2 1.9 copy-start.2
  224.0 3.1 %copy-start.1 = (f32[16,448,256]{2,1,0:T(8,128)S(1)}, f32[16,448,256]{2,1,0:T(8,128)}, u32[]{:S(2)}) copy-start(f32[16,448,256]{2,1,0:T(8,128)} %copy-done) | copy-start | bytes 22020100
  227.1 2.0 copy-start.3

commit v5 on v4

--- a/solution.py
+++ b/solution.py
@@ -294,8 +294,8 @@
             right[k, rows - kept[k] :, panel : 2 * panel] = low
             right[k, rows - kept[k] :, 2 * panel :] = high
             total = total - dot_nt(left[k], right[k]) * scale[k : k + 1]
-        done[2 * step + d] = total[:, : 2 * LANE].astype(jnp.bfloat16)
-        open_[2 * step + d] = total[:, 2 * LANE :]
+        done[d] = total[:, : 2 * LANE].astype(jnp.bfloat16)
+        open_[d] = total[:, 2 * LANE :]
 
 
 def finish_kernel(pivots, start, order, column, rest, done, open_, out, acc):
@@ -305,7 +305,6 @@
     kept = 4 * LANE - dead
     per = step_rows // block_rows
     row = pl.program_id(0) * per + groups - pl.num_programs(0) * per
-    here = pl.ds(pl.multiple_of(pl.program_id(0) * step_rows, ROWTILE), step_rows)
     acc[...] = jnp.zeros(acc.shape, jnp.float32)
     for p in range(per):
 
@@ -317,8 +316,8 @@
     for m in range(groups // 2):
         sides = []
         for c in (2 * m, 2 * m + 1):
-            sides.append(done[c, here, dead:])
-            sides.append((open_[c, here] + acc[c]).astype(jnp.bfloat16))
+            sides.append(done[c, :, dead:])
+            sides.append((open_[c] + acc[c]).astype(jnp.bfloat16))
         pair = jnp.concatenate(sides, axis=1)
         out[0, :, 2 * m * kept : 2 * (m + 1) * kept] = pair
 
@@ -334,7 +333,6 @@
     slot_count = 2 * device_total
     rest_cols = block_cols - 2 * LANE
     hbm = pl.BlockSpec(memory_space=pl.ANY)
-    vmem = pl.BlockSpec(memory_space=pltpu.VMEM)
     smem = pl.BlockSpec(memory_space=pltpu.SMEM)
     whole = lambda *shape: pl.BlockSpec(shape, lambda i: (0,) * len(shape))
 
@@ -343,11 +341,11 @@
         pack_first_kernel,
         grid=(1,),
         out_shape=(
-            pltpu.VMEM((device_total, first_rows, LANE), jnp.bfloat16),
+            jax.ShapeDtypeStruct((device_total, first_rows, LANE), jnp.bfloat16),
             jax.ShapeDtypeStruct((slots,), jnp.int32),
         ),
         in_specs=[smem, smem, smem, hbm],
-        out_specs=(vmem, smem),
+        out_specs=(whole(device_total, first_rows, LANE), smem),
         scratch_shapes=[
             pltpu.VMEM((slots, block_rows, LANE), jnp.bfloat16),
             pltpu.SMEM((3, device_total), jnp.int32),
@@ -436,8 +434,8 @@
         functools.partial(update_kernel, pivots),
         grid=(grp_total // 2,),
         out_shape=(
-            pltpu.VMEM((grp_total, kept, 2 * LANE), jnp.bfloat16),
-            pltpu.VMEM((grp_total, kept, rest_cols), jnp.float32),
+            jax.ShapeDtypeStruct((grp_total, kept, 2 * LANE), jnp.bfloat16),
+            jax.ShapeDtypeStruct((grp_total, kept, rest_cols), jnp.float32),
         ),
         in_specs=[
             smem,
@@ -449,18 +447,20 @@
             whole(*first.shape),
             whole(*middle.shape),
         ],
-        out_specs=(vmem, vmem),
+        out_specs=(
+            pl.BlockSpec((2, kept, 2 * LANE), lambda i: (i, 0, 0)),
+            pl.BlockSpec((2, kept, rest_cols), lambda i: (i, 0, 0)),
+        ),
         scratch_shapes=[
             pltpu.VMEM((2, rows, 3 * panel), jnp.bfloat16),
             pltpu.VMEM((2, rows, 2 * LANE), jnp.float32),
         ],
-        compiler_params=params(52),
+        compiler_params=params(),
         cost_estimate=pl.CostEstimate(flops=20 * 10**9, bytes_accessed=40 * 2**20, transcendentals=0),
         name="update",
     )(label, head, follow, left, gathered, front_entries, first, middle)
 
     step_rows = kept // 2
-    done, open_ = (pltpu.with_memory_space_constraint(x, pltpu.VMEM) for x in (done, open_))
     schur = pl.pallas_call(
         functools.partial(finish_kernel, pivots),
         grid=(kept // step_rows,),
@@ -470,12 +470,12 @@
             smem,
             smem,
             whole(*rest.shape),
-            vmem,
-            vmem,
+            pl.BlockSpec((grp_total, step_rows, 2 * LANE), lambda i: (0, i, 0)),
+            pl.BlockSpec((grp_total, step_rows, rest_cols), lambda i: (0, i, 0)),
         ],
         out_specs=pl.BlockSpec((1, step_rows, grp_total * kept), lambda i: (0, i, 0)),
         scratch_shapes=[pltpu.VMEM((grp_total, step_rows, rest_cols), jnp.float32)],
-        compiler_params=params(52),
+        compiler_params=params(),
         cost_estimate=pl.CostEstimate(flops=10**7, bytes_accessed=30 * 2**20, transcendentals=0),
         name="finish",
     )(start, order, column, rest, done, open_)

time: 237 us -> 233 us (0.983)
  local copies, waits for them, and re-layouts: 9.96 us -> 0.01 us
  Pallas kernels: 77.1 us -> 83.5 us
    unnamed x10 -> x2, local copies, waits for them, and re-layouts: 9.96 us -> 0.01 us
    pallas_call x1, Pallas kernels: 32.8 us -> 36.6 us  [local(): pl.pallas_call(functools.partial(update_kernel, pivots), grid=(grp_total...]
    pallas_call x1, Pallas kernels: 6.73 us -> 9.35 us  [local(): pl.pallas_call(functools.partial(finish_kernel, pivots), grid=(kept // st...]
  transfers between devices with their start and end apart: 3 -> 3, of which waited for: 2 -> 2; matrix products, arithmetic and copies ran while one was open for 0% -> 0% of each run, Pallas kernels for 27% -> 29%
where the time goes in v5:
time: 233 us
  blocking collectives  93.1 us (40%)
  Pallas kernels  83.5 us (36%)
  waiting for transfers between devices  32.1 us (14%)
  starting transfers between devices  23.3 us (10%)
    all_gather x1, blocking collectives, local(): gathered = lax.all_gather(code, 'grp', axis=0, tiled=False)  93.1 us
    pallas_call x1, Pallas kernels, local(): pl.pallas_call(functools.partial(update_kernel, pivots), grid=(grp_total...  36.6 us
    all_to_all x1, waiting for transfers between devices, local(): lax.all_to_all(first_out, axes, split_axis=0, concat_axis=0, tiled=True)  25.1 us
    pallas_call x1, Pallas kernels, local(): pl.pallas_call(functools.partial(panel_kernel, pivots), grid=(1,), out_sh...  16 us
    all_to_all x1, starting transfers between devices, local(): lax.all_to_all(first_out, axes, split_axis=0, concat_axis=0, tiled=True)  11.5 us
    pallas_call x1, Pallas kernels, local(): pl.pallas_call(functools.partial(finish_kernel, pivots), grid=(kept // st...  9.35 us
    pallas_call x1, Pallas kernels, local(): pl.pallas_call(functools.partial(left_kernel, pivots), grid=(1,), out_sha...  8.51 us
    pallas_call x1, Pallas kernels, local(): pl.pallas_call(pack_rest_kernel, grid=(1,), out_shape=(jax.ShapeDtypeStru...  7.3 us
  transfers between devices with their start and end apart: 3, of which 2 were waited for; matrix products, arithmetic and copies ran while one was open for 0% of the time, Pallas kernels for 29%

profile of v5, /device:TPU:1, one launch (start us, length us, event | category | flops | bytes accessed | tf_op | source)
XLA Modules:
  0.0 233.3 jit_solution(2242054384164361131)
XLA Ops:
  1.3 5.7 %pack_first.1 = (bf16[128,72,128]{2,1,0:T(8,128)(2,1)}, s32[128]{0:T(128)}) custom-call(s32[1]{0:T(128)S(6)} %copy.8.count, s32[128]{0:T(128)} %bitcast.4, s32[128]{0:T(128)} %tile.1, bf16[128,32,512]{2,1,0:T(8,128)(2,1)} %blocks.3), custom_call_target="tpu_custom_call" | custom-call | tf_op jit(solution)/shard_map/pack_first/pallas_call | solution.py:340
  6.9 11.5 %all-to-all-start = ((bf16[128,72,128]{2,1,0:T(8,128)(2,1)}), bf16[128,72,128]{2,1,0:T(8,128)(2,1)S(1)}, u32[]{:S(2)}, u32[]{:S(2)}) async-start(bf16[128,72,128]{2,1,0:T(8,128)(2,1)} %get-tuple-element.25), calls=%async_computation | async-start | bytes 4718592 | tf_op jit(solution)/shard_map/all_to_all | solution.py:357
  18.4 7.3 %pack_rest.1 = (bf16[256,32,128]{2,1,0:T(8,128)(2,1)}, bf16[256,32,256]{2,1,0:T(8,128)(2,1)}, bf16[16,512,128]{2,1,0:T(8,128)(2,1)}) custom-call(s32[128]{0:T(128)} %get-tuple-element.26.position, bf16[128,32,512]{2,1,0:T(8,128)(2,1)} %blocks.3, bf16[1,512,8192]{2,1,0:T(8,128)(2,1)} %front.3), custom_call_target="tpu_custom_call" | custom-call | bytes 16777216 | tf_op jit(solution)/shard_map/pack_rest/pallas_call | solution.py:358
  25.8 25.1 %all-to-all-done.arrived.first = bf16[128,72,128]{2,1,0:T(8,128)(2,1)S(1)} async-done(((bf16[128,72,128]{2,1,0:T(8,128)(2,1)}), bf16[128,72,128]{2,1,0:T(8,128)(2,1)S(1)}, u32[]{:S(2)}, u32[]{:S(2)}) %all-to-all-start) | async-done | bytes 2359328 | tf_op jit(solution)/shard_map/all_to_all | solution.py:357
  50.9 0.0 copy-start
  50.9 5.7 %all-to-all-start.2 = ((bf16[256,32,128]{2,1,0:T(8,128)(2,1)}), bf16[256,32,128]{2,1,0:T(8,128)(2,1)}, u32[]{:S(2)}, u32[]{:S(2)}) async-start(bf16[256,32,128]{2,1,0:T(8,128)(2,1)} %get-tuple-element.44), calls=%async_computation.2 | async-start | bytes 4194304 | tf_op jit(solution)/shard_map/all_to_all | solution.py:377
  56.6 0.0 copy-done
  56.6 16.0 %panels.1 = (f32[512,512]{1,0:T(8,128)}, f32[512,512]{1,0:T(8,128)}, s16[944,512]{1,0:T(8,128)(2,1)}, s32[8,128]{1,0:T(8,128)}, s32[17]{0:T(128)}, /*index=5*/s3...) custom-call(bf16[128,72,128]{2,1,0:T(8,128)(2,1)} %copy-done, bf16[16,512,128]{2,1,0:T(8,128)(2,1)} %get-tuple-element.30.entries, ...), custom_call_target="tpu_custom_call" | custom-call | flops 2000000000 | bytes 10485760 | tf_op jit(solution)/shard_map/panels/pallas_call | solution.py:385
  72.6 93.1 %all-gather.2 = s16[15104,512]{1,0:T(8,128)(2,1)} all-gather(s16[944,512]{1,0:T(8,128)(2,1)} %get-tuple-element.34), channel_id=2, replica_groups=mesh['front'=8,'grp'=16] {'grp'}, dimensions={0}, use_global_device_ids=true | all-gather | bytes 16433152 | tf_op jit(solution)/shard_map/all_gather | solution.py:409
  165.7 0.0 all-to-all-done.2.middle
  165.7 6.1 %all-to-all-start.1 = ((bf16[256,32,256]{2,1,0:T(8,128)(2,1)}), bf16[256,32,256]{2,1,0:T(8,128)(2,1)}, u32[]{:S(2)}, u32[]{:S(2)}) async-start(bf16[256,32,256]{2,1,0:T(8,128)(2,1)} %get-tuple-element.36), calls=%async_computation.1 | async-start | bytes 8388608 | tf_op jit(solution)/shard_map/all_to_all | solution.py:412
  171.9 8.5 %left_factors.1 = (f32[1,2,512,512]{3,2,1,0:T(8,128)}, bf16[2,448,1536]{2,1,0:T(8,128)(2,1)}) custom-call(s16[16,944,512]{2,1,0:T(8,128)(2,1)} %bitcast.2, f32[512,512]{1,0:T(8,128)} %get-tuple-element.41.factor, f32[512,512]{1,0:T(8,128)} %get-tuple-element.42.second, f32[1,2,512,512]{3,2,1,0:T(8,128)} %inverse.3), custom_call_target="tpu_custom_call" | custom-call | flops 4000000000 | bytes 8388608 | tf_op jit(solution)/shard_map/left_factors/pallas_call | solution.py:414
  180.4 36.6 %update.1 = (bf16[16,448,256]{2,1,0:T(8,128)(2,1)}, f32[16,448,256]{2,1,0:T(8,128)}) custom-call(s32[8,128]{1,0:T(8,128)} %get-tuple-element.37.label, s32[16]{0:T(128)} %get-tuple-element.38.head, s32[256]{0:T(256)} %get-tuple-element.39.follow, bf16[2,448,1536]{2,1,0:T(8,128)(2,1)} %get-tuple-element.43.left, s16[16,944,512]{2,1,0:T(8,128)(2,1)} %bitcast.3, ...), custom_call_target="tpu_custom_call" | custom-call | flops 20000000000 | bytes 41943040 | tf_op jit(solution)/shard_map/update/pallas_call | solution.py:433
  217.0 6.9 %all-to-all-done.1.rest = bf16[256,32,256]{2,1,0:T(8,128)(2,1)} async-done(((bf16[256,32,256]{2,1,0:T(8,128)(2,1)}), bf16[256,32,256]{2,1,0:T(8,128)(2,1)}, u32[]{:S(2)}, u32[]{:S(2)}) %all-to-all-start.1) | async-done | bytes 4194336 | tf_op jit(solution)/shard_map/all_to_all | solution.py:412
  224.0 9.3 %finish.1 = bf16[1,448,7168]{2,1,0:T(8,128)(2,1)} custom-call(s32[17]{0:T(128)} %get-tuple-element.31.start, s32[256]{0:T(256)} %get-tuple-element.32.order, s32[256]{0:T(256)} %get-tuple-element.33.column, bf16[256,32,256]{2,1,0:T(8,128)(2,1)} %all-to-all-done.1.rest, bf16[16,448,256]{2,1,0:T(8,128)(2,1)} %get-tuple-element.45.done, ...), custom_call_target="tpu_custom_call" | custom-call | flops 10000000 | bytes 31457280 | tf_op jit(solution)/shard_map/finish/pallas_call | solution.py:464
Async XLA Ops:
  6.9 44.0 %all-to-all-start = ((bf16[128,72,128]{2,1,0:T(8,128)(2,1)}), bf16[128,72,128]{2,1,0:T(8,128)(2,1)S(1)}, u32[]{:S(2)}, u32[]{:S(2)}) async-start(bf16[128,72,128]{2,1,0:T(8,128)(2,1)} %get-tuple-element.25), calls=%async_computation | async-start | bytes 4718592 | tf_op jit(solution)/shard_map/all_to_all | solution.py:357
  50.9 5.7 %copy-start = (bf16[128,72,128]{2,1,0:T(8,128)(2,1)}, bf16[128,72,128]{2,1,0:T(8,128)(2,1)S(1)}, u32[]{:S(2)}) copy-start(bf16[128,72,128]{2,1,0:T(8,128)(2,1)S(1)} %all-to-all-done.arrived.first) | copy-start | bytes 7077892
  50.9 114.8 %all-to-all-start.2 = ((bf16[256,32,128]{2,1,0:T(8,128)(2,1)}), bf16[256,32,128]{2,1,0:T(8,128)(2,1)}, u32[]{:S(2)}, u32[]{:S(2)}) async-start(bf16[256,32,128]{2,1,0:T(8,128)(2,1)} %get-tuple-element.44), calls=%async_computation.2 | async-start | bytes 4194304 | tf_op jit(solution)/shard_map/all_to_all | solution.py:377
  165.7 58.2 %all-to-all-start.1 = ((bf16[256,32,256]{2,1,0:T(8,128)(2,1)}), bf16[256,32,256]{2,1,0:T(8,128)(2,1)}, u32[]{:S(2)}, u32[]{:S(2)}) async-start(bf16[256,32,256]{2,1,0:T(8,128)(2,1)} %get-tuple-element.36), calls=%async_computation.1 | async-start | bytes 8388608 | tf_op jit(solution)/shard_map/all_to_all | solution.py:412

commit v6 on v5

--- a/solution.py
+++ b/solution.py
@@ -254,7 +254,7 @@
 
 
 def update_kernel(
-    pivots, label, head, follow, left, code, front, first, middle, done, open_, right, acc
+    pivots, label, head, follow, left, code, front, first, middle, base, edge, open_, right, acc
 ):
     rows, panel = right.shape[1], code.shape[2]
     groups = head.shape[0]
@@ -282,6 +282,7 @@
 
     kept = (rows - pivots, rows - dead)
     starts = (0, kept[0])
+    sides = []
     for d in range(2):
         scale = scale_of(code[d, kept[0] + kept[1] :])
         columns = slice(d * rows + 2 * LANE, (d + 1) * rows)
@@ -294,17 +295,21 @@
             right[k, rows - kept[k] :, panel : 2 * panel] = low
             right[k, rows - kept[k] :, 2 * panel :] = high
             total = total - dot_nt(left[k], right[k]) * scale[k : k + 1]
-        done[d] = total[:, : 2 * LANE].astype(jnp.bfloat16)
         open_[d] = total[:, 2 * LANE :]
-
-
-def finish_kernel(pivots, start, order, column, rest, done, open_, out, acc):
-    groups, step_rows, _ = acc.shape
+        sides.append(total.astype(jnp.bfloat16))
+    even, odd = sides
+    base[0] = jnp.concatenate([even[:, dead:], odd[:, dead:]], axis=1)
+    edge[0] = jnp.concatenate([even[:, 2 * LANE - dead : 2 * LANE], odd[:, dead : 2 * dead]], axis=1)
+
+
+def finish_kernel(pivots, start, order, column, rest, edge, open_, base, out, acc, even, odd, sem):
+    groups, step_rows, width = acc.shape
     block_rows = rest.shape[1]
     dead = 2 * pivots
-    kept = 4 * LANE - dead
+    pair_width = base.shape[2] // (groups // 2)
     per = step_rows // block_rows
-    row = pl.program_id(0) * per + groups - pl.num_programs(0) * per
+    step, steps = pl.program_id(0), pl.num_programs(0)
+    row = step * per + groups - steps * per
     acc[...] = jnp.zeros(acc.shape, jnp.float32)
     for p in range(per):
 
@@ -313,13 +318,33 @@
             block = rest[order[i]].astype(jnp.float32)
             acc[column[i], p * block_rows : (p + 1) * block_rows, :] += block
 
+    def copies(at, m):
+        here = pl.ds(pl.multiple_of(at * step_rows, ROWTILE), step_rows)
+        first = m * pair_width + LANE
+        last = (m + 1) * pair_width - width
+        return (
+            pltpu.make_async_copy(
+                even.at[at, m], out.at[0, here, pl.ds(first, even.shape[3])], sem.at[at, m]
+            ),
+            pltpu.make_async_copy(
+                odd.at[at, m], out.at[0, here, pl.ds(last, width)], sem.at[at, groups // 2 + m]
+            ),
+        )
+
     for m in range(groups // 2):
-        sides = []
-        for c in (2 * m, 2 * m + 1):
-            sides.append(done[c, :, dead:])
-            sides.append((open_[c] + acc[c]).astype(jnp.bfloat16))
-        pair = jnp.concatenate(sides, axis=1)
-        out[0, :, 2 * m * kept : 2 * (m + 1) * kept] = pair
+        low = (open_[2 * m] + acc[2 * m]).astype(jnp.bfloat16)
+        even[step, m] = jnp.concatenate([edge[m, :, :dead], low, edge[m, :, dead:]], axis=1)
+        odd[step, m] = (open_[2 * m + 1] + acc[2 * m + 1]).astype(jnp.bfloat16)
+        for copy in copies(step, m):
+            copy.start()
+
+    @pl.when(step == steps - 1)
+    def _():
+        @pl.loop(0, steps)
+        def _(at):
+            for m in range(groups // 2):
+                for copy in copies(at, m):
+                    copy.wait()
 
 
 def local(front_entries, child_blocks, dest_device, dest_tile, child_count, diag_inverse):
@@ -430,11 +455,12 @@
         name="left_factors",
     )(gathered, factor, second, diag_inverse)
 
-    done, open_ = pl.pallas_call(
+    base, edge, open_ = pl.pallas_call(
         functools.partial(update_kernel, pivots),
         grid=(grp_total // 2,),
         out_shape=(
-            jax.ShapeDtypeStruct((grp_total, kept, 2 * LANE), jnp.bfloat16),
+            jax.ShapeDtypeStruct((1, kept, grp_total * kept), jnp.bfloat16),
+            jax.ShapeDtypeStruct((grp_total // 2, kept, LANE), jnp.bfloat16),
             jax.ShapeDtypeStruct((grp_total, kept, rest_cols), jnp.float32),
         ),
         in_specs=[
@@ -448,7 +474,8 @@
             whole(*middle.shape),
         ],
         out_specs=(
-            pl.BlockSpec((2, kept, 2 * LANE), lambda i: (i, 0, 0)),
+            pl.BlockSpec((1, kept, 2 * kept), lambda i: (0, 0, i)),
+            pl.BlockSpec((1, kept, LANE), lambda i: (i, 0, 0)),
             pl.BlockSpec((2, kept, rest_cols), lambda i: (i, 0, 0)),
         ),
         scratch_shapes=[
@@ -470,15 +497,22 @@
             smem,
             smem,
             whole(*rest.shape),
-            pl.BlockSpec((grp_total, step_rows, 2 * LANE), lambda i: (0, i, 0)),
+            pl.BlockSpec((grp_total // 2, step_rows, LANE), lambda i: (0, i, 0)),
             pl.BlockSpec((grp_total, step_rows, rest_cols), lambda i: (0, i, 0)),
-        ],
-        out_specs=pl.BlockSpec((1, step_rows, grp_total * kept), lambda i: (0, i, 0)),
-        scratch_shapes=[pltpu.VMEM((grp_total, step_rows, rest_cols), jnp.float32)],
+            hbm,
+        ],
+        out_specs=hbm,
+        input_output_aliases={6: 0},
+        scratch_shapes=[
+            pltpu.VMEM((grp_total, step_rows, rest_cols), jnp.float32),
+            pltpu.VMEM((2, grp_total // 2, step_rows, rest_cols + LANE), jnp.bfloat16),
+            pltpu.VMEM((2, grp_total // 2, step_rows, rest_cols), jnp.bfloat16),
+            pltpu.SemaphoreType.DMA((2, grp_total)),
+        ],
         compiler_params=params(),
         cost_estimate=pl.CostEstimate(flops=10**7, bytes_accessed=30 * 2**20, transcendentals=0),
         name="finish",
-    )(start, order, column, rest, done, open_)
+    )(start, order, column, rest, edge, open_, base)
     return schur, factors
 
 

time: 233 us -> 232 us (level)
  Pallas kernels: 83.5 us -> 78.6 us
  waiting for transfers between devices: 32.1 us -> 34.6 us
    all_to_all x1, waiting for transfers between devices: 6.94 us -> 9.48 us  [local(): lax.all_to_all(rest_out, axes, split_axis=0, concat_axis=0, tiled=True)]
    pallas_call x1, Pallas kernels: 36.6 us -> 34.1 us  [local(): pl.pallas_call(functools.partial(update_kernel, pivots), grid=(grp_total...]
where the time goes in v6:
time: 232 us; the launch traced here: 231 us
  blocking collectives  93.1 us (40%)
  Pallas kernels  78.6 us (34%)
  waiting for transfers between devices  34.6 us (15%)
  starting transfers between devices  23.3 us (10%)
    all_gather x1, blocking collectives, local(): gathered = lax.all_gather(code, 'grp', axis=0, tiled=False)  93.1 us
    pallas_call x1, Pallas kernels, local(): pl.pallas_call(functools.partial(update_kernel, pivots), grid=(grp_total...  34.1 us
    all_to_all x1, waiting for transfers between devices, local(): lax.all_to_all(first_out, axes, split_axis=0, concat_axis=0, tiled=True)  25.1 us
    pallas_call x1, Pallas kernels, local(): pl.pallas_call(functools.partial(panel_kernel, pivots), grid=(1,), out_sh...  16 us
    all_to_all x1, starting transfers between devices, local(): lax.all_to_all(first_out, axes, split_axis=0, concat_axis=0, tiled=True)  11.5 us
    all_to_all x1, waiting for transfers between devices, local(): lax.all_to_all(rest_out, axes, split_axis=0, concat_axis=0, tiled=True)  9.48 us
    pallas_call x1, Pallas kernels, local(): pl.pallas_call(functools.partial(left_kernel, pivots), grid=(1,), out_sha...  8.51 us
    pallas_call x1, Pallas kernels, local(): pl.pallas_call(pack_rest_kernel, grid=(1,), out_shape=(jax.ShapeDtypeStru...  7.3 us
  transfers between devices with their start and end apart: 3, of which 2 were waited for; matrix products, arithmetic and copies ran while one was open for 0% of the time, Pallas kernels for 29%

profile of v6, /device:TPU:1, one launch (start us, length us, event | category | flops | bytes accessed | tf_op | source)
XLA Modules:
  0.0 231.2 jit_solution(7154563484146623970)
XLA Ops:
  1.3 5.6 %pack_first.1 = (bf16[128,72,128]{2,1,0:T(8,128)(2,1)}, s32[128]{0:T(128)}) custom-call(s32[1]{0:T(128)S(6)} %copy.10.count, s32[128]{0:T(128)} %bitcast.4, s32[128]{0:T(128)} %tile.1, bf16[128,32,512]{2,1,0:T(8,128)(2,1)} %blocks.3), custom_call_target="tpu_custom_call" | custom-call | tf_op jit(solution)/shard_map/pack_first/pallas_call | solution.py:365
  6.9 11.5 %all-to-all-start = ((bf16[128,72,128]{2,1,0:T(8,128)(2,1)}), bf16[128,72,128]{2,1,0:T(8,128)(2,1)S(1)}, u32[]{:S(2)}, u32[]{:S(2)}) async-start(bf16[128,72,128]{2,1,0:T(8,128)(2,1)} %get-tuple-element.26), calls=%async_computation | async-start | bytes 4718592 | tf_op jit(solution)/shard_map/all_to_all | solution.py:382
  18.4 7.3 %pack_rest.1 = (bf16[256,32,128]{2,1,0:T(8,128)(2,1)}, bf16[256,32,256]{2,1,0:T(8,128)(2,1)}, bf16[16,512,128]{2,1,0:T(8,128)(2,1)}) custom-call(s32[128]{0:T(128)} %get-tuple-element.27.position, bf16[128,32,512]{2,1,0:T(8,128)(2,1)} %blocks.3, bf16[1,512,8192]{2,1,0:T(8,128)(2,1)} %front.3), custom_call_target="tpu_custom_call" | custom-call | bytes 16777216 | tf_op jit(solution)/shard_map/pack_rest/pallas_call | solution.py:383
  25.8 25.1 %all-to-all-done.arrived.first = bf16[128,72,128]{2,1,0:T(8,128)(2,1)S(1)} async-done(((bf16[128,72,128]{2,1,0:T(8,128)(2,1)}), bf16[128,72,128]{2,1,0:T(8,128)(2,1)S(1)}, u32[]{:S(2)}, u32[]{:S(2)}) %all-to-all-start) | async-done | bytes 2359328 | tf_op jit(solution)/shard_map/all_to_all | solution.py:382
  50.9 0.0 copy-start
  50.9 5.7 %all-to-all-start.2 = ((bf16[256,32,128]{2,1,0:T(8,128)(2,1)}), bf16[256,32,128]{2,1,0:T(8,128)(2,1)}, u32[]{:S(2)}, u32[]{:S(2)}) async-start(bf16[256,32,128]{2,1,0:T(8,128)(2,1)} %get-tuple-element.45), calls=%async_computation.2 | async-start | bytes 4194304 | tf_op jit(solution)/shard_map/all_to_all | solution.py:402
  56.6 0.0 copy-done
  56.6 16.0 %panels.1 = (f32[512,512]{1,0:T(8,128)}, f32[512,512]{1,0:T(8,128)}, s16[944,512]{1,0:T(8,128)(2,1)}, s32[8,128]{1,0:T(8,128)}, s32[17]{0:T(128)}, /*index=5*/s3...) custom-call(bf16[128,72,128]{2,1,0:T(8,128)(2,1)} %copy-done, bf16[16,512,128]{2,1,0:T(8,128)(2,1)} %get-tuple-element.31.entries, ...), custom_call_target="tpu_custom_call" | custom-call | flops 2000000000 | bytes 10485760 | tf_op jit(solution)/shard_map/panels/pallas_call | solution.py:410
  72.6 93.1 %all-gather.2 = s16[15104,512]{1,0:T(8,128)(2,1)} all-gather(s16[944,512]{1,0:T(8,128)(2,1)} %get-tuple-element.35), channel_id=2, replica_groups=mesh['front'=8,'grp'=16] {'grp'}, dimensions={0}, use_global_device_ids=true | all-gather | bytes 16433152 | tf_op jit(solution)/shard_map/all_gather | solution.py:434
  165.7 0.0 all-to-all-done.2.middle
  165.7 6.2 %all-to-all-start.1 = ((bf16[256,32,256]{2,1,0:T(8,128)(2,1)}), bf16[256,32,256]{2,1,0:T(8,128)(2,1)}, u32[]{:S(2)}, u32[]{:S(2)}) async-start(bf16[256,32,256]{2,1,0:T(8,128)(2,1)} %get-tuple-element.37), calls=%async_computation.1 | async-start | bytes 8388608 | tf_op jit(solution)/shard_map/all_to_all | solution.py:437
  171.9 8.5 %left_factors.1 = (f32[1,2,512,512]{3,2,1,0:T(8,128)}, bf16[2,448,1536]{2,1,0:T(8,128)(2,1)}) custom-call(s16[16,944,512]{2,1,0:T(8,128)(2,1)} %bitcast.2, f32[512,512]{1,0:T(8,128)} %get-tuple-element.42.factor, f32[512,512]{1,0:T(8,128)} %get-tuple-element.43.second, f32[1,2,512,512]{3,2,1,0:T(8,128)} %inverse.3), custom_call_target="tpu_custom_call" | custom-call | flops 4000000000 | bytes 8388608 | tf_op jit(solution)/shard_map/left_factors/pallas_call | solution.py:439
  180.4 34.1 %update.1 = (bf16[1,448,7168]{2,1,0:T(8,128)(2,1)}, bf16[8,448,128]{2,1,0:T(8,128)(2,1)}, f32[16,448,256]{2,1,0:T(8,128)}) custom-call(s32[8,128]{1,0:T(8,128)} %get-tuple-element.38.label, s32[16]{0:T(128)} %get-tuple-element.39.head, s32[256]{0:T(256)} %get-tuple-element.40.follow, bf16[2,448,1536]{2,1,0:T(8,128)(2,1)} %get-tuple-element.44.left, ...), custom_call_target="tpu_custom_call" | custom-call | flops 20000000000 | bytes 41943040 | tf_op jit(solution)/shard_map/update/pallas_call | solution.py:458
  214.5 9.5 %all-to-all-done.1.rest = bf16[256,32,256]{2,1,0:T(8,128)(2,1)} async-done(((bf16[256,32,256]{2,1,0:T(8,128)(2,1)}), bf16[256,32,256]{2,1,0:T(8,128)(2,1)}, u32[]{:S(2)}, u32[]{:S(2)}) %all-to-all-start.1) | async-done | bytes 4194336 | tf_op jit(solution)/shard_map/all_to_all | solution.py:437
  224.0 7.1 %finish.1 = bf16[1,448,7168]{2,1,0:T(8,128)(2,1)} custom-call(s32[17]{0:T(128)} %get-tuple-element.32.start, s32[256]{0:T(256)} %get-tuple-element.33.order, s32[256]{0:T(256)} %get-tuple-element.34.column, bf16[256,32,256]{2,1,0:T(8,128)(2,1)} %all-to-all-done.1.rest, bf16[8,448,128]{2,1,0:T(8,128)(2,1)} %get-tuple-element.46.edge, ...), custom_call_target="tpu_custom_call", output_to_operand_aliasing={{}: (6, {})} | custom-call | flops 10000000 | bytes 31457280 | tf_op jit(solution)/shard_map/finish/pallas_call | solution.py:491
Async XLA Ops:
  6.9 44.0 %all-to-all-start = ((bf16[128,72,128]{2,1,0:T(8,128)(2,1)}), bf16[128,72,128]{2,1,0:T(8,128)(2,1)S(1)}, u32[]{:S(2)}, u32[]{:S(2)}) async-start(bf16[128,72,128]{2,1,0:T(8,128)(2,1)} %get-tuple-element.26), calls=%async_computation | async-start | bytes 4718592 | tf_op jit(solution)/shard_map/all_to_all | solution.py:382
  50.9 5.7 %copy-start = (bf16[128,72,128]{2,1,0:T(8,128)(2,1)}, bf16[128,72,128]{2,1,0:T(8,128)(2,1)S(1)}, u32[]{:S(2)}) copy-start(bf16[128,72,128]{2,1,0:T(8,128)(2,1)S(1)} %all-to-all-done.arrived.first) | copy-start | bytes 7077892
  50.9 114.8 %all-to-all-start.2 = ((bf16[256,32,128]{2,1,0:T(8,128)(2,1)}), bf16[256,32,128]{2,1,0:T(8,128)(2,1)}, u32[]{:S(2)}, u32[]{:S(2)}) async-start(bf16[256,32,128]{2,1,0:T(8,128)(2,1)} %get-tuple-element.45), calls=%async_computation.2 | async-start | bytes 4194304 | tf_op jit(solution)/shard_map/all_to_all | solution.py:402
  165.7 58.3 %all-to-all-start.1 = ((bf16[256,32,256]{2,1,0:T(8,128)(2,1)}), bf16[256,32,256]{2,1,0:T(8,128)(2,1)}, u32[]{:S(2)}, u32[]{:S(2)}) async-start(bf16[256,32,256]{2,1,0:T(8,128)(2,1)} %get-tuple-element.37), calls=%async_computation.1 | async-start | bytes 8388608 | tf_op jit(solution)/shard_map/all_to_all | solution.py:437

commit v7 on v6

--- a/solution.py
+++ b/solution.py
@@ -9,7 +9,7 @@
 
 LANE = 128
 ROWTILE = 16
-LABELROWS = 8
+LABELROWS = ROWTILE
 MIB = 1024 * 1024
 NT = (((1,), (1,)), ((), ()))
 NN = (((1,), (0,)), ((), ()))

time: 232 us -> 235 us (1.013)
  waiting for transfers between devices: 34.6 us -> 37.3 us
    all_to_all x1, waiting for transfers between devices: 25.1 us -> 27.9 us  [local(): lax.all_to_all(first_out, axes, split_axis=0, concat_axis=0, tiled=True)]
  transfers between devices with their start and end apart: 3 -> 3, of which waited for: 2 -> 2; matrix products, arithmetic and copies ran while one was open for 0% -> 0% of each run, Pallas kernels for 29% -> 28%
where the time goes in v7:
time: 235 us; the launch traced here: 234 us
  blocking collectives  93.1 us (40%)
  Pallas kernels  79.1 us (34%)
  waiting for transfers between devices  37.3 us (16%)
  starting transfers between devices  23.1 us (10%)
    all_gather x1, blocking collectives, local(): gathered = lax.all_gather(code, 'grp', axis=0, tiled=False)  93.1 us
    pallas_call x1, Pallas kernels, local(): pl.pallas_call(functools.partial(update_kernel, pivots), grid=(grp_total...  34.2 us
    all_to_all x1, waiting for transfers between devices, local(): lax.all_to_all(first_out, axes, split_axis=0, concat_axis=0, tiled=True)  27.9 us
    pallas_call x1, Pallas kernels, local(): pl.pallas_call(functools.partial(panel_kernel, pivots), grid=(1,), out_sh...  16.2 us
    all_to_all x1, starting transfers between devices, local(): lax.all_to_all(first_out, axes, split_axis=0, concat_axis=0, tiled=True)  11.5 us
    all_to_all x1, waiting for transfers between devices, local(): lax.all_to_all(rest_out, axes, split_axis=0, concat_axis=0, tiled=True)  9.4 us
    pallas_call x1, Pallas kernels, local(): pl.pallas_call(functools.partial(left_kernel, pivots), grid=(1,), out_sha...  8.51 us
    pallas_call x1, Pallas kernels, local(): pl.pallas_call(pack_rest_kernel, grid=(1,), out_shape=(jax.ShapeDtypeStru...  7.3 us
  transfers between devices with their start and end apart: 3, of which 2 were waited for; matrix products, arithmetic and copies ran while one was open for 0% of the time, Pallas kernels for 28%

profile of v7, /device:TPU:1, one launch (start us, length us, event | category | flops | bytes accessed | tf_op | source)
XLA Modules:
  0.0 234.1 jit_solution(4983946151049403621)
XLA Ops:
  1.3 5.8 %pack_first.1 = (bf16[128,80,128]{2,1,0:T(8,128)(2,1)}, s32[128]{0:T(128)}) custom-call(s32[1]{0:T(128)S(6)} %copy.10.count, s32[128]{0:T(128)} %bitcast.4, s32[128]{0:T(128)} %tile.1, bf16[128,32,512]{2,1,0:T(8,128)(2,1)} %blocks.3), custom_call_target="tpu_custom_call" | custom-call | tf_op jit(solution)/shard_map/pack_first/pallas_call | solution.py:365
  7.0 11.5 %all-to-all-start = ((bf16[128,80,128]{2,1,0:T(8,128)(2,1)}), bf16[128,80,128]{2,1,0:T(8,128)(2,1)S(1)}, u32[]{:S(2)}, u32[]{:S(2)}) async-start(bf16[128,80,128]{2,1,0:T(8,128)(2,1)} %get-tuple-element.26), calls=%async_computation | async-start | bytes 5242880 | tf_op jit(solution)/shard_map/all_to_all | solution.py:382
  18.5 7.3 %pack_rest.1 = (bf16[256,32,128]{2,1,0:T(8,128)(2,1)}, bf16[256,32,256]{2,1,0:T(8,128)(2,1)}, bf16[16,512,128]{2,1,0:T(8,128)(2,1)}) custom-call(s32[128]{0:T(128)} %get-tuple-element.27.position, bf16[128,32,512]{2,1,0:T(8,128)(2,1)} %blocks.3, bf16[1,512,8192]{2,1,0:T(8,128)(2,1)} %front.3), custom_call_target="tpu_custom_call" | custom-call | bytes 16777216 | tf_op jit(solution)/shard_map/pack_rest/pallas_call | solution.py:383
  25.9 27.9 %all-to-all-done.arrived.first = bf16[128,80,128]{2,1,0:T(8,128)(2,1)S(1)} async-done(((bf16[128,80,128]{2,1,0:T(8,128)(2,1)}), bf16[128,80,128]{2,1,0:T(8,128)(2,1)S(1)}, u32[]{:S(2)}, u32[]{:S(2)}) %all-to-all-start) | async-done | bytes 2621472 | tf_op jit(solution)/shard_map/all_to_all | solution.py:382
  53.7 0.0 copy-start
  53.7 5.6 %all-to-all-start.2 = ((bf16[256,32,128]{2,1,0:T(8,128)(2,1)}), bf16[256,32,128]{2,1,0:T(8,128)(2,1)}, u32[]{:S(2)}, u32[]{:S(2)}) async-start(bf16[256,32,128]{2,1,0:T(8,128)(2,1)} %get-tuple-element.45), calls=%async_computation.2 | async-start | bytes 4194304 | tf_op jit(solution)/shard_map/all_to_all | solution.py:402
  59.4 0.0 copy-done
  59.4 16.2 %panels.1 = (f32[512,512]{1,0:T(8,128)}, f32[512,512]{1,0:T(8,128)}, s16[944,512]{1,0:T(8,128)(2,1)}, s32[16,128]{1,0:T(8,128)}, s32[17]{0:T(128)}, /*index=5*/s...) custom-call(bf16[128,80,128]{2,1,0:T(8,128)(2,1)} %copy-done, bf16[16,512,128]{2,1,0:T(8,128)(2,1)} %get-tuple-element.31.entries, ...), custom_call_target="tpu_custom_call" | custom-call | flops 2000000000 | bytes 10485760 | tf_op jit(solution)/shard_map/panels/pallas_call | solution.py:410
  75.6 93.1 %all-gather.2 = s16[15104,512]{1,0:T(8,128)(2,1)} all-gather(s16[944,512]{1,0:T(8,128)(2,1)} %get-tuple-element.35), channel_id=2, replica_groups=mesh['front'=8,'grp'=16] {'grp'}, dimensions={0}, use_global_device_ids=true | all-gather | bytes 16433152 | tf_op jit(solution)/shard_map/all_gather | solution.py:434
  168.7 0.0 all-to-all-done.2.middle
  168.7 6.0 %all-to-all-start.1 = ((bf16[256,32,256]{2,1,0:T(8,128)(2,1)}), bf16[256,32,256]{2,1,0:T(8,128)(2,1)}, u32[]{:S(2)}, u32[]{:S(2)}) async-start(bf16[256,32,256]{2,1,0:T(8,128)(2,1)} %get-tuple-element.37), calls=%async_computation.1 | async-start | bytes 8388608 | tf_op jit(solution)/shard_map/all_to_all | solution.py:437
  174.7 8.5 %left_factors.1 = (f32[1,2,512,512]{3,2,1,0:T(8,128)}, bf16[2,448,1536]{2,1,0:T(8,128)(2,1)}) custom-call(s16[16,944,512]{2,1,0:T(8,128)(2,1)} %bitcast.2, f32[512,512]{1,0:T(8,128)} %get-tuple-element.42.factor, f32[512,512]{1,0:T(8,128)} %get-tuple-element.43.second, f32[1,2,512,512]{3,2,1,0:T(8,128)} %inverse.3), custom_call_target="tpu_custom_call" | custom-call | flops 4000000000 | bytes 8388608 | tf_op jit(solution)/shard_map/left_factors/pallas_call | solution.py:439
  183.2 34.2 %update.1 = (bf16[1,448,7168]{2,1,0:T(8,128)(2,1)}, bf16[8,448,128]{2,1,0:T(8,128)(2,1)}, f32[16,448,256]{2,1,0:T(8,128)}) custom-call(s32[16,128]{1,0:T(8,128)} %get-tuple-element.38.label, s32[16]{0:T(128)} %get-tuple-element.39.head, s32[256]{0:T(256)} %get-tuple-element.40.follow, bf16[2,448,1536]{2,1,0:T(8,128)(2,1)} %get-tuple-element.44.left, ...), custom_call_target="tpu_custom_call" | custom-call | flops 20000000000 | bytes 41943040 | tf_op jit(solution)/shard_map/update/pallas_call | solution.py:458
  217.4 9.4 %all-to-all-done.1.rest = bf16[256,32,256]{2,1,0:T(8,128)(2,1)} async-done(((bf16[256,32,256]{2,1,0:T(8,128)(2,1)}), bf16[256,32,256]{2,1,0:T(8,128)(2,1)}, u32[]{:S(2)}, u32[]{:S(2)}) %all-to-all-start.1) | async-done | bytes 4194336 | tf_op jit(solution)/shard_map/all_to_all | solution.py:437
  226.8 7.1 %finish.1 = bf16[1,448,7168]{2,1,0:T(8,128)(2,1)} custom-call(s32[17]{0:T(128)} %get-tuple-element.32.start, s32[256]{0:T(256)} %get-tuple-element.33.order, s32[256]{0:T(256)} %get-tuple-element.34.column, bf16[256,32,256]{2,1,0:T(8,128)(2,1)} %all-to-all-done.1.rest, bf16[8,448,128]{2,1,0:T(8,128)(2,1)} %get-tuple-element.46.edge, ...), custom_call_target="tpu_custom_call", output_to_operand_aliasing={{}: (6, {})} | custom-call | flops 10000000 | bytes 31457280 | tf_op jit(solution)/shard_map/finish/pallas_call | solution.py:491
Async XLA Ops:
  7.0 46.7 %all-to-all-start = ((bf16[128,80,128]{2,1,0:T(8,128)(2,1)}), bf16[128,80,128]{2,1,0:T(8,128)(2,1)S(1)}, u32[]{:S(2)}, u32[]{:S(2)}) async-start(bf16[128,80,128]{2,1,0:T(8,128)(2,1)} %get-tuple-element.26), calls=%async_computation | async-start | bytes 5242880 | tf_op jit(solution)/shard_map/all_to_all | solution.py:382
  53.7 5.7 %copy-start = (bf16[128,80,128]{2,1,0:T(8,128)(2,1)}, bf16[128,80,128]{2,1,0:T(8,128)(2,1)S(1)}, u32[]{:S(2)}) copy-start(bf16[128,80,128]{2,1,0:T(8,128)(2,1)S(1)} %all-to-all-done.arrived.first) | copy-start | bytes 7864324
  53.7 115.0 %all-to-all-start.2 = ((bf16[256,32,128]{2,1,0:T(8,128)(2,1)}), bf16[256,32,128]{2,1,0:T(8,128)(2,1)}, u32[]{:S(2)}, u32[]{:S(2)}) async-start(bf16[256,32,128]{2,1,0:T(8,128)(2,1)} %get-tuple-element.45), calls=%async_computation.2 | async-start | bytes 4194304 | tf_op jit(solution)/shard_map/all_to_all | solution.py:402
  168.7 58.1 %all-to-all-start.1 = ((bf16[256,32,256]{2,1,0:T(8,128)(2,1)}), bf16[256,32,256]{2,1,0:T(8,128)(2,1)}, u32[]{:S(2)}, u32[]{:S(2)}) async-start(bf16[256,32,256]{2,1,0:T(8,128)(2,1)} %get-tuple-element.37), calls=%async_computation.1 | async-start | bytes 8388608 | tf_op jit(solution)/shard_map/all_to_all | solution.py:437

commit v8 on v6

--- a/solution.py
+++ b/solution.py
@@ -54,8 +54,8 @@
     return jnp.exp2(exponent.astype(jnp.int32).astype(jnp.float32) - 15.0)
 
 
-def pack_first_kernel(count, target, tile, blocks, out, position, load, marks, sem):
-    devices = out.shape[0]
+def pack_first_kernel(count, target, tile, blocks, packed, position, load, out, marks, sem):
+    devices = packed.shape[0]
     slots, rows, _ = blocks.shape
     copy = pltpu.make_async_copy(blocks.at[:, :, pl.ds(0, LANE)], load, sem)
     copy.start()
@@ -87,6 +87,10 @@
     def _(i):
         at = position[i]
         out[at // 2, pl.ds(pl.multiple_of((at % 2) * rows, rows), rows), :] = load[i]
+
+    copy = pltpu.make_async_copy(out.at[pl.ds(0, devices)], packed, sem)
+    copy.start()
+    copy.wait()
 
 
 def pack_rest_kernel(position, blocks, front, middle, rest, entries, sem):
@@ -168,23 +172,26 @@
 
 
 def panel_kernel(
-    pivots, arrived, entries, inverse, factor, second, code, label, start, order, column, head, follow,
-    acc, marks, load, later, result, sem,
+    pivots, sent, entries, inverse, factor, second, code, label, start, order, column, head, follow,
+    arrived, acc, marks, load, later, result, sem,
 ):
     groups, rows, _ = entries.shape
-    sources = arrived.shape[0]
+    sources = sent.shape[0]
     block_rows = rows // groups
     dead = 2 * pivots
+    sent_copy = pltpu.make_async_copy(sent, arrived.at[pl.ds(0, sources)], sem.at[4])
+    sent_copy.start()
     inverse_copy = pltpu.make_async_copy(inverse.at[0, 0], load, sem.at[1])
     inverse_copy.start()
+    acc[:, :rows] = entries[...].astype(jnp.float32)
+    sent_copy.wait()
 
     shape = (sources, LABELROWS, LANE)
     own = lax.broadcasted_iota(jnp.int32, shape, 0) == lax.broadcasted_iota(jnp.int32, shape, 2)
-    sent = arrived[:, 2 * block_rows :, :].astype(jnp.float32)
-    label[...] = jnp.sum(jnp.where(own, sent, 0.0), axis=0).astype(jnp.int32) - 1
+    marked = arrived[:sources, 2 * block_rows :, :].astype(jnp.float32)
+    label[...] = jnp.sum(jnp.where(own, marked, 0.0), axis=0).astype(jnp.int32) - 1
     copy = pltpu.make_async_copy(label, marks, sem.at[0])
     copy.start()
-    acc[:, :rows] = entries[...].astype(jnp.float32)
     copy.wait()
 
     @pl.loop(0, sources, unroll=4)
@@ -370,9 +377,10 @@
             jax.ShapeDtypeStruct((slots,), jnp.int32),
         ),
         in_specs=[smem, smem, smem, hbm],
-        out_specs=(whole(device_total, first_rows, LANE), smem),
+        out_specs=(hbm, smem),
         scratch_shapes=[
             pltpu.VMEM((slots, block_rows, LANE), jnp.bfloat16),
+            pltpu.VMEM((device_total + 1, first_rows, LANE), jnp.bfloat16),
             pltpu.SMEM((3, device_total), jnp.int32),
             pltpu.SemaphoreType.DMA,
         ],
@@ -417,15 +425,16 @@
             jax.ShapeDtypeStruct((LABELROWS, LANE), jnp.int32),
             *(jax.ShapeDtypeStruct((length,), jnp.int32) for length in lengths),
         ),
-        in_specs=[whole(*first.shape), whole(*entries.shape), hbm],
+        in_specs=[hbm, whole(*entries.shape), hbm],
         out_specs=(hbm, hbm, whole(code_rows, panel), whole(LABELROWS, LANE)) + (smem,) * 5,
         scratch_shapes=[
+            pltpu.VMEM((device_total + 1, first_rows, LANE), jnp.bfloat16),
             pltpu.VMEM((grp_total, rows + block_rows, LANE), jnp.float32),
             pltpu.SMEM((LABELROWS, LANE), jnp.int32),
             pltpu.VMEM((panel, panel), jnp.float32),
             pltpu.VMEM((rows, panel), jnp.float32),
             pltpu.VMEM((rows, panel), jnp.float32),
-            pltpu.SemaphoreType.DMA((4,)),
+            pltpu.SemaphoreType.DMA((5,)),
         ],
         compiler_params=params(),
         cost_estimate=pl.CostEstimate(flops=2 * 10**9, bytes_accessed=10 * 2**20, transcendentals=0),

time: 232 us -> 233 us (level)
  no operation moved by 1% of the time
where the time goes in v8:
time: 233 us; the launch traced here: 232 us
  blocking collectives  92.4 us (40%)
  Pallas kernels  80.2 us (34%)
  waiting for transfers between devices  34.5 us (15%)
  starting transfers between devices  23.5 us (10%)
    all_gather x1, blocking collectives, local(): gathered = lax.all_gather(code, 'grp', axis=0, tiled=False)  92.4 us
    pallas_call x1, Pallas kernels, local(): pl.pallas_call(functools.partial(update_kernel, pivots), grid=(grp_total...  34.2 us
    all_to_all x1, waiting for transfers between devices, local(): lax.all_to_all(first_out, axes, split_axis=0, concat_axis=0, tiled=True)  25.1 us
    pallas_call x1, Pallas kernels, local(): pl.pallas_call(functools.partial(panel_kernel, pivots), grid=(1,), out_sh...  16.9 us
    all_to_all x1, starting transfers between devices, local(): lax.all_to_all(first_out, axes, split_axis=0, concat_axis=0, tiled=True)  11.5 us
    all_to_all x1, waiting for transfers between devices, local(): lax.all_to_all(rest_out, axes, split_axis=0, concat_axis=0, tiled=True)  9.34 us
    pallas_call x1, Pallas kernels, local(): pl.pallas_call(functools.partial(left_kernel, pivots), grid=(1,), out_sha...  8.51 us
    pallas_call x1, Pallas kernels, local(): pl.pallas_call(pack_rest_kernel, grid=(1,), out_shape=(jax.ShapeDtypeStru...  7.3 us
  transfers between devices with their start and end apart: 3, of which 2 were waited for; matrix products, arithmetic and copies ran while one was open for 0% of the time, Pallas kernels for 29%

profile of v8, /device:TPU:1, one launch (start us, length us, event | category | flops | bytes accessed | tf_op | source)
XLA Modules:
  0.0 232.2 jit_solution(183958356411234878)
XLA Ops:
  1.3 6.2 %pack_first.1 = (bf16[128,72,128]{2,1,0:T(8,128)(2,1)}, s32[128]{0:T(128)}) custom-call(s32[1]{0:T(128)S(6)} %copy.10.count, s32[128]{0:T(128)} %bitcast.4, s32[128]{0:T(128)} %tile.1, bf16[128,32,512]{2,1,0:T(8,128)(2,1)} %blocks.3), custom_call_target="tpu_custom_call" | custom-call | tf_op jit(solution)/shard_map/pack_first/pallas_call | solution.py:372
  7.4 11.5 %all-to-all-start = ((bf16[128,72,128]{2,1,0:T(8,128)(2,1)}), bf16[128,72,128]{2,1,0:T(8,128)(2,1)S(1)}, u32[]{:S(2)}, u32[]{:S(2)}) async-start(bf16[128,72,128]{2,1,0:T(8,128)(2,1)} %get-tuple-element.26), calls=%async_computation | async-start | bytes 4718592 | tf_op jit(solution)/shard_map/all_to_all | solution.py:390
  18.9 7.3 %pack_rest.1 = (bf16[256,32,128]{2,1,0:T(8,128)(2,1)}, bf16[256,32,256]{2,1,0:T(8,128)(2,1)}, bf16[16,512,128]{2,1,0:T(8,128)(2,1)}) custom-call(s32[128]{0:T(128)} %get-tuple-element.27.position, bf16[128,32,512]{2,1,0:T(8,128)(2,1)} %blocks.3, bf16[1,512,8192]{2,1,0:T(8,128)(2,1)} %front.3), custom_call_target="tpu_custom_call" | custom-call | bytes 16777216 | tf_op jit(solution)/shard_map/pack_rest/pallas_call | solution.py:391
  26.3 25.1 %all-to-all-done.sent.first = bf16[128,72,128]{2,1,0:T(8,128)(2,1)S(1)} async-done(((bf16[128,72,128]{2,1,0:T(8,128)(2,1)}), bf16[128,72,128]{2,1,0:T(8,128)(2,1)S(1)}, u32[]{:S(2)}, u32[]{:S(2)}) %all-to-all-start) | async-done | bytes 2359328 | tf_op jit(solution)/shard_map/all_to_all | solution.py:390
  51.4 0.0 copy-start
  51.4 5.7 %all-to-all-start.2 = ((bf16[256,32,128]{2,1,0:T(8,128)(2,1)}), bf16[256,32,128]{2,1,0:T(8,128)(2,1)}, u32[]{:S(2)}, u32[]{:S(2)}) async-start(bf16[256,32,128]{2,1,0:T(8,128)(2,1)} %get-tuple-element.45), calls=%async_computation.2 | async-start | bytes 4194304 | tf_op jit(solution)/shard_map/all_to_all | solution.py:410
  57.1 0.0 copy-done
  57.1 16.9 %panels.1 = (f32[512,512]{1,0:T(8,128)}, f32[512,512]{1,0:T(8,128)}, s16[944,512]{1,0:T(8,128)(2,1)}, s32[8,128]{1,0:T(8,128)}, s32[17]{0:T(128)}, /*index=5*/s3...) custom-call(bf16[128,72,128]{2,1,0:T(8,128)(2,1)} %copy-done, bf16[16,512,128]{2,1,0:T(8,128)(2,1)} %get-tuple-element.31.entries, ...), custom_call_target="tpu_custom_call" | custom-call | flops 2000000000 | bytes 10485760 | tf_op jit(solution)/shard_map/panels/pallas_call | solution.py:418
  74.0 92.4 %all-gather.2 = s16[15104,512]{1,0:T(8,128)(2,1)} all-gather(s16[944,512]{1,0:T(8,128)(2,1)} %get-tuple-element.35), channel_id=2, replica_groups=mesh['front'=8,'grp'=16] {'grp'}, dimensions={0}, use_global_device_ids=true | all-gather | bytes 16433152 | tf_op jit(solution)/shard_map/all_gather | solution.py:443
  166.4 0.0 all-to-all-done.2.middle
  166.4 6.4 %all-to-all-start.1 = ((bf16[256,32,256]{2,1,0:T(8,128)(2,1)}), bf16[256,32,256]{2,1,0:T(8,128)(2,1)}, u32[]{:S(2)}, u32[]{:S(2)}) async-start(bf16[256,32,256]{2,1,0:T(8,128)(2,1)} %get-tuple-element.37), calls=%async_computation.1 | async-start | bytes 8388608 | tf_op jit(solution)/shard_map/all_to_all | solution.py:446
  172.8 8.5 %left_factors.1 = (f32[1,2,512,512]{3,2,1,0:T(8,128)}, bf16[2,448,1536]{2,1,0:T(8,128)(2,1)}) custom-call(s16[16,944,512]{2,1,0:T(8,128)(2,1)} %bitcast.2, f32[512,512]{1,0:T(8,128)} %get-tuple-element.42.factor, f32[512,512]{1,0:T(8,128)} %get-tuple-element.43.second, f32[1,2,512,512]{3,2,1,0:T(8,128)} %inverse.3), custom_call_target="tpu_custom_call" | custom-call | flops 4000000000 | bytes 8388608 | tf_op jit(solution)/shard_map/left_factors/pallas_call | solution.py:448
  181.3 34.2 %update.1 = (bf16[1,448,7168]{2,1,0:T(8,128)(2,1)}, bf16[8,448,128]{2,1,0:T(8,128)(2,1)}, f32[16,448,256]{2,1,0:T(8,128)}) custom-call(s32[8,128]{1,0:T(8,128)} %get-tuple-element.38.label, s32[16]{0:T(128)} %get-tuple-element.39.head, s32[256]{0:T(256)} %get-tuple-element.40.follow, bf16[2,448,1536]{2,1,0:T(8,128)(2,1)} %get-tuple-element.44.left, ...), custom_call_target="tpu_custom_call" | custom-call | flops 20000000000 | bytes 41943040 | tf_op jit(solution)/shard_map/update/pallas_call | solution.py:467
  215.6 9.3 %all-to-all-done.1.rest = bf16[256,32,256]{2,1,0:T(8,128)(2,1)} async-done(((bf16[256,32,256]{2,1,0:T(8,128)(2,1)}), bf16[256,32,256]{2,1,0:T(8,128)(2,1)}, u32[]{:S(2)}, u32[]{:S(2)}) %all-to-all-start.1) | async-done | bytes 4194336 | tf_op jit(solution)/shard_map/all_to_all | solution.py:446
  224.9 7.1 %finish.1 = bf16[1,448,7168]{2,1,0:T(8,128)(2,1)} custom-call(s32[17]{0:T(128)} %get-tuple-element.32.start, s32[256]{0:T(256)} %get-tuple-element.33.order, s32[256]{0:T(256)} %get-tuple-element.34.column, bf16[256,32,256]{2,1,0:T(8,128)(2,1)} %all-to-all-done.1.rest, bf16[8,448,128]{2,1,0:T(8,128)(2,1)} %get-tuple-element.46.edge, ...), custom_call_target="tpu_custom_call", output_to_operand_aliasing={{}: (6, {})} | custom-call | flops 10000000 | bytes 31457280 | tf_op jit(solution)/shard_map/finish/pallas_call | solution.py:500
Async XLA Ops:
  7.4 44.0 %all-to-all-start = ((bf16[128,72,128]{2,1,0:T(8,128)(2,1)}), bf16[128,72,128]{2,1,0:T(8,128)(2,1)S(1)}, u32[]{:S(2)}, u32[]{:S(2)}) async-start(bf16[128,72,128]{2,1,0:T(8,128)(2,1)} %get-tuple-element.26), calls=%async_computation | async-start | bytes 4718592 | tf_op jit(solution)/shard_map/all_to_all | solution.py:390
  51.4 5.7 %copy-start = (bf16[128,72,128]{2,1,0:T(8,128)(2,1)}, bf16[128,72,128]{2,1,0:T(8,128)(2,1)S(1)}, u32[]{:S(2)}) copy-start(bf16[128,72,128]{2,1,0:T(8,128)(2,1)S(1)} %all-to-all-done.sent.first) | copy-start | bytes 7077892
  51.4 115.0 %all-to-all-start.2 = ((bf16[256,32,128]{2,1,0:T(8,128)(2,1)}), bf16[256,32,128]{2,1,0:T(8,128)(2,1)}, u32[]{:S(2)}, u32[]{:S(2)}) async-start(bf16[256,32,128]{2,1,0:T(8,128)(2,1)} %get-tuple-element.45), calls=%async_computation.2 | async-start | bytes 4194304 | tf_op jit(solution)/shard_map/all_to_all | solution.py:410
  166.4 58.5 %all-to-all-start.1 = ((bf16[256,32,256]{2,1,0:T(8,128)(2,1)}), bf16[256,32,256]{2,1,0:T(8,128)(2,1)}, u32[]{:S(2)}, u32[]{:S(2)}) async-start(bf16[256,32,256]{2,1,0:T(8,128)(2,1)} %get-tuple-element.37), calls=%async_computation.1 | async-start | bytes 8388608 | tf_op jit(solution)/shard_map/all_to_all | solution.py:446

commit v9 on v8

--- a/solution.py
+++ b/solution.py
@@ -54,7 +54,7 @@
     return jnp.exp2(exponent.astype(jnp.int32).astype(jnp.float32) - 15.0)
 
 
-def pack_first_kernel(count, target, tile, blocks, packed, position, load, out, marks, sem):
+def pack_first_kernel(count, target, tile, blocks, packed, position, load, out, marks, sem, out_sem):
     devices = packed.shape[0]
     slots, rows, _ = blocks.shape
     copy = pltpu.make_async_copy(blocks.at[:, :, pl.ds(0, LANE)], load, sem)
@@ -88,9 +88,16 @@
         at = position[i]
         out[at // 2, pl.ds(pl.multiple_of((at % 2) * rows, rows), rows), :] = load[i]
 
-    copy = pltpu.make_async_copy(out.at[pl.ds(0, devices)], packed, sem)
-    copy.start()
-    copy.wait()
+    parts = out_sem.shape[0]
+    pieces = [pl.ds(n * (devices // parts), devices // parts) for n in range(parts)]
+    copies = [
+        pltpu.make_async_copy(out.at[piece], packed.at[piece], out_sem.at[n])
+        for n, piece in enumerate(pieces)
+    ]
+    for copy in copies:
+        copy.start()
+    for copy in copies:
+        copy.wait()
 
 
 def pack_rest_kernel(position, blocks, front, middle, rest, entries, sem):
@@ -131,44 +138,27 @@
     return jnp.concatenate(out, axis=1)
 
 
-def list_blocks(label, groups, start, order, column, head, follow):
+def place_blocks(label, groups, start, order, column):
     sources = label.shape[1]
-
-    @pl.loop(0, groups)
-    def _(r):
-        start[r] = 0
-        head[r] = -1
-
-    def each(act):
-        @pl.loop(0, sources)
-        def _(source):
-            for k in range(2):
-                at = label[k, source]
-
-                @pl.when(at >= 0)
-                def _():
-                    act(2 * source + k, at // groups, at % groups)
-
-    def count(slot, r, c):
-        start[r] += 1
-        follow[slot] = head[c]
-        head[c] = slot
-
-    def place(slot, r, c):
-        at = start[r] - 1
-        start[r] = at
-        order[at] = slot
-        column[at] = c
-
-    each(count)
     start[groups] = 0
 
-    @pl.loop(0, groups)
+    @pl.loop(0, groups, unroll=4)
     def _(r):
         start[groups] += start[r]
         start[r] = start[groups]
 
-    each(place)
+    @pl.loop(0, sources, unroll=2)
+    def _(source):
+        for k in range(2):
+            at = label[k, source]
+
+            @pl.when(at >= 0)
+            def _():
+                r = at // groups
+                index = start[r] - 1
+                start[r] = index
+                order[index] = 2 * source + k
+                column[index] = at % groups
 
 
 def panel_kernel(
@@ -194,12 +184,22 @@
     copy.start()
     copy.wait()
 
+    @pl.loop(0, groups + 1)
+    def _(r):
+        start[r] = 0
+        head[r] = -1
+
     @pl.loop(0, sources, unroll=4)
     def _(source):
         for k in range(2):
             at = marks[k, source]
-            at = jnp.where(at < 0, groups * groups, at)
+            spare = at < 0
+            at = jnp.where(spare, groups * groups, at)
             r, c = at // groups, at % groups
+            chain = jnp.where(spare, groups, c)
+            start[r] += 1
+            follow[2 * source + k] = head[chain]
+            head[chain] = 2 * source + k
             where = pl.ds(pl.multiple_of(r * block_rows, block_rows), block_rows)
             block = arrived[source, k * block_rows : (k + 1) * block_rows, :]
             acc[c, where, :] += block.astype(jnp.float32)
@@ -219,7 +219,7 @@
     code[kept : kept + kept_later] = later_codes[dead:]
     row = lax.broadcasted_iota(jnp.int32, exponents.shape, 0)
     code[kept + kept_later :] = jnp.where(row == 0, exponents, later_exponents).astype(jnp.int16)
-    list_blocks(marks, groups, start, order, column, head, follow)
+    place_blocks(marks, groups, start, order, column)
     later_copy.wait()
     result_copy.wait()
 
@@ -264,7 +264,7 @@
     pivots, label, head, follow, left, code, front, first, middle, base, edge, open_, right, acc
 ):
     rows, panel = right.shape[1], code.shape[2]
-    groups = head.shape[0]
+    groups = head.shape[0] - 1
     block_rows = rows // groups
     dead = 2 * pivots
     step = pl.program_id(0)
@@ -383,6 +383,7 @@
             pltpu.VMEM((device_total + 1, first_rows, LANE), jnp.bfloat16),
             pltpu.SMEM((3, device_total), jnp.int32),
             pltpu.SemaphoreType.DMA,
+            pltpu.SemaphoreType.DMA((4,)),
         ],
         compiler_params=params(),
         name="pack_first",
@@ -414,7 +415,7 @@
     code_rows = (rows - pivots) + kept + ROWTILE
     inverse_spec = lambda k: pl.BlockSpec((1, 1, panel, panel), lambda i: (0, k, 0, 0))
     row_blocks = rows // block_rows
-    lengths = (row_blocks + 1, slot_count, slot_count, row_blocks, slot_count)
+    lengths = (row_blocks + 1, slot_count, slot_count, row_blocks + 1, slot_count)
     factor, second, code, label, start, order, column, head, follow = pl.pallas_call(
         functools.partial(panel_kernel, pivots),
         grid=(1,),

time: 233 us -> 232 us (level)
  Pallas kernels: 80.2 us -> 77.2 us
    pallas_call x1, Pallas kernels: 16.9 us -> 14.2 us  [local(): pl.pallas_call(functools.partial(panel_kernel, pivots), grid=(1,), out_sh...]
  transfers between devices with their start and end apart: 3 -> 3, of which waited for: 2 -> 2; matrix products, arithmetic and copies ran while one was open for 0% -> 0% of each run, Pallas kernels for 29% -> 28%
where the time goes in v9:
time: 232 us
  blocking collectives  94.4 us (41%)
  Pallas kernels  77.2 us (33%)
  waiting for transfers between devices  34.7 us (15%)
  starting transfers between devices  23.8 us (10%)
    all_gather x1, blocking collectives, local(): gathered = lax.all_gather(code, 'grp', axis=0, tiled=False)  94.4 us
    pallas_call x1, Pallas kernels, local(): pl.pallas_call(functools.partial(update_kernel, pivots), grid=(grp_total...  34 us
    all_to_all x1, waiting for transfers between devices, local(): lax.all_to_all(first_out, axes, split_axis=0, concat_axis=0, tiled=True)  25.1 us
    pallas_call x1, Pallas kernels, local(): pl.pallas_call(functools.partial(panel_kernel, pivots), grid=(1,), out_sh...  14.2 us
    all_to_all x1, starting transfers between devices, local(): lax.all_to_all(first_out, axes, split_axis=0, concat_axis=0, tiled=True)  11.5 us
    all_to_all x1, waiting for transfers between devices, local(): lax.all_to_all(rest_out, axes, split_axis=0, concat_axis=0, tiled=True)  9.59 us
    pallas_call x1, Pallas kernels, local(): pl.pallas_call(functools.partial(left_kernel, pivots), grid=(1,), out_sha...  8.52 us
    pallas_call x1, Pallas kernels, local(): pl.pallas_call(pack_rest_kernel, grid=(1,), out_shape=(jax.ShapeDtypeStru...  7.3 us
  transfers between devices with their start and end apart: 3, of which 2 were waited for; matrix products, arithmetic and copies ran while one was open for 0% of the time, Pallas kernels for 28%

profile of v9, /device:TPU:1, one launch (start us, length us, event | category | flops | bytes accessed | tf_op | source)
XLA Modules:
  0.0 231.7 jit_solution(3972502124080942985)
XLA Ops:
  1.3 6.2 %pack_first.1 = (bf16[128,72,128]{2,1,0:T(8,128)(2,1)}, s32[128]{0:T(128)}) custom-call(s32[1]{0:T(128)S(6)} %copy.10.count, s32[128]{0:T(128)} %bitcast.4, s32[128]{0:T(128)} %tile.1, bf16[128,32,512]{2,1,0:T(8,128)(2,1)} %blocks.3), custom_call_target="tpu_custom_call" | custom-call | tf_op jit(solution)/shard_map/pack_first/pallas_call | solution.py:372
  7.5 11.5 %all-to-all-start = ((bf16[128,72,128]{2,1,0:T(8,128)(2,1)}), bf16[128,72,128]{2,1,0:T(8,128)(2,1)S(1)}, u32[]{:S(2)}, u32[]{:S(2)}) async-start(bf16[128,72,128]{2,1,0:T(8,128)(2,1)} %get-tuple-element.26), calls=%async_computation | async-start | bytes 4718592 | tf_op jit(solution)/shard_map/all_to_all | solution.py:391
  19.0 7.3 %pack_rest.1 = (bf16[256,32,128]{2,1,0:T(8,128)(2,1)}, bf16[256,32,256]{2,1,0:T(8,128)(2,1)}, bf16[16,512,128]{2,1,0:T(8,128)(2,1)}) custom-call(s32[128]{0:T(128)} %get-tuple-element.27.position, bf16[128,32,512]{2,1,0:T(8,128)(2,1)} %blocks.3, bf16[1,512,8192]{2,1,0:T(8,128)(2,1)} %front.3), custom_call_target="tpu_custom_call" | custom-call | bytes 16777216 | tf_op jit(solution)/shard_map/pack_rest/pallas_call | solution.py:392
  26.3 25.1 %all-to-all-done.sent.first = bf16[128,72,128]{2,1,0:T(8,128)(2,1)S(1)} async-done(((bf16[128,72,128]{2,1,0:T(8,128)(2,1)}), bf16[128,72,128]{2,1,0:T(8,128)(2,1)S(1)}, u32[]{:S(2)}, u32[]{:S(2)}) %all-to-all-start) | async-done | bytes 2359328 | tf_op jit(solution)/shard_map/all_to_all | solution.py:391
  51.4 0.0 copy-start
  51.4 5.7 %all-to-all-start.2 = ((bf16[256,32,128]{2,1,0:T(8,128)(2,1)}), bf16[256,32,128]{2,1,0:T(8,128)(2,1)}, u32[]{:S(2)}, u32[]{:S(2)}) async-start(bf16[256,32,128]{2,1,0:T(8,128)(2,1)} %get-tuple-element.45), calls=%async_computation.2 | async-start | bytes 4194304 | tf_op jit(solution)/shard_map/all_to_all | solution.py:411
  57.1 0.0 copy-done
  57.1 14.2 %panels.1 = (f32[512,512]{1,0:T(8,128)}, f32[512,512]{1,0:T(8,128)}, s16[944,512]{1,0:T(8,128)(2,1)}, s32[8,128]{1,0:T(8,128)}, s32[17]{0:T(128)}, /*index=5*/s3...) custom-call(bf16[128,72,128]{2,1,0:T(8,128)(2,1)} %copy-done, bf16[16,512,128]{2,1,0:T(8,128)(2,1)} %get-tuple-element.31.entries, ...), custom_call_target="tpu_custom_call" | custom-call | flops 2000000000 | bytes 10485760 | tf_op jit(solution)/shard_map/panels/pallas_call | solution.py:419
  71.3 94.4 %all-gather.2 = s16[15104,512]{1,0:T(8,128)(2,1)} all-gather(s16[944,512]{1,0:T(8,128)(2,1)} %get-tuple-element.35), channel_id=2, replica_groups=mesh['front'=8,'grp'=16] {'grp'}, dimensions={0}, use_global_device_ids=true | all-gather | bytes 16433152 | tf_op jit(solution)/shard_map/all_gather | solution.py:444
  165.7 0.0 all-to-all-done.2.middle
  165.7 6.7 %all-to-all-start.1 = ((bf16[256,32,256]{2,1,0:T(8,128)(2,1)}), bf16[256,32,256]{2,1,0:T(8,128)(2,1)}, u32[]{:S(2)}, u32[]{:S(2)}) async-start(bf16[256,32,256]{2,1,0:T(8,128)(2,1)} %get-tuple-element.37), calls=%async_computation.1 | async-start | bytes 8388608 | tf_op jit(solution)/shard_map/all_to_all | solution.py:447
  172.4 8.5 %left_factors.1 = (f32[1,2,512,512]{3,2,1,0:T(8,128)}, bf16[2,448,1536]{2,1,0:T(8,128)(2,1)}) custom-call(s16[16,944,512]{2,1,0:T(8,128)(2,1)} %bitcast.2, f32[512,512]{1,0:T(8,128)} %get-tuple-element.42.factor, f32[512,512]{1,0:T(8,128)} %get-tuple-element.43.second, f32[1,2,512,512]{3,2,1,0:T(8,128)} %inverse.3), custom_call_target="tpu_custom_call" | custom-call | flops 4000000000 | bytes 8388608 | tf_op jit(solution)/shard_map/left_factors/pallas_call | solution.py:449
  180.9 34.0 %update.1 = (bf16[1,448,7168]{2,1,0:T(8,128)(2,1)}, bf16[8,448,128]{2,1,0:T(8,128)(2,1)}, f32[16,448,256]{2,1,0:T(8,128)}) custom-call(s32[8,128]{1,0:T(8,128)} %get-tuple-element.38.label, s32[17]{0:T(128)} %get-tuple-element.39.head, s32[256]{0:T(256)} %get-tuple-element.40.follow, bf16[2,448,1536]{2,1,0:T(8,128)(2,1)} %get-tuple-element.44.left, ...), custom_call_target="tpu_custom_call" | custom-call | flops 20000000000 | bytes 41943040 | tf_op jit(solution)/shard_map/update/pallas_call | solution.py:468
  214.9 9.6 %all-to-all-done.1.rest = bf16[256,32,256]{2,1,0:T(8,128)(2,1)} async-done(((bf16[256,32,256]{2,1,0:T(8,128)(2,1)}), bf16[256,32,256]{2,1,0:T(8,128)(2,1)}, u32[]{:S(2)}, u32[]{:S(2)}) %all-to-all-start.1) | async-done | bytes 4194336 | tf_op jit(solution)/shard_map/all_to_all | solution.py:447
  224.5 7.0 %finish.1 = bf16[1,448,7168]{2,1,0:T(8,128)(2,1)} custom-call(s32[17]{0:T(128)} %get-tuple-element.32.start, s32[256]{0:T(256)} %get-tuple-element.33.order, s32[256]{0:T(256)} %get-tuple-element.34.column, bf16[256,32,256]{2,1,0:T(8,128)(2,1)} %all-to-all-done.1.rest, bf16[8,448,128]{2,1,0:T(8,128)(2,1)} %get-tuple-element.46.edge, ...), custom_call_target="tpu_custom_call", output_to_operand_aliasing={{}: (6, {})} | custom-call | flops 10000000 | bytes 31457280 | tf_op jit(solution)/shard_map/finish/pallas_call | solution.py:501
Async XLA Ops:
  7.5 44.0 %all-to-all-start = ((bf16[128,72,128]{2,1,0:T(8,128)(2,1)}), bf16[128,72,128]{2,1,0:T(8,128)(2,1)S(1)}, u32[]{:S(2)}, u32[]{:S(2)}) async-start(bf16[128,72,128]{2,1,0:T(8,128)(2,1)} %get-tuple-element.26), calls=%async_computation | async-start | bytes 4718592 | tf_op jit(solution)/shard_map/all_to_all | solution.py:391
  51.4 5.7 %copy-start = (bf16[128,72,128]{2,1,0:T(8,128)(2,1)}, bf16[128,72,128]{2,1,0:T(8,128)(2,1)S(1)}, u32[]{:S(2)}) copy-start(bf16[128,72,128]{2,1,0:T(8,128)(2,1)S(1)} %all-to-all-done.sent.first) | copy-start | bytes 7077892
  51.4 114.3 %all-to-all-start.2 = ((bf16[256,32,128]{2,1,0:T(8,128)(2,1)}), bf16[256,32,128]{2,1,0:T(8,128)(2,1)}, u32[]{:S(2)}, u32[]{:S(2)}) async-start(bf16[256,32,128]{2,1,0:T(8,128)(2,1)} %get-tuple-element.45), calls=%async_computation.2 | async-start | bytes 4194304 | tf_op jit(solution)/shard_map/all_to_all | solution.py:411
  165.7 58.8 %all-to-all-start.1 = ((bf16[256,32,256]{2,1,0:T(8,128)(2,1)}), bf16[256,32,256]{2,1,0:T(8,128)(2,1)}, u32[]{:S(2)}, u32[]{:S(2)}) async-start(bf16[256,32,256]{2,1,0:T(8,128)(2,1)} %get-tuple-element.37), calls=%async_computation.1 | async-start | bytes 8388608 | tf_op jit(solution)/shard_map/all_to_all | solution.py:447
